TPU v7x, 32 devices: a whole 2x2x4 slice. The times are simulated.
32 devices in a mesh: areal: 16 (over z, y, x), layer: 2 (over core).
Axes of the slice: x: 2, y: 2, z: 4, core: 2. Of those that a mesh axis runs over, the one named last changes fastest.
Arguments:
- rhs: bfloat16 [16, 4, 112, 384], P('areal', 'layer'), may hold values from -6 to 6
- areal_blocks: bfloat16 [16, 4, 6, 384, 384], P('areal', 'layer'), may hold values from -0.078125 to 0.078125
- vertical_blocks: bfloat16 [16, 4, 2, 384, 384], P('areal', 'layer'), may hold values from -0.078125 to 0.078125
- conn_src: int32 [16, 2, 6], P('areal', 'layer'), may hold values from 0 to 31, as said below
- conn_count: int32 [16, 2], P('areal', 'layer'), may hold values from 1 to 6, as said below
- tile_map: int32 [32], replicated, may hold values from 0 to 31, as said below
- well_cells: int32 [16, 4, 4], P('areal', 'layer'), may hold values from 0 to 127
- well_gain: float32 [16, 4, 4], P('areal', 'layer'), may hold values from -24 to 24
- sens: float32 [16, 4, 3, 128], P('areal', 'layer'), may hold values from -6 to 6
- basis: bfloat16 [16, 4, 128, 256], P('areal', 'layer'), may hold values from -0.0625 to 0.0625
Outputs:
- adjoint: bfloat16 [16, 4, 112, 384], P('areal', 'layer')
- coefficients: bfloat16 [112, 256], P('layer', 'areal')
Inputs may be any that keep to these rules, and one draw needn't show every extreme that they name: Tile t of a layer group's plane is held by device column tile_map[t] // 2 in tile layer 2 g + tile_map[t] % 2; each value is held by one tile. `conn_src`: the 6 sources of device column c lie, in some order, on the 6 device columns (c + k) mod 16 with k one of 1 to 2, their negatives, 8 and 9, one on each. `conn_count`: the live connections of a device are its first ones. `well_cells`: cells of a tile, repeats allowed.
All inputs are finite; a program needn't handle non-finite values.
Results may differ from a plain program's by a relative error of at most 0.02.
Values may be sent and summed in bfloat16 or wider, within the bound.
No kernel may reach another device: no remote copies, remote signals or barrier semaphores. Data moves between devices by JAX's collectives and lax.ppermute only.
A program may use at most 64 MiB of HBM per device.

v0:
```python
import functools

import jax
import jax.numpy as jnp
from jax import lax
from jax.experimental import pallas as pl
from jax.experimental.pallas import tpu as pltpu
from jax.sharding import PartitionSpec as P

ITERS = 3
F32 = jnp.float32
BF16 = jnp.bfloat16
SMEM = pl.BlockSpec(memory_space=pltpu.SMEM)
VMEM = pl.BlockSpec(memory_space=pltpu.VMEM)
LIMIT = 32 * 1024 * 1024


def near_steps(count):
    return [sign * k for k in range(1, count // 2) for sign in (-1, 1)]


def far_steps(columns):
    return [columns // 2 + 1, columns // 2]


def held(x):
    return pltpu.with_memory_space_constraint(x, pltpu.VMEM)


def dot(a, b):
    return jnp.dot(a, b, preferred_element_type=F32)


def plan_kernel(columns, steps, src, count, tile_map, me, rhs, meta, payload):
    number = len(steps)
    conn = [0] * number
    slots = [0] * number
    for s in range(number):
        place = tile_map[src[s]]
        peer = lax.shift_right_logical(place, 1)
        slot = lax.bitwise_and(place, 1)
        away = peer - me[0]
        away = jnp.where(away < 0, away + columns, away)
        for i, k in enumerate(steps):
            hit = away == k % columns
            conn[i] = jnp.where(hit, s, conn[i])
            slots[i] = jnp.where(hit, slot, slots[i])
    rows = rhs.shape[0]
    line = lax.broadcasted_iota(jnp.int32, (16, rhs.shape[1]), 0)
    asked = jnp.zeros(line.shape, F32)
    for i in range(number):
        meta[i] = conn[i]
        meta[number + i] = slots[i]
        meta[2 * number + i] = jnp.where(conn[i] < count[0], 1, 0)
        asked = jnp.where(line == i, slots[i].astype(F32), asked)
    payload[0:rows] = rhs[...]
    payload[rows:] = asked.astype(BF16)


def load_kernel(blocks, vert, blocks_held, vert_held, sems):
    first = pltpu.make_async_copy(vert, vert_held, sems.at[0])
    second = pltpu.make_async_copy(blocks, blocks_held, sems.at[1])
    first.start()
    second.start()
    first.wait()
    second.wait()


def chosen(mask, low, high):
    return jnp.where(mask > 0.5, high, low).astype(BF16)


def asks_of(payload):
    return payload[payload.shape[0] - 16 :, :].astype(F32)


def far_pick_kernel(number, pair, own, told, tile, relayed):
    rows = tile.shape[0]
    mine, theirs = asks_of(own), asks_of(told)
    mask = theirs[number - 2 : number - 1, :]
    tile[...] = chosen(mask, pair[0:rows].astype(F32), pair[rows:].astype(F32))
    relayed[...] = mine[0:8, :]
    relayed[number - 2 : number - 1, :] = mask


def own_kernel(lam, rhs, vert, part):
    rows = rhs.shape[0] // 2
    part[0] = rhs[0:rows].astype(F32) - dot(lam[rows : 2 * rows], vert[0, 1])
    part[1] = rhs[rows:].astype(F32) - dot(lam[0:rows], vert[1, 0])


def tile_of(ref, slot, rows):
    if ref.shape[0] == rows:
        return ref[...]
    return ref[pl.ds(pl.multiple_of(slot * rows, 16), rows), :]


def less_sources(total, number, meta, blocks, numbered):
    rows = total[0].shape[0]
    for i, ref in numbered:
        tile = tile_of(ref, meta[number + i], rows)
        tile = jnp.where(meta[2 * number + i] > 0, tile, jnp.zeros_like(tile))
        total = [total[d] - dot(tile, blocks[d, meta[i]]) for d in range(2)]
    return total


def less_beside(total, two, group, vert, beside):
    if two:
        mine = group[0]
        term = dot(tile_of(beside[0], mine, total[0].shape[0]), vert[1 - mine, 1 - mine])
        none = jnp.zeros_like(term)
        return [
            total[0] - jnp.where(mine == 1, term, none),
            total[1] - jnp.where(mine == 0, term, none),
        ]
    return [
        total[d] - dot(tile_of(beside[d], 1 - d, total[d].shape[0]), vert[d, d]) for d in range(2)
    ]


def early_kernel(steps, two, first, meta, group, part, blocks, vert, *refs):
    near, number = len(steps) - 2, len(steps)
    arrived, refs = refs[:near], refs[near:]
    sums = less_sources([part[0], part[1]], number, meta, blocks, list(enumerate(arrived)))
    if first:
        beside, (out, masks) = refs[:-2], refs[-2:]
        sums = less_beside(sums, two, group, vert, beside)
        for i in range(near):
            asking = arrived[steps.index(-steps[i])]
            masks[i : i + 1, :] = asks_of(asking)[i : i + 1, :]
    else:
        (out,) = refs
    out[0], out[1] = sums


def late_kernel(number, two, first, meta, group, total, blocks, vert, *refs):
    sides = 0 if first else 1 if two else 2
    far, beside, refs = refs[:2], refs[2 : 2 + sides], refs[2 + sides :]
    numbered = list(enumerate(far, number - 2))
    sums = less_sources([total[0], total[1]], number, meta, blocks, numbered)
    if beside:
        sums = less_beside(sums, two, group, vert, beside)
    low, high = sums
    told, refs = refs[: 2 if first else 1], refs[2 if first else 1 :]
    lam, sends, refs = refs[0], refs[1 : 1 + number], refs[1 + number :]
    outer, refs = refs[: 1 if two else 2], refs[1 if two else 2 :]
    masks = told[0]
    if first:
        masks = refs[0]
        masks[0 : number - 2, :] = told[0][0 : number - 2, :]
        masks[number - 2 : number, :] = told[1][number - 2 : number, :]
    rows = low.shape[0]
    lam[0:rows] = low.astype(BF16)
    lam[rows:] = high.astype(BF16)
    for i, send in enumerate(sends):
        send[...] = chosen(masks[i : i + 1, :], low, high)
    if two:
        outer[0][...] = jnp.where(group[0] == 0, high, low).astype(BF16)
    else:
        outer[0][...] = high.astype(BF16)
        outer[1][...] = low.astype(BF16)


def last_kernel(number, two, columns, meta, group, wells, gains, total, blocks, vert, sens, basis, *refs):
    far, beside, (lam, pieces) = refs[:2], refs[2:-2], refs[-2:]
    numbered = list(enumerate(far, number - 2))
    sums = less_sources([total[0], total[1]], number, meta, blocks, numbered)
    sums = less_beside(sums, two, group, vert, beside)
    phases, _, cells = sens.shape
    spot = lax.broadcasted_iota(jnp.int32, (1, cells), 1)
    projected = None
    for d in range(2):
        rounded = sums[d].astype(BF16)
        lam[d] = rounded
        back = rounded.astype(F32)
        well = jnp.zeros((1, cells), F32)
        for w in range(wells.shape[1]):
            well = well + jnp.where(spot == wells[d, w], gains[d, w], 0.0)
        grad = back[:, :cells] * (sens[0, d : d + 1, :] + well)
        for p in range(1, phases):
            grad = grad + back[:, p * cells : (p + 1) * cells] * sens[p, d : d + 1, :]
        term = dot(grad.astype(BF16), basis[d])
        projected = term if projected is None else projected + term
    if two:
        turned = projected.T
        modes, rows = turned.shape
        share, half = modes // columns, rows // 2
        for c in range(columns):
            top = turned[c * share : c * share + share // 2]
            low = turned[c * share + share // 2 : (c + 1) * share]
            for g in range(2):
                cut = slice(g * half, (g + 1) * half)
                pieces[2 * c + g] = jnp.concatenate([top[:, cut], low[:, cut]], axis=1)
    else:
        pieces[...] = projected


def sum_kernel(pieces, out):
    total = pieces[0]
    for i in range(1, pieces.shape[0]):
        total = total + pieces[i]
    half = total.shape[1] // 2
    out[...] = jnp.concatenate([total[:, :half], total[:, half:]], axis=0).astype(BF16)


def call(kernel, outs, ins, specs, scratch=(), flops=0, moved=0, out_specs=None):
    return pl.pallas_call(
        kernel,
        out_shape=outs,
        in_specs=specs,
        out_specs=out_specs or [VMEM] * len(outs),
        scratch_shapes=list(scratch),
        compiler_params=pltpu.CompilerParams(vmem_limit_bytes=LIMIT),
        cost_estimate=pl.CostEstimate(
            flops=flops, bytes_accessed=moved or flops // 200, transcendentals=0
        ),
    )(*ins)


def shift(x, k):
    columns = lax.axis_size("areal")
    return held(lax.ppermute(x, "areal", [(i, (i - k) % columns) for i in range(columns)]))


def beside_layers(tiles):
    groups = lax.axis_size("layer")
    if groups == 2:
        return [held(lax.ppermute(tiles[0], "layer", [(0, 1), (1, 0)]))]
    up = [(i, i + 1) for i in range(groups - 1)]
    down = [(i + 1, i) for i in range(groups - 1)]
    return [held(lax.ppermute(tiles[0], "layer", up)), held(lax.ppermute(tiles[-1], "layer", down))]


def outside(x):
    return pltpu.with_memory_space_constraint(x, pltpu.HBM)


def on_device(
    rhs,
    areal_blocks,
    vertical_blocks,
    conn_src,
    conn_count,
    tile_map,
    well_cells,
    well_gain,
    sens,
    basis,
):
    columns = lax.axis_size("areal")
    groups = lax.axis_size("layer")
    two = groups == 2
    rows, width = rhs.shape[2:]
    modes = basis.shape[-1]
    number = conn_src.shape[-1]
    steps = near_steps(number) + far_steps(columns)
    rhs = rhs[0].reshape(2 * rows, width)
    me = lax.axis_index("areal").astype(jnp.int32).reshape(1)
    group = lax.axis_index("layer").astype(jnp.int32).reshape(1)

    tile = pltpu.VMEM((rows, width), BF16)
    pair = pltpu.VMEM((2 * rows, width), BF16)
    sums = pltpu.VMEM((2, rows, width), F32)
    one = 2 * rows * width * width
    partial = functools.partial

    with jax.named_scope("plan"):
        far_pair = shift(rhs, steps[-1])
        meta, payload = call(
            partial(plan_kernel, columns, steps),
            [jax.ShapeDtypeStruct((3 * number,), jnp.int32), pltpu.VMEM((2 * rows + 16, width), BF16)],
            (outside(conn_src[0, 0]), conn_count[0], outside(tile_map), me, outside(rhs)),
            [SMEM] * 4 + [VMEM],
            out_specs=[SMEM, VMEM],
        )
        payload = held(payload)

    with jax.named_scope("load"):
        blocks, vert = call(
            load_kernel,
            [pltpu.VMEM(areal_blocks.shape[1:], BF16), pltpu.VMEM(vertical_blocks.shape[1:], BF16)],
            (outside(areal_blocks[0]), outside(vertical_blocks[0])),
            [pl.BlockSpec(memory_space=pltpu.HBM)] * 2,
            [pltpu.SemaphoreType.DMA((2,))],
            moved=areal_blocks.size * 2 + vertical_blocks.size * 2,
        )
        blocks, vert = held(blocks), held(vert)

    rhs_held = held(rhs)
    lam = rhs_held
    sends = [payload] * (number - 2)
    outer = [payload]
    masks_type = pltpu.VMEM((8, width), F32)
    for step in range(ITERS):
        first = step == 0
        with jax.named_scope("apply"):
            arrived = [shift(x, k) for x, k in zip(sends, steps)]
            if first:
                picked, relayed = call(
                    partial(far_pick_kernel, number),
                    [tile, masks_type],
                    (far_pair, payload, arrived[steps.index(-1)]),
                    [VMEM] * 3,
                )
                arrived = [*arrived, shift(picked, 1), far_pair]
                told = shift(relayed, steps[-1])
            beside = beside_layers(outer)
            (part,) = call(own_kernel, [sums], (lam, rhs_held, vert), [VMEM] * 3, flops=2 * one)
            tiles = arrived[:-2] + (beside if first else [])
            total, *rest = call(
                partial(early_kernel, steps, two, first),
                [sums] + ([masks_type] if first else []),
                (meta, group, held(part), blocks, vert, *tiles),
                [SMEM] * 2 + [VMEM] * (3 + len(tiles)),
                flops=2 * (number - 2) * one,
            )
            total = held(total)
            told = [held(rest[0]), told] if first else [masks]
            tiles = arrived[-2:] + ([] if first else beside)
            if step < ITERS - 1:
                lam, *rest = call(
                    partial(late_kernel, number, two, first),
                    [pair] + [tile] * (number + len(beside)) + ([masks_type] if first else []),
                    (meta, group, total, blocks, vert, *tiles, *told),
                    [SMEM] * 2 + [VMEM] * (3 + len(tiles) + len(told)),
                    flops=4 * one,
                )
                lam = held(lam)
                if first:
                    masks = held(rest.pop())
                sends, outer = rest[:number], rest[number:]
            else:
                adjoint, pieces = call(
                    partial(last_kernel, number, two, columns),
                    [
                        jax.ShapeDtypeStruct((2, rows, width), BF16),
                        pltpu.VMEM(
                            (2 * columns, modes // columns // 2, rows) if two else (rows, modes), F32
                        ),
                    ],
                    (meta, group, well_cells[0], well_gain[0], total, blocks, vert, held(sens[0].transpose(1, 0, 2)), held(basis[0]), *tiles),
                    [SMEM] * 4 + [VMEM] * (5 + len(tiles)),
                    flops=5 * one,
                )

    with jax.named_scope("project"):
        if two:
            landed = lax.all_to_all(pieces, ("areal", "layer"), 0, 0, tiled=True)
            (coefficients,) = call(
                sum_kernel,
                [jax.ShapeDtypeStruct((modes // columns, rows // 2), BF16)],
                (held(landed),),
                [VMEM],
            )
            coefficients = coefficients.T
        else:
            cut = pieces.reshape(groups, rows // groups, columns, modes // columns)
            cut = cut.transpose(2, 0, 1, 3).reshape(columns * groups, rows // groups, modes // columns)
            landed = lax.all_to_all(cut, ("areal", "layer"), 0, 0, tiled=True)
            coefficients = jnp.sum(landed, axis=0).astype(BF16)
    return (adjoint[None], coefficients)


def solution(mesh):
    in_specs = (
        P("areal", "layer", None, None),
        P("areal", "layer", None, None, None),
        P("areal", "layer", None, None, None),
        P("areal", "layer", None),
        P("areal", "layer"),
        P(),
        P("areal", "layer", None),
        P("areal", "layer", None),
        P("areal", "layer", None, None),
        P("areal", "layer", None, None),
    )
    out_specs = (P("areal", "layer", None, None), P("layer", "areal"))
    return jax.shard_map(
        on_device, mesh=mesh, in_specs=in_specs, out_specs=out_specs, check_vma=False
    )
```

profile of v0, /device:TPU:0, one launch (start us, length us, event | category | flops | bytes accessed | tf_op | source)
XLA Modules:
  0.0 81.0 jit_solution(8820083482508821068)
XLA Ops:
  0.6 4.1 %collective-permute-start.5 = (bf16[224,384]{1,0:T(8,128)(2,1)}, bf16[224,384]{1,0:T(8,128)(2,1)S(1)}, u32[]{:S(2)}, u32[]{:S(2)}) collective-permute-start(bf16[224,384]{1,0:T(8,128)(2,1)} %bitcast.16), channel_id=1, source_target_pairs={{0,16},{2,18},{4,20},{6,22},{8,24},{10,26},{12,28},{14,30},{16,0},... | collective-permute-start | bytes 516104 | tf_op jit(solution)/shard_map/plan/ppermute | solution.py:222
  5.4 1.6 %plan.1 = (s32[18]{0:T(128)S(1)}, bf16[240,384]{1,0:T(8,128)(2,1)S(1)}) custom-call(s32[6]{0:T(128)} %bitcast.29, s32[1]{0:T(128)} %bitcast.15.count, s32[32]{0:T(128)} %tile_map.1, s32[1]{0:T(128)} %bitcast.2.me, bf16[224,384]{1,0:T(8,128)(2,1)} %bitcast.17), custom_call_target="tpu_custom_call" | custom-call | tf_op jit(solution)/shard_map/plan/pallas_call | solution.py:207
  7.0 1.5 %collective-permute-start = (bf16[240,384]{1,0:T(8,128)(2,1)S(1)}, bf16[240,384]{1,0:T(8,128)(2,1)S(1)}, u32[]{:S(2)}, u32[]{:S(2)}) collective-permute-start(bf16[240,384]{1,0:T(8,128)(2,1)S(1)} %get-tuple-element.32.own), channel_id=1, source_target_pairs={{0,2},{2,4},{4,6},{6,8},{8,10},{10,12},{12,14},{14,16},{16,18},{18... | collective-permute-start | bytes 552968 | tf_op jit(solution)/shard_map/apply/ppermute | solution.py:222
  8.5 4.1 %collective-permute-start.1 = (bf16[240,384]{1,0:T(8,128)(2,1)S(1)}, bf16[240,384]{1,0:T(8,128)(2,1)S(1)}, u32[]{:S(2)}, u32[]{:S(2)}) collective-permute-start(bf16[240,384]{1,0:T(8,128)(2,1)S(1)} %get-tuple-element.32.own), channel_id=1, source_target_pairs={{0,30},{2,0},{4,2},{6,4},{8,6},{10,8},{12,10},{14,12},{16,14},{18,... | collective-permute-start | bytes 552968 | tf_op jit(solution)/shard_map/apply/ppermute | solution.py:222
  12.7 4.7 %collective-permute-start.3 = (bf16[240,384]{1,0:T(8,128)(2,1)S(1)}, bf16[240,384]{1,0:T(8,128)(2,1)S(1)}, u32[]{:S(2)}, u32[]{:S(2)}) collective-permute-start(bf16[240,384]{1,0:T(8,128)(2,1)S(1)} %get-tuple-element.32.own), channel_id=1, source_target_pairs={{0,28},{2,30},{4,0},{6,2},{8,4},{10,6},{12,8},{14,10},{16,12},{18,... | collective-permute-start | bytes 552968 | tf_op jit(solution)/shard_map/apply/ppermute | solution.py:222
  17.4 1.4 %collective-permute-done.refs_0_.told = bf16[240,384]{1,0:T(8,128)(2,1)S(1)} collective-permute-done((bf16[240,384]{1,0:T(8,128)(2,1)S(1)}, bf16[240,384]{1,0:T(8,128)(2,1)S(1)}, u32[]{:S(2)}, u32[]{:S(2)}) %collective-permute-start) | collective-permute-done | bytes 184352 | tf_op jit(solution)/shard_map/apply/ppermute | solution.py:222
  18.9 2.4 %load.1 = (bf16[2,6,384,384]{3,2,1,0:T(8,128)(2,1)S(1)}, bf16[2,2,384,384]{3,2,1,0:T(8,128)(2,1)S(1)}) custom-call(bf16[2,6,384,384]{3,2,1,0:T(8,128)(2,1)} %bitcast.26, bf16[2,2,384,384]{3,2,1,0:T(8,128)(2,1)} %bitcast.27), custom_call_target="tpu_custom_call" | custom-call | bytes 4718592 | tf_op jit(solution)/shard_map/load/pallas_call | solution.py:207
  21.6 5.9 %collective-permute-start.7 = (f32[8,384]{1,0:T(8,128)S(1)}, f32[8,384]{1,0:T(8,128)S(1)}, u32[]{:S(2)}, u32[]{:S(2)}) collective-permute-start(f32[8,384]{1,0:T(8,128)S(1)} %get-tuple-element.36), channel_id=1, source_target_pairs={{0,16},{2,18},{4,20},{6,22},{8,24},{10,26},{12,28},{14,30},{16,0},... | collective-permute-start | bytes 36872 | tf_op jit(solution)/shard_map/apply/ppermute | solution.py:222
  27.5 1.3 %apply.11 = (f32[2,112,384]{2,1,0:T(8,128)S(1)}, f32[8,384]{1,0:T(8,128)S(1)}) custom-call(s32[18]{0:T(128)S(1)} %get-tuple-element.29.meta, s32[1]{0:T(128)} %bitcast.4.group, f32[2,112,384]{2,1,0:T(8,128)S(1)} %apply.10.part, bf16[2,6,384,384]{3,2,1,0:T(8,128)(2,1)S(1)} %get-tuple-element.31.blocks, bf16[2,2,384,384]{3,2,1,0:T(8,128)(2,1)S(1)} %get-tuple-element.30.vert, ...), custom_call_target="tpu_custom_call" | custom-call | flops 264241152 | bytes 1321205 | tf_op jit(solution)/shard_map/apply/pallas_call | solution.py:207
  30.4 4.7 %collective-permute-start.11 = (bf16[112,384]{1,0:T(8,128)(2,1)S(1)}, bf16[112,384]{1,0:T(8,128)(2,1)S(1)}, u32[]{:S(2)}, u32[]{:S(2)}) collective-permute-start(bf16[112,384]{1,0:T(8,128)(2,1)S(1)} %get-tuple-element.41), channel_id=1, source_target_pairs={{0,28},{2,30},{4,0},{6,2},{8,4},{10,6},{12,8},{14,10},{16,12},{18,... | collective-permute-start | bytes 258056 | tf_op jit(solution)/shard_map/apply/ppermute | solution.py:222
  35.1 1.9 %collective-permute-start.8 = (bf16[112,384]{1,0:T(8,128)(2,1)S(1)}, bf16[112,384]{1,0:T(8,128)(2,1)S(1)}, u32[]{:S(2)}, u32[]{:S(2)}) collective-permute-start(bf16[112,384]{1,0:T(8,128)(2,1)S(1)} %get-tuple-element.38), channel_id=1, source_target_pairs={{0,2},{2,4},{4,6},{6,8},{8,10},{10,12},{12,14},{14,16},{16,18},{18... | collective-permute-start | bytes 258056 | tf_op jit(solution)/shard_map/apply/ppermute | solution.py:222
  37.0 3.7 %collective-permute-start.9 = (bf16[112,384]{1,0:T(8,128)(2,1)S(1)}, bf16[112,384]{1,0:T(8,128)(2,1)S(1)}, u32[]{:S(2)}, u32[]{:S(2)}) collective-permute-start(bf16[112,384]{1,0:T(8,128)(2,1)S(1)} %get-tuple-element.39), channel_id=1, source_target_pairs={{0,30},{2,0},{4,2},{6,4},{8,6},{10,8},{12,10},{14,12},{16,14},{18,... | collective-permute-start | bytes 258056 | tf_op jit(solution)/shard_map/apply/ppermute | solution.py:222
  40.7 1.1 %collective-permute-start.13 = (bf16[112,384]{1,0:T(8,128)(2,1)S(1)}, bf16[112,384]{1,0:T(8,128)(2,1)S(1)}, u32[]{:S(2)}, u32[]{:S(2)}) collective-permute-start(bf16[112,384]{1,0:T(8,128)(2,1)S(1)} %get-tuple-element.43), channel_id=1, source_target_pairs={{0,16},{2,18},{4,20},{6,22},{8,24},{10,26},{12,28},{14,30},{16,0},... | collective-permute-start | bytes 258056 | tf_op jit(solution)/shard_map/apply/ppermute | solution.py:222
  42.1 2.0 %collective-permute-done.8.refs_0_ = bf16[112,384]{1,0:T(8,128)(2,1)S(1)} collective-permute-done((bf16[112,384]{1,0:T(8,128)(2,1)S(1)}, bf16[112,384]{1,0:T(8,128)(2,1)S(1)}, u32[]{:S(2)}, u32[]{:S(2)}) %collective-permute-start.8) | collective-permute-done | bytes 86048 | tf_op jit(solution)/shard_map/apply/ppermute | solution.py:222
  44.1 1.2 %apply.15.total = f32[2,112,384]{2,1,0:T(8,128)S(1)} custom-call(s32[18]{0:T(128)S(1)} %get-tuple-element.29.meta, s32[1]{0:T(128)} %bitcast.4.group, f32[2,112,384]{2,1,0:T(8,128)S(1)} %apply.14.part, bf16[2,6,384,384]{3,2,1,0:T(8,128)(2,1)S(1)} %get-tuple-element.31.blocks, bf16[2,2,384,384]{3,2,1,0:T(8,128)(2,1)S(1)} %get-tuple-element.30.vert, ...), custom_call_target="tpu_custom_call" | custom-call | flops 264241152 | bytes 1321205 | tf_op jit(solution)/shard_map/apply/pallas_call | solution.py:207
  45.3 4.1 %collective-permute-done.12.refs_0_ = bf16[112,384]{1,0:T(8,128)(2,1)S(1)} collective-permute-done((bf16[112,384]{1,0:T(8,128)(2,1)S(1)}, bf16[112,384]{1,0:T(8,128)(2,1)S(1)}, u32[]{:S(2)}, u32[]{:S(2)}) %collective-permute-start.12) | collective-permute-done | bytes 86048 | tf_op jit(solution)/shard_map/apply/ppermute | solution.py:222
  50.5 1.5 %collective-permute-start.15 = (bf16[112,384]{1,0:T(8,128)(2,1)S(1)}, bf16[112,384]{1,0:T(8,128)(2,1)S(1)}, u32[]{:S(2)}, u32[]{:S(2)}) collective-permute-start(bf16[112,384]{1,0:T(8,128)(2,1)S(1)} %get-tuple-element.47), channel_id=1, source_target_pairs={{0,2},{2,4},{4,6},{6,8},{8,10},{10,12},{12,14},{14,16},{16,18},{18... | collective-permute-start | bytes 258056 | tf_op jit(solution)/shard_map/apply/ppermute | solution.py:222
  52.1 4.1 %collective-permute-start.16 = (bf16[112,384]{1,0:T(8,128)(2,1)S(1)}, bf16[112,384]{1,0:T(8,128)(2,1)S(1)}, u32[]{:S(2)}, u32[]{:S(2)}) collective-permute-start(bf16[112,384]{1,0:T(8,128)(2,1)S(1)} %get-tuple-element.48), channel_id=1, source_target_pairs={{0,30},{2,0},{4,2},{6,4},{8,6},{10,8},{12,10},{14,12},{16,14},{18,... | collective-permute-start | bytes 258056 | tf_op jit(solution)/shard_map/apply/ppermute | solution.py:222
  56.2 4.7 %collective-permute-start.18 = (bf16[112,384]{1,0:T(8,128)(2,1)S(1)}, bf16[112,384]{1,0:T(8,128)(2,1)S(1)}, u32[]{:S(2)}, u32[]{:S(2)}) collective-permute-start(bf16[112,384]{1,0:T(8,128)(2,1)S(1)} %get-tuple-element.50), channel_id=1, source_target_pairs={{0,28},{2,30},{4,0},{6,2},{8,4},{10,6},{12,8},{14,10},{16,12},{18,... | collective-permute-start | bytes 258056 | tf_op jit(solution)/shard_map/apply/ppermute | solution.py:222
  61.4 2.0 %collective-permute-done.17.refs_2_ = bf16[112,384]{1,0:T(8,128)(2,1)S(1)} collective-permute-done((bf16[112,384]{1,0:T(8,128)(2,1)S(1)}, bf16[112,384]{1,0:T(8,128)(2,1)S(1)}, u32[]{:S(2)}, u32[]{:S(2)}) %collective-permute-start.17) | collective-permute-done | bytes 86048 | tf_op jit(solution)/shard_map/apply/ppermute | solution.py:222
  63.4 1.2 %apply.18.total = f32[2,112,384]{2,1,0:T(8,128)S(1)} custom-call(s32[18]{0:T(128)S(1)} %get-tuple-element.29.meta, s32[1]{0:T(128)} %bitcast.4.group, f32[2,112,384]{2,1,0:T(8,128)S(1)} %apply.17.part, bf16[2,6,384,384]{3,2,1,0:T(8,128)(2,1)S(1)} %get-tuple-element.31.blocks, bf16[2,2,384,384]{3,2,1,0:T(8,128)(2,1)S(1)} %get-tuple-element.30.vert, ...), custom_call_target="tpu_custom_call" | custom-call | flops 264241152 | bytes 1321205 | tf_op jit(solution)/shard_map/apply/pallas_call | solution.py:207
  64.6 2.6 %collective-permute-done.19.refs_0_ = bf16[112,384]{1,0:T(8,128)(2,1)S(1)} collective-permute-done((bf16[112,384]{1,0:T(8,128)(2,1)S(1)}, bf16[112,384]{1,0:T(8,128)(2,1)S(1)}, u32[]{:S(2)}, u32[]{:S(2)}) %collective-permute-start.19) | collective-permute-done | bytes 86048 | tf_op jit(solution)/shard_map/apply/ppermute | solution.py:222
  67.3 1.8 %apply.19 = (bf16[2,112,384]{2,1,0:T(8,128)(2,1)}, f32[32,8,112]{2,1,0:T(8,128)S(1)}) custom-call(s32[18]{0:T(128)S(1)} %get-tuple-element.29.meta, s32[1]{0:T(128)} %bitcast.4.group, s32[2,4]{1,0:T(2,128)S(1)} %bitcast.24, f32[2,4]{1,0:T(2,128)S(1)} %bitcast.25, f32[2,112,384]{2,1,0:T(8,128)S(1)} %apply.18.total, ...), custom_call_target="tpu_custom_call" | custom-call | flops 165150720 | bytes 825753 | tf_op jit(solution)/shard_map/apply/pallas_call | solution.py:207
  69.0 11.3 %all_to_all.5.pieces = f32[32,8,112]{2,1,0:T(8,128)S(1)} all-to-all(f32[32,8,112]{2,1,0:T(8,128)S(1)} %get-tuple-element.55), channel_id=1, replica_groups=mesh['areal'=16,'layer'=2] {'areal','layer'}, dimensions={0} | all-to-all | bytes 229376 | tf_op jit(solution)/shard_map/project/all_to_all | solution.py:348
  (44 shorter events, 4.4 us)
Async XLA Ops:
  0.6 20.7 %copy-start = (bf16[1,2,112,384]{3,2,1,0:T(8,128)(2,1)S(1)}, bf16[1,2,112,384]{3,2,1,0:T(8,128)(2,1)}, u32[]{:S(2)}) copy-start(bf16[1,2,112,384]{3,2,1,0:T(8,128)(2,1)} %param.10) | copy-start | bytes 516100
  0.6 16.8 %collective-permute-start.5 = (bf16[224,384]{1,0:T(8,128)(2,1)}, bf16[224,384]{1,0:T(8,128)(2,1)S(1)}, u32[]{:S(2)}, u32[]{:S(2)}) collective-permute-start(bf16[224,384]{1,0:T(8,128)(2,1)} %bitcast.16), channel_id=1, source_target_pairs={{0,16},{2,18},{4,20},{6,22},{8,24},{10,26},{12,28},{14,30},{16,0},... | collective-permute-start | bytes 516104 | tf_op jit(solution)/shard_map/plan/ppermute | solution.py:222
  7.0 11.8 %collective-permute-start = (bf16[240,384]{1,0:T(8,128)(2,1)S(1)}, bf16[240,384]{1,0:T(8,128)(2,1)S(1)}, u32[]{:S(2)}, u32[]{:S(2)}) collective-permute-start(bf16[240,384]{1,0:T(8,128)(2,1)S(1)} %get-tuple-element.32.own), channel_id=1, source_target_pairs={{0,2},{2,4},{4,6},{6,8},{8,10},{10,12},{12,14},{14,16},{16,18},{18... | collective-permute-start | bytes 552968 | tf_op jit(solution)/shard_map/apply/ppermute | solution.py:222
  8.5 13.1 %collective-permute-start.1 = (bf16[240,384]{1,0:T(8,128)(2,1)S(1)}, bf16[240,384]{1,0:T(8,128)(2,1)S(1)}, u32[]{:S(2)}, u32[]{:S(2)}) collective-permute-start(bf16[240,384]{1,0:T(8,128)(2,1)S(1)} %get-tuple-element.32.own), channel_id=1, source_target_pairs={{0,30},{2,0},{4,2},{6,4},{8,6},{10,8},{12,10},{14,12},{16,14},{18,... | collective-permute-start | bytes 552968 | tf_op jit(solution)/shard_map/apply/ppermute | solution.py:222
  12.7 14.8 %collective-permute-start.2 = (bf16[240,384]{1,0:T(8,128)(2,1)S(1)}, bf16[240,384]{1,0:T(8,128)(2,1)S(1)}, u32[]{:S(2)}, u32[]{:S(2)}) collective-permute-start(bf16[240,384]{1,0:T(8,128)(2,1)S(1)} %get-tuple-element.32.own), channel_id=1, source_target_pairs={{0,4},{2,6},{4,8},{6,10},{8,12},{10,14},{12,16},{14,18},{16,20},{1... | collective-permute-start | bytes 552968 | tf_op jit(solution)/shard_map/apply/ppermute | solution.py:222
  12.7 14.8 %collective-permute-start.3 = (bf16[240,384]{1,0:T(8,128)(2,1)S(1)}, bf16[240,384]{1,0:T(8,128)(2,1)S(1)}, u32[]{:S(2)}, u32[]{:S(2)}) collective-permute-start(bf16[240,384]{1,0:T(8,128)(2,1)S(1)} %get-tuple-element.32.own), channel_id=1, source_target_pairs={{0,28},{2,30},{4,0},{6,2},{8,4},{10,6},{12,8},{14,10},{16,12},{18,... | collective-permute-start | bytes 552968 | tf_op jit(solution)/shard_map/apply/ppermute | solution.py:222
  17.4 10.1 %collective-permute-start.4 = (bf16[240,384]{1,0:T(8,128)(2,1)S(1)}, bf16[240,384]{1,0:T(8,128)(2,1)S(1)}, u32[]{:S(2)}, u32[]{:S(2)}) collective-permute-start(bf16[240,384]{1,0:T(8,128)(2,1)S(1)} %get-tuple-element.32.own), channel_id=1, source_target_pairs={{0,1},{1,0},{2,3},{3,2},{4,5},{5,4},{6,7},{7,6},{8,9},{9,8},{10,11... | collective-permute-start | bytes 552968 | tf_op jit(solution)/shard_map/apply/ppermute | solution.py:228
  18.9 10.4 %collective-permute-start.6 = (bf16[112,384]{1,0:T(8,128)(2,1)S(1)}, bf16[112,384]{1,0:T(8,128)(2,1)S(1)}, u32[]{:S(2)}, u32[]{:S(2)}) collective-permute-start(bf16[112,384]{1,0:T(8,128)(2,1)S(1)} %get-tuple-element.34), channel_id=1, source_target_pairs={{0,30},{2,0},{4,2},{6,4},{8,6},{10,8},{12,10},{14,12},{16,14},{18,... | collective-permute-start | bytes 258056 | tf_op jit(solution)/shard_map/apply/ppermute | solution.py:222
  21.6 7.7 %collective-permute-start.7 = (f32[8,384]{1,0:T(8,128)S(1)}, f32[8,384]{1,0:T(8,128)S(1)}, u32[]{:S(2)}, u32[]{:S(2)}) collective-permute-start(f32[8,384]{1,0:T(8,128)S(1)} %get-tuple-element.36), channel_id=1, source_target_pairs={{0,16},{2,18},{4,20},{6,22},{8,24},{10,26},{12,28},{14,30},{16,0},... | collective-permute-start | bytes 36872 | tf_op jit(solution)/shard_map/apply/ppermute | solution.py:222
  30.3 10.4 %collective-permute-start.10 = (bf16[112,384]{1,0:T(8,128)(2,1)S(1)}, bf16[112,384]{1,0:T(8,128)(2,1)S(1)}, u32[]{:S(2)}, u32[]{:S(2)}) collective-permute-start(bf16[112,384]{1,0:T(8,128)(2,1)S(1)} %get-tuple-element.40), channel_id=1, source_target_pairs={{0,4},{2,6},{4,8},{6,10},{8,12},{10,14},{12,16},{14,18},{16,20},{1... | collective-permute-start | bytes 258056 | tf_op jit(solution)/shard_map/apply/ppermute | solution.py:222
  30.4 11.5 %collective-permute-start.11 = (bf16[112,384]{1,0:T(8,128)(2,1)S(1)}, bf16[112,384]{1,0:T(8,128)(2,1)S(1)}, u32[]{:S(2)}, u32[]{:S(2)}) collective-permute-start(bf16[112,384]{1,0:T(8,128)(2,1)S(1)} %get-tuple-element.41), channel_id=1, source_target_pairs={{0,28},{2,30},{4,0},{6,2},{8,4},{10,6},{12,8},{14,10},{16,12},{18,... | collective-permute-start | bytes 258056 | tf_op jit(solution)/shard_map/apply/ppermute | solution.py:222
  35.1 9.0 %collective-permute-start.8 = (bf16[112,384]{1,0:T(8,128)(2,1)S(1)}, bf16[112,384]{1,0:T(8,128)(2,1)S(1)}, u32[]{:S(2)}, u32[]{:S(2)}) collective-permute-start(bf16[112,384]{1,0:T(8,128)(2,1)S(1)} %get-tuple-element.38), channel_id=1, source_target_pairs={{0,2},{2,4},{4,6},{6,8},{8,10},{10,12},{12,14},{14,16},{16,18},{18... | collective-permute-start | bytes 258056 | tf_op jit(solution)/shard_map/apply/ppermute | solution.py:222
  37.0 7.1 %collective-permute-start.9 = (bf16[112,384]{1,0:T(8,128)(2,1)S(1)}, bf16[112,384]{1,0:T(8,128)(2,1)S(1)}, u32[]{:S(2)}, u32[]{:S(2)}) collective-permute-start(bf16[112,384]{1,0:T(8,128)(2,1)S(1)} %get-tuple-element.39), channel_id=1, source_target_pairs={{0,30},{2,0},{4,2},{6,4},{8,6},{10,8},{12,10},{14,12},{16,14},{18,... | collective-permute-start | bytes 258056 | tf_op jit(solution)/shard_map/apply/ppermute | solution.py:222
  40.7 8.7 %collective-permute-start.12 = (bf16[112,384]{1,0:T(8,128)(2,1)S(1)}, bf16[112,384]{1,0:T(8,128)(2,1)S(1)}, u32[]{:S(2)}, u32[]{:S(2)}) collective-permute-start(bf16[112,384]{1,0:T(8,128)(2,1)S(1)} %get-tuple-element.42), channel_id=1, source_target_pairs={{0,14},{2,16},{4,18},{6,20},{8,22},{10,24},{12,26},{14,28},{16,30}... | collective-permute-start | bytes 258056 | tf_op jit(solution)/shard_map/apply/ppermute | solution.py:222
  40.7 8.7 %collective-permute-start.13 = (bf16[112,384]{1,0:T(8,128)(2,1)S(1)}, bf16[112,384]{1,0:T(8,128)(2,1)S(1)}, u32[]{:S(2)}, u32[]{:S(2)}) collective-permute-start(bf16[112,384]{1,0:T(8,128)(2,1)S(1)} %get-tuple-element.43), channel_id=1, source_target_pairs={{0,16},{2,18},{4,20},{6,22},{8,24},{10,26},{12,28},{14,30},{16,0},... | collective-permute-start | bytes 258056 | tf_op jit(solution)/shard_map/apply/ppermute | solution.py:222
  41.8 7.6 %collective-permute-start.14 = (bf16[112,384]{1,0:T(8,128)(2,1)S(1)}, bf16[112,384]{1,0:T(8,128)(2,1)S(1)}, u32[]{:S(2)}, u32[]{:S(2)}) collective-permute-start(bf16[112,384]{1,0:T(8,128)(2,1)S(1)} %get-tuple-element.44), channel_id=1, source_target_pairs={{0,1},{1,0},{2,3},{3,2},{4,5},{5,4},{6,7},{7,6},{8,9},{9,8},{10,11... | collective-permute-start | bytes 258056 | tf_op jit(solution)/shard_map/apply/ppermute | solution.py:228
  50.5 10.4 %collective-permute-start.15 = (bf16[112,384]{1,0:T(8,128)(2,1)S(1)}, bf16[112,384]{1,0:T(8,128)(2,1)S(1)}, u32[]{:S(2)}, u32[]{:S(2)}) collective-permute-start(bf16[112,384]{1,0:T(8,128)(2,1)S(1)} %get-tuple-element.47), channel_id=1, source_target_pairs={{0,2},{2,4},{4,6},{6,8},{8,10},{10,12},{12,14},{14,16},{16,18},{18... | collective-permute-start | bytes 258056 | tf_op jit(solution)/shard_map/apply/ppermute | solution.py:222
  52.1 8.9 %collective-permute-start.16 = (bf16[112,384]{1,0:T(8,128)(2,1)S(1)}, bf16[112,384]{1,0:T(8,128)(2,1)S(1)}, u32[]{:S(2)}, u32[]{:S(2)}) collective-permute-start(bf16[112,384]{1,0:T(8,128)(2,1)S(1)} %get-tuple-element.48), channel_id=1, source_target_pairs={{0,30},{2,0},{4,2},{6,4},{8,6},{10,8},{12,10},{14,12},{16,14},{18,... | collective-permute-start | bytes 258056 | tf_op jit(solution)/shard_map/apply/ppermute | solution.py:222
  56.2 7.2 %collective-permute-start.17 = (bf16[112,384]{1,0:T(8,128)(2,1)S(1)}, bf16[112,384]{1,0:T(8,128)(2,1)S(1)}, u32[]{:S(2)}, u32[]{:S(2)}) collective-permute-start(bf16[112,384]{1,0:T(8,128)(2,1)S(1)} %get-tuple-element.49), channel_id=1, source_target_pairs={{0,4},{2,6},{4,8},{6,10},{8,12},{10,14},{12,16},{14,18},{16,20},{1... | collective-permute-start | bytes 258056 | tf_op jit(solution)/shard_map/apply/ppermute | solution.py:222
  56.2 7.2 %collective-permute-start.18 = (bf16[112,384]{1,0:T(8,128)(2,1)S(1)}, bf16[112,384]{1,0:T(8,128)(2,1)S(1)}, u32[]{:S(2)}, u32[]{:S(2)}) collective-permute-start(bf16[112,384]{1,0:T(8,128)(2,1)S(1)} %get-tuple-element.50), channel_id=1, source_target_pairs={{0,28},{2,30},{4,0},{6,2},{8,4},{10,6},{12,8},{14,10},{16,12},{18,... | collective-permute-start | bytes 258056 | tf_op jit(solution)/shard_map/apply/ppermute | solution.py:222
  60.9 6.3 %collective-permute-start.19 = (bf16[112,384]{1,0:T(8,128)(2,1)S(1)}, bf16[112,384]{1,0:T(8,128)(2,1)S(1)}, u32[]{:S(2)}, u32[]{:S(2)}) collective-permute-start(bf16[112,384]{1,0:T(8,128)(2,1)S(1)} %get-tuple-element.51), channel_id=1, source_target_pairs={{0,14},{2,16},{4,18},{6,20},{8,22},{10,24},{12,26},{14,28},{16,30}... | collective-permute-start | bytes 258056 | tf_op jit(solution)/shard_map/apply/ppermute | solution.py:222
  60.9 6.3 %collective-permute-start.20 = (bf16[112,384]{1,0:T(8,128)(2,1)S(1)}, bf16[112,384]{1,0:T(8,128)(2,1)S(1)}, u32[]{:S(2)}, u32[]{:S(2)}) collective-permute-start(bf16[112,384]{1,0:T(8,128)(2,1)S(1)} %get-tuple-element.52), channel_id=1, source_target_pairs={{0,16},{2,18},{4,20},{6,22},{8,24},{10,26},{12,28},{14,30},{16,0},... | collective-permute-start | bytes 258056 | tf_op jit(solution)/shard_map/apply/ppermute | solution.py:222
  61.0 6.3 %collective-permute-start.21 = (bf16[112,384]{1,0:T(8,128)(2,1)S(1)}, bf16[112,384]{1,0:T(8,128)(2,1)S(1)}, u32[]{:S(2)}, u32[]{:S(2)}) collective-permute-start(bf16[112,384]{1,0:T(8,128)(2,1)S(1)} %get-tuple-element.53), channel_id=1, source_target_pairs={{0,1},{1,0},{2,3},{3,2},{4,5},{5,4},{6,7},{7,6},{8,9},{9,8},{10,11... | collective-permute-start | bytes 258056 | tf_op jit(solution)/shard_map/apply/ppermute | solution.py:228
  61.0 6.2 %copy-start.1 = (bf16[1,2,128,256]{3,2,1,0:T(8,128)(2,1)S(1)}, bf16[1,2,128,256]{3,2,1,0:T(8,128)(2,1)}, u32[]{:S(2)}) copy-start(bf16[1,2,128,256]{3,2,1,0:T(8,128)(2,1)} %param.19) | copy-start | bytes 393220
  (3 other events, 18.5 us)
where the time goes:
time: 81.2 us; the launch traced here: 81 us
  starting transfers between devices  42.4 us (52%)
  Pallas kernels  13.1 us (16%)
  waiting for transfers between devices  12.7 us (16%)
  blocking collectives  11.3 us (14%)
  between operations  1.5 us (2%)
    ppermute x19, starting transfers between devices, shift(): lax.ppermute(x, 'areal', [(i, (i - k) % columns) for i in range(columns)])  42.4 us
    pallas_call x13, Pallas kernels, call(): pl.pallas_call(kernel, out_shape=outs, in_specs=specs, out_specs=out_spec...  13.1 us
    ppermute x19, waiting for transfers between devices, shift(): lax.ppermute(x, 'areal', [(i, (i - k) % columns) for i in range(columns)])  12.7 us
    all_to_all x1, blocking collectives, on_device(): landed = lax.all_to_all(pieces, ('areal', 'layer'), 0, 0, tiled=True)  11.3 us
  transfers between devices with their start and end apart: 22, of which 6 were waited for; matrix products, arithmetic and copies ran while one was open for 0% of the time, Pallas kernels for 11%

commit v1 on v0

--- a/solution.py
+++ b/solution.py
@@ -15,12 +15,14 @@
 LIMIT = 32 * 1024 * 1024
 
 
-def near_steps(count):
-    return [sign * k for k in range(1, count // 2) for sign in (-1, 1)]
-
-
-def far_steps(columns):
-    return [columns // 2 + 1, columns // 2]
+def near_swaps(count):
+    return [(k, color) for color in (1, 0) for k in range(count // 2 - 1, 0, -1)]
+
+
+def swap_pairs(columns, k, color):
+    return [
+        (c, (c + k if (c // k) % 2 == color else c - k) % columns) for c in range(columns)
+    ]
 
 
 def held(x):
@@ -31,7 +33,10 @@
     return jnp.dot(a, b, preferred_element_type=F32)
 
 
-def plan_kernel(columns, steps, src, count, tile_map, me, rhs, meta, payload):
+def plan_kernel(columns, swaps, src, count, tile_map, me, rhs, meta, payload):
+    steps = [
+        jnp.where(lax.rem(lax.div(me[0], k), 2) == color, k, columns - k) for k, color in swaps
+    ] + [columns // 2 + 1, columns // 2]
     number = len(steps)
     conn = [0] * number
     slots = [0] * number
@@ -42,7 +47,7 @@
         away = peer - me[0]
         away = jnp.where(away < 0, away + columns, away)
         for i, k in enumerate(steps):
-            hit = away == k % columns
+            hit = away == k
             conn[i] = jnp.where(hit, s, conn[i])
             slots[i] = jnp.where(hit, slot, slots[i])
     rows = rhs.shape[0]
@@ -74,9 +79,9 @@
     return payload[payload.shape[0] - 16 :, :].astype(F32)
 
 
-def far_pick_kernel(number, pair, own, told, tile, relayed):
+def far_pick_kernel(number, me, pair, own, even, odd, tile, relayed):
     rows = tile.shape[0]
-    mine, theirs = asks_of(own), asks_of(told)
+    mine, theirs = asks_of(own), jnp.where(lax.rem(me[0], 2) == 0, asks_of(even), asks_of(odd))
     mask = theirs[number - 2 : number - 1, :]
     tile[...] = chosen(mask, pair[0:rows].astype(F32), pair[rows:].astype(F32))
     relayed[...] = mine[0:8, :]
@@ -118,37 +123,37 @@
     ]
 
 
-def early_kernel(steps, two, first, meta, group, part, blocks, vert, *refs):
-    near, number = len(steps) - 2, len(steps)
-    arrived, refs = refs[:near], refs[near:]
-    sums = less_sources([part[0], part[1]], number, meta, blocks, list(enumerate(arrived)))
-    if first:
-        beside, (out, masks) = refs[:-2], refs[-2:]
-        sums = less_beside(sums, two, group, vert, beside)
-        for i in range(near):
-            asking = arrived[steps.index(-steps[i])]
-            masks[i : i + 1, :] = asks_of(asking)[i : i + 1, :]
-    else:
-        (out,) = refs
-    out[0], out[1] = sums
-
-
-def late_kernel(number, two, first, meta, group, total, blocks, vert, *refs):
-    sides = 0 if first else 1 if two else 2
-    far, beside, refs = refs[:2], refs[2 : 2 + sides], refs[2 + sides :]
-    numbered = list(enumerate(far, number - 2))
-    sums = less_sources([total[0], total[1]], number, meta, blocks, numbered)
-    if beside:
-        sums = less_beside(sums, two, group, vert, beside)
-    low, high = sums
-    told, refs = refs[: 2 if first else 1], refs[2 if first else 1 :]
+def local_kernel(number, two, first_index, meta, group, part, blocks, vert, *refs):
+    sides = 1 if two else 2
+    arrived, beside, out = refs[: -sides - 1], refs[-sides - 1 : -1], refs[-1]
+    numbered = list(enumerate(arrived, first_index))
+    sums = less_sources([part[0], part[1]], number, meta, blocks, numbered)
+    out[0], out[1] = less_beside(sums, two, group, vert, beside)
+
+
+def cross_kernel(number, meta, blocks, *refs):
+    arrived, out = refs[:-1], refs[-1]
+    zero = jnp.zeros(out.shape[1:], F32)
+    out[0], out[1] = less_sources([zero, zero], number, meta, blocks, list(enumerate(arrived)))
+
+
+def far_kernel(number, meta, blocks, cross, passed, pair, out):
+    numbered = list(enumerate([passed, pair], number - 2))
+    out[0], out[1] = less_sources([cross[0], cross[1]], number, meta, blocks, numbered)
+
+
+def update_kernel(number, two, first, group, total, far, *refs):
+    low, high = total[0] + far[0], total[1] + far[1]
+    count = number - 1 if first else 1
+    told, refs = refs[:count], refs[count:]
     lam, sends, refs = refs[0], refs[1 : 1 + number], refs[1 + number :]
     outer, refs = refs[: 1 if two else 2], refs[1 if two else 2 :]
     masks = told[0]
     if first:
         masks = refs[0]
-        masks[0 : number - 2, :] = told[0][0 : number - 2, :]
-        masks[number - 2 : number, :] = told[1][number - 2 : number, :]
+        for i in range(number - 2):
+            masks[i : i + 1, :] = asks_of(told[i])[i : i + 1, :]
+        masks[number - 2 : number, :] = told[-1][number - 2 : number, :]
     rows = low.shape[0]
     lam[0:rows] = low.astype(BF16)
     lam[rows:] = high.astype(BF16)
@@ -161,11 +166,8 @@
         outer[1][...] = low.astype(BF16)
 
 
-def last_kernel(number, two, columns, meta, group, wells, gains, total, blocks, vert, sens, basis, *refs):
-    far, beside, (lam, pieces) = refs[:2], refs[2:-2], refs[-2:]
-    numbered = list(enumerate(far, number - 2))
-    sums = less_sources([total[0], total[1]], number, meta, blocks, numbered)
-    sums = less_beside(sums, two, group, vert, beside)
+def last_kernel(columns, two, wells, gains, total, far, sens, basis, lam, pieces):
+    sums = [total[0] + far[0], total[1] + far[1]]
     phases, _, cells = sens.shape
     spot = lax.broadcasted_iota(jnp.int32, (1, cells), 1)
     projected = None
@@ -217,9 +219,12 @@
     )(*ins)
 
 
-def shift(x, k):
-    columns = lax.axis_size("areal")
-    return held(lax.ppermute(x, "areal", [(i, (i - k) % columns) for i in range(columns)]))
+def moved_by(x, pairs):
+    return held(lax.ppermute(x, "areal", pairs))
+
+
+def shift_pairs(columns, k):
+    return [(i, (i - k) % columns) for i in range(columns)]
 
 
 def beside_layers(tiles):
@@ -253,7 +258,9 @@
     rows, width = rhs.shape[2:]
     modes = basis.shape[-1]
     number = conn_src.shape[-1]
-    steps = near_steps(number) + far_steps(columns)
+    swaps = near_swaps(number)
+    routes = [swap_pairs(columns, k, color) for k, color in swaps]
+    routes += [shift_pairs(columns, columns // 2 + 1), shift_pairs(columns, columns // 2)]
     rhs = rhs[0].reshape(2 * rows, width)
     me = lax.axis_index("areal").astype(jnp.int32).reshape(1)
     group = lax.axis_index("layer").astype(jnp.int32).reshape(1)
@@ -265,9 +272,9 @@
     partial = functools.partial
 
     with jax.named_scope("plan"):
-        far_pair = shift(rhs, steps[-1])
+        far_pair = moved_by(rhs, routes[-1])
         meta, payload = call(
-            partial(plan_kernel, columns, steps),
+            partial(plan_kernel, columns, swaps),
             [jax.ShapeDtypeStruct((3 * number,), jnp.int32), pltpu.VMEM((2 * rows + 16, width), BF16)],
             (outside(conn_src[0, 0]), conn_count[0], outside(tile_map), me, outside(rhs)),
             [SMEM] * 4 + [VMEM],
@@ -294,36 +301,51 @@
     for step in range(ITERS):
         first = step == 0
         with jax.named_scope("apply"):
-            arrived = [shift(x, k) for x, k in zip(sends, steps)]
+            arrived = [moved_by(x, pairs) for x, pairs in zip(sends, routes)]
             if first:
+                even, odd = (arrived[swaps.index((1, color))] for color in (1, 0))
                 picked, relayed = call(
                     partial(far_pick_kernel, number),
                     [tile, masks_type],
-                    (far_pair, payload, arrived[steps.index(-1)]),
-                    [VMEM] * 3,
+                    (me, far_pair, payload, even, odd),
+                    [SMEM] + [VMEM] * 4,
                 )
-                arrived = [*arrived, shift(picked, 1), far_pair]
-                told = shift(relayed, steps[-1])
+                arrived = [*arrived, moved_by(picked, shift_pairs(columns, 1)), far_pair]
+                told = moved_by(relayed, routes[-1])
             beside = beside_layers(outer)
-            (part,) = call(own_kernel, [sums], (lam, rhs_held, vert), [VMEM] * 3, flops=2 * one)
-            tiles = arrived[:-2] + (beside if first else [])
-            total, *rest = call(
-                partial(early_kernel, steps, two, first),
-                [sums] + ([masks_type] if first else []),
+            (part,) = call(own_kernel, [sums], (lam, rhs_held, vert), [VMEM] * 3, flops=one)
+            half = len(swaps) // 2
+            tiles = arrived[half:-2] + beside
+            (total,) = call(
+                partial(local_kernel, number, two, half),
+                [sums],
                 (meta, group, held(part), blocks, vert, *tiles),
                 [SMEM] * 2 + [VMEM] * (3 + len(tiles)),
-                flops=2 * (number - 2) * one,
+                flops=one,
             )
-            total = held(total)
-            told = [held(rest[0]), told] if first else [masks]
-            tiles = arrived[-2:] + ([] if first else beside)
+            (cross,) = call(
+                partial(cross_kernel, number),
+                [sums],
+                (meta, blocks, *arrived[:half]),
+                [SMEM] + [VMEM] * (1 + half),
+                flops=4 * one,
+            )
+            (far,) = call(
+                partial(far_kernel, number),
+                [sums],
+                (meta, blocks, held(cross), *arrived[-2:]),
+                [SMEM] + [VMEM] * 4,
+                flops=4 * one,
+            )
+            total, far = held(total), held(far)
+            told = [*arrived[:-2], told] if first else [masks]
             if step < ITERS - 1:
                 lam, *rest = call(
-                    partial(late_kernel, number, two, first),
+                    partial(update_kernel, number, two, first),
                     [pair] + [tile] * (number + len(beside)) + ([masks_type] if first else []),
-                    (meta, group, total, blocks, vert, *tiles, *told),
-                    [SMEM] * 2 + [VMEM] * (3 + len(tiles) + len(told)),
-                    flops=4 * one,
+                    (group, total, far, *told),
+                    [SMEM] + [VMEM] * (2 + len(told)),
+                    flops=one,
                 )
                 lam = held(lam)
                 if first:
@@ -331,16 +353,16 @@
                 sends, outer = rest[:number], rest[number:]
             else:
                 adjoint, pieces = call(
-                    partial(last_kernel, number, two, columns),
+                    partial(last_kernel, columns, two),
                     [
                         jax.ShapeDtypeStruct((2, rows, width), BF16),
                         pltpu.VMEM(
                             (2 * columns, modes // columns // 2, rows) if two else (rows, modes), F32
                         ),
                     ],
-                    (meta, group, well_cells[0], well_gain[0], total, blocks, vert, held(sens[0].transpose(1, 0, 2)), held(basis[0]), *tiles),
-                    [SMEM] * 4 + [VMEM] * (5 + len(tiles)),
-                    flops=5 * one,
+                    (well_cells[0], well_gain[0], total, far, held(sens[0].transpose(1, 0, 2)), held(basis[0])),
+                    [SMEM] * 2 + [VMEM] * 4,
+                    flops=one,
                 )
 
     with jax.named_scope("project"):

time: 81.2 us -> 77.7 us (0.957)
  waiting for transfers between devices: 12.7 us -> 8.2 us
  starting transfers between devices: 42.4 us -> 39.1 us
  Pallas kernels: 13.1 us -> 15.8 us
  blocking collectives: 11.3 us -> 12.7 us
    ppermute x19, waiting for transfers between devices: 12.7 us -> 8.19 us  [moved_by(): return held(lax.ppermute(x, 'areal', pairs))]
    ppermute x19, starting transfers between devices: 42.4 us -> 39.1 us  [moved_by(): return held(lax.ppermute(x, 'areal', pairs))]
    pallas_call x13 -> x19, Pallas kernels: 13.1 us -> 15.8 us  [call(): pl.pallas_call(kernel, out_shape=outs, in_specs=specs, out_specs=out_spec...]
    all_to_all x1, blocking collectives: 11.3 us -> 12.7 us  [on_device(): landed = lax.all_to_all(pieces, ('areal', 'layer'), 0, 0, tiled=True)]
  transfers between devices with their start and end apart: 22 -> 22, of which waited for: 6 -> 6; matrix products, arithmetic and copies ran while one was open for 0% -> 0% of each run, Pallas kernels for 11% -> 15%
where the time goes in v1:
time: 77.7 us; the launch traced here: 77.5 us
  starting transfers between devices  39.1 us (50%)
  Pallas kernels  15.8 us (20%)
  blocking collectives  12.7 us (16%)
  waiting for transfers between devices  8.2 us (11%)
  between operations  1.58 us (2%)
    ppermute x19, starting transfers between devices, moved_by(): return held(lax.ppermute(x, 'areal', pairs))  39.1 us
    pallas_call x19, Pallas kernels, call(): pl.pallas_call(kernel, out_shape=outs, in_specs=specs, out_specs=out_spec...  15.8 us
    all_to_all x1, blocking collectives, on_device(): landed = lax.all_to_all(pieces, ('areal', 'layer'), 0, 0, tiled=True)  12.7 us
    ppermute x19, waiting for transfers between devices, moved_by(): return held(lax.ppermute(x, 'areal', pairs))  8.19 us
  transfers between devices with their start and end apart: 22, of which 6 were waited for; matrix products, arithmetic and copies ran while one was open for 0% of the time, Pallas kernels for 15%

profile of v1, /device:TPU:0, one launch (start us, length us, event | category | flops | bytes accessed | tf_op | source)
XLA Modules:
  0.0 77.5 jit_solution(5650113817877169995)
XLA Ops:
  0.6 4.1 %collective-permute-start.5 = (bf16[224,384]{1,0:T(8,128)(2,1)}, bf16[224,384]{1,0:T(8,128)(2,1)S(1)}, u32[]{:S(2)}, u32[]{:S(2)}) collective-permute-start(bf16[224,384]{1,0:T(8,128)(2,1)} %bitcast.16), channel_id=1, source_target_pairs={{0,16},{2,18},{4,20},{6,22},{8,24},{10,26},{12,28},{14,30},{16,0},... | collective-permute-start | bytes 516104 | tf_op jit(solution)/shard_map/plan/ppermute | solution.py:223
  5.4 1.6 %plan.1 = (s32[18]{0:T(128)S(1)}, bf16[240,384]{1,0:T(8,128)(2,1)S(1)}) custom-call(s32[6]{0:T(128)} %bitcast.29, s32[1]{0:T(128)} %bitcast.15.count, s32[32]{0:T(128)} %tile_map.1, s32[1]{0:T(128)} %bitcast.4.me, bf16[224,384]{1,0:T(8,128)(2,1)} %bitcast.17), custom_call_target="tpu_custom_call" | custom-call | tf_op jit(solution)/shard_map/plan/pallas_call | solution.py:209
  7.0 3.3 %collective-permute-start.4 = (bf16[240,384]{1,0:T(8,128)(2,1)S(1)}, bf16[240,384]{1,0:T(8,128)(2,1)S(1)}, u32[]{:S(2)}, u32[]{:S(2)}) collective-permute-start(bf16[240,384]{1,0:T(8,128)(2,1)S(1)} %get-tuple-element.30.own), channel_id=1, source_target_pairs={{0,30},{2,4},{4,2},{6,8},{8,6},{10,12},{12,10},{14,16},{16,14},{18... | collective-permute-start | bytes 552968 | tf_op jit(solution)/shard_map/apply/ppermute | solution.py:223
  10.3 1.3 %collective-permute-start = (bf16[240,384]{1,0:T(8,128)(2,1)S(1)}, bf16[240,384]{1,0:T(8,128)(2,1)S(1)}, u32[]{:S(2)}, u32[]{:S(2)}) collective-permute-start(bf16[240,384]{1,0:T(8,128)(2,1)S(1)} %get-tuple-element.30.own), channel_id=1, source_target_pairs={{0,4},{2,6},{4,0},{6,2},{8,12},{10,14},{12,8},{14,10},{16,20},{18,... | collective-permute-start | bytes 552968 | tf_op jit(solution)/shard_map/apply/ppermute | solution.py:223
  11.6 2.3 %collective-permute-done.5.pair = bf16[224,384]{1,0:T(8,128)(2,1)S(1)} collective-permute-done((bf16[224,384]{1,0:T(8,128)(2,1)}, bf16[224,384]{1,0:T(8,128)(2,1)S(1)}, u32[]{:S(2)}, u32[]{:S(2)}) %collective-permute-start.5) | collective-permute-done | bytes 172064 | tf_op jit(solution)/shard_map/plan/ppermute | solution.py:223
  13.8 3.7 %collective-permute-start.3 = (bf16[240,384]{1,0:T(8,128)(2,1)S(1)}, bf16[240,384]{1,0:T(8,128)(2,1)S(1)}, u32[]{:S(2)}, u32[]{:S(2)}) collective-permute-start(bf16[240,384]{1,0:T(8,128)(2,1)S(1)} %get-tuple-element.30.own), channel_id=1, source_target_pairs={{0,28},{2,30},{4,8},{6,10},{8,4},{10,6},{12,16},{14,18},{16,12},{1... | collective-permute-start | bytes 552968 | tf_op jit(solution)/shard_map/apply/ppermute | solution.py:223
  18.1 2.3 %collective-permute-start.6 = (bf16[112,384]{1,0:T(8,128)(2,1)S(1)}, bf16[112,384]{1,0:T(8,128)(2,1)S(1)}, u32[]{:S(2)}, u32[]{:S(2)}) collective-permute-start(bf16[112,384]{1,0:T(8,128)(2,1)S(1)} %get-tuple-element.31), channel_id=1, source_target_pairs={{0,30},{2,0},{4,2},{6,4},{8,6},{10,8},{12,10},{14,12},{16,14},{18,... | collective-permute-start | bytes 258056 | tf_op jit(solution)/shard_map/apply/ppermute | solution.py:223
  20.4 2.4 %load.1 = (bf16[2,6,384,384]{3,2,1,0:T(8,128)(2,1)S(1)}, bf16[2,2,384,384]{3,2,1,0:T(8,128)(2,1)S(1)}) custom-call(bf16[2,6,384,384]{3,2,1,0:T(8,128)(2,1)} %bitcast.26, bf16[2,2,384,384]{3,2,1,0:T(8,128)(2,1)} %bitcast.27), custom_call_target="tpu_custom_call" | custom-call | bytes 4718592 | tf_op jit(solution)/shard_map/load/pallas_call | solution.py:209
  23.1 4.7 %collective-permute-start.7 = (f32[8,384]{1,0:T(8,128)S(1)}, f32[8,384]{1,0:T(8,128)S(1)}, u32[]{:S(2)}, u32[]{:S(2)}) collective-permute-start(f32[8,384]{1,0:T(8,128)S(1)} %get-tuple-element.32), channel_id=1, source_target_pairs={{0,16},{2,18},{4,20},{6,22},{8,24},{10,26},{12,28},{14,30},{16,0},... | collective-permute-start | bytes 36872 | tf_op jit(solution)/shard_map/apply/ppermute | solution.py:223
  27.8 1.0 %apply.17.total = f32[2,112,384]{2,1,0:T(8,128)S(1)} custom-call(s32[18]{0:T(128)S(1)} %get-tuple-element.27.meta, s32[1]{0:T(128)} %bitcast.6.group, f32[2,112,384]{2,1,0:T(8,128)S(1)} %apply.16.part, bf16[2,6,384,384]{3,2,1,0:T(8,128)(2,1)S(1)} %get-tuple-element.29.blocks, bf16[2,2,384,384]{3,2,1,0:T(8,128)(2,1)S(1)} %get-tuple-element.28.vert, ...), custom_call_target="tpu_custom_call" | custom-call | flops 33030144 | bytes 165150 | tf_op jit(solution)/shard_map/apply/pallas_call | solution.py:209
  28.8 0.9 %apply.18.cross = f32[2,112,384]{2,1,0:T(8,128)S(1)} custom-call(s32[18]{0:T(128)S(1)} %get-tuple-element.27.meta, bf16[2,6,384,384]{3,2,1,0:T(8,128)(2,1)S(1)} %get-tuple-element.29.blocks, bf16[240,384]{1,0:T(8,128)(2,1)S(1)} %collective-permute-done.3.refs_0_, bf16[240,384]{1,0:T(8,128)(2,1)S(1)} %collective-permute-done.4.refs_1_.even), custom_call_target="tpu_custom_call" | custom-call | flops 132120576 | bytes 660602 | tf_op jit(solution)/shard_map/apply/pallas_call | solution.py:209
  31.0 6.1 %collective-permute-start.12 = (bf16[112,384]{1,0:T(8,128)(2,1)S(1)}, bf16[112,384]{1,0:T(8,128)(2,1)S(1)}, u32[]{:S(2)}, u32[]{:S(2)}) collective-permute-start(bf16[112,384]{1,0:T(8,128)(2,1)S(1)} %get-tuple-element.38), channel_id=1, source_target_pairs={{0,30},{2,4},{4,2},{6,8},{8,6},{10,12},{12,10},{14,16},{16,14},{18... | collective-permute-start | bytes 258056 | tf_op jit(solution)/shard_map/apply/ppermute | solution.py:223
  37.7 1.8 %collective-permute-done.11.refs_0_ = bf16[112,384]{1,0:T(8,128)(2,1)S(1)} collective-permute-done((bf16[112,384]{1,0:T(8,128)(2,1)S(1)}, bf16[112,384]{1,0:T(8,128)(2,1)S(1)}, u32[]{:S(2)}, u32[]{:S(2)}) %collective-permute-start.11) | collective-permute-done | bytes 86048 | tf_op jit(solution)/shard_map/apply/ppermute | solution.py:223
  39.5 2.1 %collective-permute-start.9 = (bf16[112,384]{1,0:T(8,128)(2,1)S(1)}, bf16[112,384]{1,0:T(8,128)(2,1)S(1)}, u32[]{:S(2)}, u32[]{:S(2)}) collective-permute-start(bf16[112,384]{1,0:T(8,128)(2,1)S(1)} %get-tuple-element.35), channel_id=1, source_target_pairs={{0,2},{2,0},{4,6},{6,4},{8,10},{10,8},{12,14},{14,12},{16,18},{18,... | collective-permute-start | bytes 258056 | tf_op jit(solution)/shard_map/apply/ppermute | solution.py:223
  41.5 1.0 %collective-permute-done.12.refs_1_ = bf16[112,384]{1,0:T(8,128)(2,1)S(1)} collective-permute-done((bf16[112,384]{1,0:T(8,128)(2,1)S(1)}, bf16[112,384]{1,0:T(8,128)(2,1)S(1)}, u32[]{:S(2)}, u32[]{:S(2)}) %collective-permute-start.12) | collective-permute-done | bytes 86048 | tf_op jit(solution)/shard_map/apply/ppermute | solution.py:223
  44.8 1.0 %apply.23.total = f32[2,112,384]{2,1,0:T(8,128)S(1)} custom-call(s32[18]{0:T(128)S(1)} %get-tuple-element.27.meta, s32[1]{0:T(128)} %bitcast.6.group, f32[2,112,384]{2,1,0:T(8,128)S(1)} %apply.22.part, bf16[2,6,384,384]{3,2,1,0:T(8,128)(2,1)S(1)} %get-tuple-element.29.blocks, bf16[2,2,384,384]{3,2,1,0:T(8,128)(2,1)S(1)} %get-tuple-element.28.vert, ...), custom_call_target="tpu_custom_call" | custom-call | flops 33030144 | bytes 165150 | tf_op jit(solution)/shard_map/apply/pallas_call | solution.py:209
  45.9 3.6 %collective-permute-start.18 = (bf16[112,384]{1,0:T(8,128)(2,1)S(1)}, bf16[112,384]{1,0:T(8,128)(2,1)S(1)}, u32[]{:S(2)}, u32[]{:S(2)}) collective-permute-start(bf16[112,384]{1,0:T(8,128)(2,1)S(1)} %get-tuple-element.46), channel_id=1, source_target_pairs={{0,28},{2,30},{4,8},{6,10},{8,4},{10,6},{12,16},{14,18},{16,12},{1... | collective-permute-start | bytes 258056 | tf_op jit(solution)/shard_map/apply/ppermute | solution.py:223
  49.6 2.1 %collective-permute-start.19 = (bf16[112,384]{1,0:T(8,128)(2,1)S(1)}, bf16[112,384]{1,0:T(8,128)(2,1)S(1)}, u32[]{:S(2)}, u32[]{:S(2)}) collective-permute-start(bf16[112,384]{1,0:T(8,128)(2,1)S(1)} %get-tuple-element.47), channel_id=1, source_target_pairs={{0,30},{2,4},{4,2},{6,8},{8,6},{10,12},{12,10},{14,16},{16,14},{18... | collective-permute-start | bytes 258056 | tf_op jit(solution)/shard_map/apply/ppermute | solution.py:223
  51.7 4.0 %collective-permute-start.21 = (bf16[112,384]{1,0:T(8,128)(2,1)S(1)}, bf16[112,384]{1,0:T(8,128)(2,1)S(1)}, u32[]{:S(2)}, u32[]{:S(2)}) collective-permute-start(bf16[112,384]{1,0:T(8,128)(2,1)S(1)} %get-tuple-element.49), channel_id=1, source_target_pairs={{0,16},{2,18},{4,20},{6,22},{8,24},{10,26},{12,28},{14,30},{16,0},... | collective-permute-start | bytes 258056 | tf_op jit(solution)/shard_map/apply/ppermute | solution.py:223
  55.7 1.1 %collective-permute-start.16 = (bf16[112,384]{1,0:T(8,128)(2,1)S(1)}, bf16[112,384]{1,0:T(8,128)(2,1)S(1)}, u32[]{:S(2)}, u32[]{:S(2)}) collective-permute-start(bf16[112,384]{1,0:T(8,128)(2,1)S(1)} %get-tuple-element.44), channel_id=1, source_target_pairs={{0,2},{2,0},{4,6},{6,4},{8,10},{10,8},{12,14},{14,12},{16,18},{18,... | collective-permute-start | bytes 258056 | tf_op jit(solution)/shard_map/apply/ppermute | solution.py:223
  56.9 1.7 %collective-permute-done.19.refs_1_ = bf16[112,384]{1,0:T(8,128)(2,1)S(1)} collective-permute-done((bf16[112,384]{1,0:T(8,128)(2,1)S(1)}, bf16[112,384]{1,0:T(8,128)(2,1)S(1)}, u32[]{:S(2)}, u32[]{:S(2)}) %collective-permute-start.19) | collective-permute-done | bytes 86048 | tf_op jit(solution)/shard_map/apply/ppermute | solution.py:223
  61.7 1.0 %apply.28.total = f32[2,112,384]{2,1,0:T(8,128)S(1)} custom-call(s32[18]{0:T(128)S(1)} %get-tuple-element.27.meta, s32[1]{0:T(128)} %bitcast.6.group, f32[2,112,384]{2,1,0:T(8,128)S(1)} %apply.27.part, bf16[2,6,384,384]{3,2,1,0:T(8,128)(2,1)S(1)} %get-tuple-element.29.blocks, bf16[2,2,384,384]{3,2,1,0:T(8,128)(2,1)S(1)} %get-tuple-element.28.vert, ...), custom_call_target="tpu_custom_call" | custom-call | flops 33030144 | bytes 165150 | tf_op jit(solution)/shard_map/apply/pallas_call | solution.py:209
  62.8 1.3 %apply.31 = (bf16[2,112,384]{2,1,0:T(8,128)(2,1)}, f32[32,8,112]{2,1,0:T(8,128)S(1)}) custom-call(s32[2,4]{1,0:T(2,128)S(1)} %bitcast.24, f32[2,4]{1,0:T(2,128)S(1)} %bitcast.25, f32[2,112,384]{2,1,0:T(8,128)S(1)} %apply.28.total, f32[2,112,384]{2,1,0:T(8,128)S(1)} %apply.30.far, f32[3,2,128]{2,1,0:T(2,128)S(1)} %bitcast.23, bf16[2,128,256]{2,1,0:T(8,128)(2,1)S(1)} %bitcast.22), custom_call_target="tpu_custom_call" | custom-call | flops 33030144 | bytes 165150 | tf_op jit(solution)/shard_map/apply/pallas_call | solution.py:209
  64.1 12.7 %all_to_all.5.pieces = f32[32,8,112]{2,1,0:T(8,128)S(1)} all-to-all(f32[32,8,112]{2,1,0:T(8,128)S(1)} %get-tuple-element.51), channel_id=1, replica_groups=mesh['areal'=16,'layer'=2] {'areal','layer'}, dimensions={0} | all-to-all | bytes 229376 | tf_op jit(solution)/shard_map/project/all_to_all | solution.py:370
  (50 shorter events, 8.8 us)
Async XLA Ops:
  0.6 22.1 %copy-start = (bf16[1,2,112,384]{3,2,1,0:T(8,128)(2,1)S(1)}, bf16[1,2,112,384]{3,2,1,0:T(8,128)(2,1)}, u32[]{:S(2)}) copy-start(bf16[1,2,112,384]{3,2,1,0:T(8,128)(2,1)} %param.10) | copy-start | bytes 516100
  0.6 13.2 %collective-permute-start.5 = (bf16[224,384]{1,0:T(8,128)(2,1)}, bf16[224,384]{1,0:T(8,128)(2,1)S(1)}, u32[]{:S(2)}, u32[]{:S(2)}) collective-permute-start(bf16[224,384]{1,0:T(8,128)(2,1)} %bitcast.16), channel_id=1, source_target_pairs={{0,16},{2,18},{4,20},{6,22},{8,24},{10,26},{12,28},{14,30},{16,0},... | collective-permute-start | bytes 516104 | tf_op jit(solution)/shard_map/plan/ppermute | solution.py:223
  7.0 10.5 %collective-permute-start.4 = (bf16[240,384]{1,0:T(8,128)(2,1)S(1)}, bf16[240,384]{1,0:T(8,128)(2,1)S(1)}, u32[]{:S(2)}, u32[]{:S(2)}) collective-permute-start(bf16[240,384]{1,0:T(8,128)(2,1)S(1)} %get-tuple-element.30.own), channel_id=1, source_target_pairs={{0,30},{2,4},{4,2},{6,8},{8,6},{10,12},{12,10},{14,16},{16,14},{18... | collective-permute-start | bytes 552968 | tf_op jit(solution)/shard_map/apply/ppermute | solution.py:223
  10.3 7.8 %collective-permute-start.1 = (bf16[240,384]{1,0:T(8,128)(2,1)S(1)}, bf16[240,384]{1,0:T(8,128)(2,1)S(1)}, u32[]{:S(2)}, u32[]{:S(2)}) collective-permute-start(bf16[240,384]{1,0:T(8,128)(2,1)S(1)} %get-tuple-element.30.own), channel_id=1, source_target_pairs={{0,2},{2,0},{4,6},{6,4},{8,10},{10,8},{12,14},{14,12},{16,18},{18,... | collective-permute-start | bytes 552968 | tf_op jit(solution)/shard_map/apply/ppermute | solution.py:223
  10.3 17.5 %collective-permute-start.2 = (bf16[240,384]{1,0:T(8,128)(2,1)S(1)}, bf16[240,384]{1,0:T(8,128)(2,1)S(1)}, u32[]{:S(2)}, u32[]{:S(2)}) collective-permute-start(bf16[240,384]{1,0:T(8,128)(2,1)S(1)} %get-tuple-element.30.own), channel_id=1, source_target_pairs={{0,1},{1,0},{2,3},{3,2},{4,5},{5,4},{6,7},{7,6},{8,9},{9,8},{10,11... | collective-permute-start | bytes 552968 | tf_op jit(solution)/shard_map/apply/ppermute | solution.py:233
  10.3 17.5 %collective-permute-start = (bf16[240,384]{1,0:T(8,128)(2,1)S(1)}, bf16[240,384]{1,0:T(8,128)(2,1)S(1)}, u32[]{:S(2)}, u32[]{:S(2)}) collective-permute-start(bf16[240,384]{1,0:T(8,128)(2,1)S(1)} %get-tuple-element.30.own), channel_id=1, source_target_pairs={{0,4},{2,6},{4,0},{6,2},{8,12},{10,14},{12,8},{14,10},{16,20},{18,... | collective-permute-start | bytes 552968 | tf_op jit(solution)/shard_map/apply/ppermute | solution.py:223
  13.8 15.0 %collective-permute-start.3 = (bf16[240,384]{1,0:T(8,128)(2,1)S(1)}, bf16[240,384]{1,0:T(8,128)(2,1)S(1)}, u32[]{:S(2)}, u32[]{:S(2)}) collective-permute-start(bf16[240,384]{1,0:T(8,128)(2,1)S(1)} %get-tuple-element.30.own), channel_id=1, source_target_pairs={{0,28},{2,30},{4,8},{6,10},{8,4},{10,6},{12,16},{14,18},{16,12},{1... | collective-permute-start | bytes 552968 | tf_op jit(solution)/shard_map/apply/ppermute | solution.py:223
  18.1 11.7 %collective-permute-start.6 = (bf16[112,384]{1,0:T(8,128)(2,1)S(1)}, bf16[112,384]{1,0:T(8,128)(2,1)S(1)}, u32[]{:S(2)}, u32[]{:S(2)}) collective-permute-start(bf16[112,384]{1,0:T(8,128)(2,1)S(1)} %get-tuple-element.31), channel_id=1, source_target_pairs={{0,30},{2,0},{4,2},{6,4},{8,6},{10,8},{12,10},{14,12},{16,14},{18,... | collective-permute-start | bytes 258056 | tf_op jit(solution)/shard_map/apply/ppermute | solution.py:223
  23.1 7.7 %collective-permute-start.7 = (f32[8,384]{1,0:T(8,128)S(1)}, f32[8,384]{1,0:T(8,128)S(1)}, u32[]{:S(2)}, u32[]{:S(2)}) collective-permute-start(f32[8,384]{1,0:T(8,128)S(1)} %get-tuple-element.32), channel_id=1, source_target_pairs={{0,16},{2,18},{4,20},{6,22},{8,24},{10,26},{12,28},{14,30},{16,0},... | collective-permute-start | bytes 36872 | tf_op jit(solution)/shard_map/apply/ppermute | solution.py:223
  30.9 8.5 %collective-permute-start.11 = (bf16[112,384]{1,0:T(8,128)(2,1)S(1)}, bf16[112,384]{1,0:T(8,128)(2,1)S(1)}, u32[]{:S(2)}, u32[]{:S(2)}) collective-permute-start(bf16[112,384]{1,0:T(8,128)(2,1)S(1)} %get-tuple-element.37), channel_id=1, source_target_pairs={{0,28},{2,30},{4,8},{6,10},{8,4},{10,6},{12,16},{14,18},{16,12},{1... | collective-permute-start | bytes 258056 | tf_op jit(solution)/shard_map/apply/ppermute | solution.py:223
  31.0 11.5 %collective-permute-start.12 = (bf16[112,384]{1,0:T(8,128)(2,1)S(1)}, bf16[112,384]{1,0:T(8,128)(2,1)S(1)}, u32[]{:S(2)}, u32[]{:S(2)}) collective-permute-start(bf16[112,384]{1,0:T(8,128)(2,1)S(1)} %get-tuple-element.38), channel_id=1, source_target_pairs={{0,30},{2,4},{4,2},{6,8},{8,6},{10,12},{12,10},{14,16},{16,14},{18... | collective-permute-start | bytes 258056 | tf_op jit(solution)/shard_map/apply/ppermute | solution.py:223
  37.1 6.6 %collective-permute-start.13 = (bf16[112,384]{1,0:T(8,128)(2,1)S(1)}, bf16[112,384]{1,0:T(8,128)(2,1)S(1)}, u32[]{:S(2)}, u32[]{:S(2)}) collective-permute-start(bf16[112,384]{1,0:T(8,128)(2,1)S(1)} %get-tuple-element.39), channel_id=1, source_target_pairs={{0,14},{2,16},{4,18},{6,20},{8,22},{10,24},{12,26},{14,28},{16,30}... | collective-permute-start | bytes 258056 | tf_op jit(solution)/shard_map/apply/ppermute | solution.py:223
  37.1 6.6 %collective-permute-start.14 = (bf16[112,384]{1,0:T(8,128)(2,1)S(1)}, bf16[112,384]{1,0:T(8,128)(2,1)S(1)}, u32[]{:S(2)}, u32[]{:S(2)}) collective-permute-start(bf16[112,384]{1,0:T(8,128)(2,1)S(1)} %get-tuple-element.40), channel_id=1, source_target_pairs={{0,16},{2,18},{4,20},{6,22},{8,24},{10,26},{12,28},{14,30},{16,0},... | collective-permute-start | bytes 258056 | tf_op jit(solution)/shard_map/apply/ppermute | solution.py:223
  37.7 7.0 %collective-permute-start.8 = (bf16[112,384]{1,0:T(8,128)(2,1)S(1)}, bf16[112,384]{1,0:T(8,128)(2,1)S(1)}, u32[]{:S(2)}, u32[]{:S(2)}) collective-permute-start(bf16[112,384]{1,0:T(8,128)(2,1)S(1)} %get-tuple-element.34), channel_id=1, source_target_pairs={{0,4},{2,6},{4,0},{6,2},{8,12},{10,14},{12,8},{14,10},{16,20},{18,... | collective-permute-start | bytes 258056 | tf_op jit(solution)/shard_map/apply/ppermute | solution.py:223
  39.5 5.3 %collective-permute-start.9 = (bf16[112,384]{1,0:T(8,128)(2,1)S(1)}, bf16[112,384]{1,0:T(8,128)(2,1)S(1)}, u32[]{:S(2)}, u32[]{:S(2)}) collective-permute-start(bf16[112,384]{1,0:T(8,128)(2,1)S(1)} %get-tuple-element.35), channel_id=1, source_target_pairs={{0,2},{2,0},{4,6},{6,4},{8,10},{10,8},{12,14},{14,12},{16,18},{18,... | collective-permute-start | bytes 258056 | tf_op jit(solution)/shard_map/apply/ppermute | solution.py:223
  42.5 2.2 %collective-permute-start.10 = (bf16[112,384]{1,0:T(8,128)(2,1)S(1)}, bf16[112,384]{1,0:T(8,128)(2,1)S(1)}, u32[]{:S(2)}, u32[]{:S(2)}) collective-permute-start(bf16[112,384]{1,0:T(8,128)(2,1)S(1)} %get-tuple-element.36), channel_id=1, source_target_pairs={{0,1},{1,0},{2,3},{3,2},{4,5},{5,4},{6,7},{7,6},{8,9},{9,8},{10,11... | collective-permute-start | bytes 258056 | tf_op jit(solution)/shard_map/apply/ppermute | solution.py:233
  45.9 9.8 %collective-permute-start.18 = (bf16[112,384]{1,0:T(8,128)(2,1)S(1)}, bf16[112,384]{1,0:T(8,128)(2,1)S(1)}, u32[]{:S(2)}, u32[]{:S(2)}) collective-permute-start(bf16[112,384]{1,0:T(8,128)(2,1)S(1)} %get-tuple-element.46), channel_id=1, source_target_pairs={{0,28},{2,30},{4,8},{6,10},{8,4},{10,6},{12,16},{14,18},{16,12},{1... | collective-permute-start | bytes 258056 | tf_op jit(solution)/shard_map/apply/ppermute | solution.py:223
  49.6 9.0 %collective-permute-start.19 = (bf16[112,384]{1,0:T(8,128)(2,1)S(1)}, bf16[112,384]{1,0:T(8,128)(2,1)S(1)}, u32[]{:S(2)}, u32[]{:S(2)}) collective-permute-start(bf16[112,384]{1,0:T(8,128)(2,1)S(1)} %get-tuple-element.47), channel_id=1, source_target_pairs={{0,30},{2,4},{4,2},{6,8},{8,6},{10,12},{12,10},{14,16},{16,14},{18... | collective-permute-start | bytes 258056 | tf_op jit(solution)/shard_map/apply/ppermute | solution.py:223
  51.7 9.0 %collective-permute-start.20 = (bf16[112,384]{1,0:T(8,128)(2,1)S(1)}, bf16[112,384]{1,0:T(8,128)(2,1)S(1)}, u32[]{:S(2)}, u32[]{:S(2)}) collective-permute-start(bf16[112,384]{1,0:T(8,128)(2,1)S(1)} %get-tuple-element.48), channel_id=1, source_target_pairs={{0,14},{2,16},{4,18},{6,20},{8,22},{10,24},{12,26},{14,28},{16,30}... | collective-permute-start | bytes 258056 | tf_op jit(solution)/shard_map/apply/ppermute | solution.py:223
  51.7 9.0 %collective-permute-start.21 = (bf16[112,384]{1,0:T(8,128)(2,1)S(1)}, bf16[112,384]{1,0:T(8,128)(2,1)S(1)}, u32[]{:S(2)}, u32[]{:S(2)}) collective-permute-start(bf16[112,384]{1,0:T(8,128)(2,1)S(1)} %get-tuple-element.49), channel_id=1, source_target_pairs={{0,16},{2,18},{4,20},{6,22},{8,24},{10,26},{12,28},{14,30},{16,0},... | collective-permute-start | bytes 258056 | tf_op jit(solution)/shard_map/apply/ppermute | solution.py:223
  55.7 6.0 %collective-permute-start.15 = (bf16[112,384]{1,0:T(8,128)(2,1)S(1)}, bf16[112,384]{1,0:T(8,128)(2,1)S(1)}, u32[]{:S(2)}, u32[]{:S(2)}) collective-permute-start(bf16[112,384]{1,0:T(8,128)(2,1)S(1)} %get-tuple-element.43), channel_id=1, source_target_pairs={{0,4},{2,6},{4,0},{6,2},{8,12},{10,14},{12,8},{14,10},{16,20},{18,... | collective-permute-start | bytes 258056 | tf_op jit(solution)/shard_map/apply/ppermute | solution.py:223
  55.7 6.0 %collective-permute-start.16 = (bf16[112,384]{1,0:T(8,128)(2,1)S(1)}, bf16[112,384]{1,0:T(8,128)(2,1)S(1)}, u32[]{:S(2)}, u32[]{:S(2)}) collective-permute-start(bf16[112,384]{1,0:T(8,128)(2,1)S(1)} %get-tuple-element.44), channel_id=1, source_target_pairs={{0,2},{2,0},{4,6},{6,4},{8,10},{10,8},{12,14},{14,12},{16,18},{18,... | collective-permute-start | bytes 258056 | tf_op jit(solution)/shard_map/apply/ppermute | solution.py:223
  58.5 3.2 %collective-permute-start.17 = (bf16[112,384]{1,0:T(8,128)(2,1)S(1)}, bf16[112,384]{1,0:T(8,128)(2,1)S(1)}, u32[]{:S(2)}, u32[]{:S(2)}) collective-permute-start(bf16[112,384]{1,0:T(8,128)(2,1)S(1)} %get-tuple-element.45), channel_id=1, source_target_pairs={{0,1},{1,0},{2,3},{3,2},{4,5},{5,4},{6,7},{7,6},{8,9},{9,8},{10,11... | collective-permute-start | bytes 258056 | tf_op jit(solution)/shard_map/apply/ppermute | solution.py:233
  61.7 1.1 %copy-start.1 = (bf16[1,2,128,256]{3,2,1,0:T(8,128)(2,1)S(1)}, bf16[1,2,128,256]{3,2,1,0:T(8,128)(2,1)}, u32[]{:S(2)}) copy-start(bf16[1,2,128,256]{3,2,1,0:T(8,128)(2,1)} %param.19) | copy-start | bytes 393220
  (3 other events, 3.3 us)

commit v2 on v1

--- a/solution.py
+++ b/solution.py
@@ -33,7 +33,7 @@
     return jnp.dot(a, b, preferred_element_type=F32)
 
 
-def plan_kernel(columns, swaps, src, count, tile_map, me, rhs, meta, payload):
+def plan_kernel(columns, swaps, src, count, tile_map, me, meta, asks):
     steps = [
         jnp.where(lax.rem(lax.div(me[0], k), 2) == color, k, columns - k) for k, color in swaps
     ] + [columns // 2 + 1, columns // 2]
@@ -50,16 +50,13 @@
             hit = away == k
             conn[i] = jnp.where(hit, s, conn[i])
             slots[i] = jnp.where(hit, slot, slots[i])
-    rows = rhs.shape[0]
-    line = lax.broadcasted_iota(jnp.int32, (16, rhs.shape[1]), 0)
-    asked = jnp.zeros(line.shape, F32)
+    line = lax.broadcasted_iota(jnp.int32, asks.shape, 0)
+    asked = jnp.zeros(asks.shape, F32)
     for i in range(number):
         meta[i] = conn[i]
-        meta[number + i] = slots[i]
-        meta[2 * number + i] = jnp.where(conn[i] < count[0], 1, 0)
+        meta[number + i] = jnp.where(conn[i] < count[0], 1, 0)
         asked = jnp.where(line == i, slots[i].astype(F32), asked)
-    payload[0:rows] = rhs[...]
-    payload[rows:] = asked.astype(BF16)
+    asks[...] = asked
 
 
 def load_kernel(blocks, vert, blocks_held, vert_held, sems):
@@ -71,21 +68,18 @@
     second.wait()
 
 
-def chosen(mask, low, high):
-    return jnp.where(mask > 0.5, high, low).astype(BF16)
-
-
-def asks_of(payload):
-    return payload[payload.shape[0] - 16 :, :].astype(F32)
-
-
-def far_pick_kernel(number, me, pair, own, even, odd, tile, relayed):
-    rows = tile.shape[0]
-    mine, theirs = asks_of(own), jnp.where(lax.rem(me[0], 2) == 0, asks_of(even), asks_of(odd))
-    mask = theirs[number - 2 : number - 1, :]
-    tile[...] = chosen(mask, pair[0:rows].astype(F32), pair[rows:].astype(F32))
-    relayed[...] = mine[0:8, :]
-    relayed[number - 2 : number - 1, :] = mask
+def pick(told, sends, low, high):
+    for i, (ask, send) in enumerate(zip(told, sends)):
+        mask = ask[i : i + 1, :]
+        mask = jnp.concatenate([mask] * (send.shape[1] // mask.shape[1]), axis=1)
+        send[...] = jnp.where(mask > 0.5, high, low).astype(BF16)
+
+
+def pick_kernel(pair, *refs):
+    number = len(refs) // 2
+    rows = pair.shape[0] // 2
+    low, high = pair[0:rows].astype(F32), pair[rows:].astype(F32)
+    pick(refs[:number], refs[number:], low, high)
 
 
 def own_kernel(lam, rhs, vert, part):
@@ -94,71 +88,65 @@
     part[1] = rhs[rows:].astype(F32) - dot(lam[0:rows], vert[1, 0])
 
 
+def source_sums(number, meta, blocks, numbered):
+    tiles, bands = [], []
+    for i, ref in numbered:
+        tile = ref[...]
+        tiles.append(jnp.where(meta[number + i] > 0, tile, jnp.zeros_like(tile)))
+        bands.append(jnp.concatenate([blocks[0, meta[i]], blocks[1, meta[i]]], axis=1))
+    both = dot(jnp.concatenate(tiles, axis=1), jnp.concatenate(bands, axis=0))
+    width = blocks.shape[-1]
+    return both[:, :width], both[:, width:]
+
+
 def tile_of(ref, slot, rows):
     if ref.shape[0] == rows:
         return ref[...]
     return ref[pl.ds(pl.multiple_of(slot * rows, 16), rows), :]
 
 
-def less_sources(total, number, meta, blocks, numbered):
-    rows = total[0].shape[0]
-    for i, ref in numbered:
-        tile = tile_of(ref, meta[number + i], rows)
-        tile = jnp.where(meta[2 * number + i] > 0, tile, jnp.zeros_like(tile))
-        total = [total[d] - dot(tile, blocks[d, meta[i]]) for d in range(2)]
-    return total
-
-
-def less_beside(total, two, group, vert, beside):
+def beside_sums(two, group, vert, beside, rows):
     if two:
         mine = group[0]
-        term = dot(tile_of(beside[0], mine, total[0].shape[0]), vert[1 - mine, 1 - mine])
+        term = dot(tile_of(beside[0], mine, rows), vert[1 - mine, 1 - mine])
         none = jnp.zeros_like(term)
-        return [
-            total[0] - jnp.where(mine == 1, term, none),
-            total[1] - jnp.where(mine == 0, term, none),
-        ]
-    return [
-        total[d] - dot(tile_of(beside[d], 1 - d, total[d].shape[0]), vert[d, d]) for d in range(2)
-    ]
-
-
-def local_kernel(number, two, first_index, meta, group, part, blocks, vert, *refs):
-    sides = 1 if two else 2
-    arrived, beside, out = refs[: -sides - 1], refs[-sides - 1 : -1], refs[-1]
-    numbered = list(enumerate(arrived, first_index))
-    sums = less_sources([part[0], part[1]], number, meta, blocks, numbered)
-    out[0], out[1] = less_beside(sums, two, group, vert, beside)
+        return jnp.where(mine == 1, term, none), jnp.where(mine == 0, term, none)
+    return [dot(tile_of(beside[d], 1 - d, rows), vert[d, d]) for d in range(2)]
 
 
 def cross_kernel(number, meta, blocks, *refs):
     arrived, out = refs[:-1], refs[-1]
-    zero = jnp.zeros(out.shape[1:], F32)
-    out[0], out[1] = less_sources([zero, zero], number, meta, blocks, list(enumerate(arrived)))
-
-
-def far_kernel(number, meta, blocks, cross, passed, pair, out):
-    numbered = list(enumerate([passed, pair], number - 2))
-    out[0], out[1] = less_sources([cross[0], cross[1]], number, meta, blocks, numbered)
-
-
-def update_kernel(number, two, first, group, total, far, *refs):
-    low, high = total[0] + far[0], total[1] + far[1]
-    count = number - 1 if first else 1
-    told, refs = refs[:count], refs[count:]
-    lam, sends, refs = refs[0], refs[1 : 1 + number], refs[1 + number :]
-    outer, refs = refs[: 1 if two else 2], refs[1 if two else 2 :]
-    masks = told[0]
-    if first:
-        masks = refs[0]
-        for i in range(number - 2):
-            masks[i : i + 1, :] = asks_of(told[i])[i : i + 1, :]
-        masks[number - 2 : number, :] = told[-1][number - 2 : number, :]
+    out[0], out[1] = source_sums(number, meta, blocks, list(enumerate(arrived)))
+
+
+def far_kernel(number, meta, blocks, cross, *refs):
+    far, out = refs[:-1], refs[-1]
+    low, high = source_sums(number, meta, blocks, list(enumerate(far, number - len(far))))
+    out[0] = cross[0] + low
+    out[1] = cross[1] + high
+
+
+def updated(number, two, first_index, meta, group, part, far, blocks, vert, near, beside):
+    numbered = list(enumerate(near, first_index))
+    sums = source_sums(number, meta, blocks, numbered)
+    terms = beside_sums(two, group, vert, beside, part.shape[1])
+    return [part[d] - far[d] - sums[d] - terms[d] for d in range(2)]
+
+
+def update_kernel(number, two, first_index, meta, group, part, far, blocks, vert, *refs):
+    sides = 1 if two else 2
+    here = number - 2 - first_index
+    near, refs = refs[:here], refs[here:]
+    beside, refs = refs[:sides], refs[sides:]
+    told, refs = refs[:number], refs[number:]
+    low, high = updated(
+        number, two, first_index, meta, group, part, far, blocks, vert, near, beside
+    )
+    lam, sends, outer = refs[0], refs[1 : 1 + number], refs[1 + number :]
     rows = low.shape[0]
     lam[0:rows] = low.astype(BF16)
     lam[rows:] = high.astype(BF16)
-    for i, send in enumerate(sends):
-        send[...] = chosen(masks[i : i + 1, :], low, high)
+    pick(told, sends, low, high)
     if two:
         outer[0][...] = jnp.where(group[0] == 0, high, low).astype(BF16)
     else:
@@ -166,8 +154,12 @@
         outer[1][...] = low.astype(BF16)
 
 
-def last_kernel(columns, two, wells, gains, total, far, sens, basis, lam, pieces):
-    sums = [total[0] + far[0], total[1] + far[1]]
+def last_kernel(
+    number, two, first_index, columns, meta, group, wells, gains, part, far, blocks, vert, sens, basis, *refs
+):
+    here = number - 2 - first_index
+    near, beside, (lam, pieces) = refs[:here], refs[here:-2], refs[-2:]
+    sums = updated(number, two, first_index, meta, group, part, far, blocks, vert, near, beside)
     phases, _, cells = sens.shape
     spot = lax.broadcasted_iota(jnp.int32, (1, cells), 1)
     projected = None
@@ -272,15 +264,17 @@
     partial = functools.partial
 
     with jax.named_scope("plan"):
-        far_pair = moved_by(rhs, routes[-1])
-        meta, payload = call(
+        meta, asks = call(
             partial(plan_kernel, columns, swaps),
-            [jax.ShapeDtypeStruct((3 * number,), jnp.int32), pltpu.VMEM((2 * rows + 16, width), BF16)],
-            (outside(conn_src[0, 0]), conn_count[0], outside(tile_map), me, outside(rhs)),
-            [SMEM] * 4 + [VMEM],
+            [jax.ShapeDtypeStruct((2 * number,), jnp.int32), pltpu.VMEM((8, 128), F32)],
+            (outside(conn_src[0, 0]), conn_count[0], outside(tile_map), me),
+            [SMEM] * 4,
             out_specs=[SMEM, VMEM],
         )
-        payload = held(payload)
+        asks = held(asks)
+        told = [moved_by(asks, [(to, at) for at, to in pairs]) for pairs in routes]
+        rhs_held = held(rhs)
+        sends = call(pick_kernel, [tile] * number, (rhs_held, *told), [VMEM] * (1 + number))
 
     with jax.named_scope("load"):
         blocks, vert = call(
@@ -293,36 +287,14 @@
         )
         blocks, vert = held(blocks), held(vert)
 
-    rhs_held = held(rhs)
     lam = rhs_held
-    sends = [payload] * (number - 2)
-    outer = [payload]
-    masks_type = pltpu.VMEM((8, width), F32)
+    outer = [rhs]
+    half = len(swaps) // 2
     for step in range(ITERS):
-        first = step == 0
         with jax.named_scope("apply"):
             arrived = [moved_by(x, pairs) for x, pairs in zip(sends, routes)]
-            if first:
-                even, odd = (arrived[swaps.index((1, color))] for color in (1, 0))
-                picked, relayed = call(
-                    partial(far_pick_kernel, number),
-                    [tile, masks_type],
-                    (me, far_pair, payload, even, odd),
-                    [SMEM] + [VMEM] * 4,
-                )
-                arrived = [*arrived, moved_by(picked, shift_pairs(columns, 1)), far_pair]
-                told = moved_by(relayed, routes[-1])
             beside = beside_layers(outer)
             (part,) = call(own_kernel, [sums], (lam, rhs_held, vert), [VMEM] * 3, flops=one)
-            half = len(swaps) // 2
-            tiles = arrived[half:-2] + beside
-            (total,) = call(
-                partial(local_kernel, number, two, half),
-                [sums],
-                (meta, group, held(part), blocks, vert, *tiles),
-                [SMEM] * 2 + [VMEM] * (3 + len(tiles)),
-                flops=one,
-            )
             (cross,) = call(
                 partial(cross_kernel, number),
                 [sums],
@@ -337,31 +309,38 @@
                 [SMEM] + [VMEM] * 4,
                 flops=4 * one,
             )
-            total, far = held(total), held(far)
-            told = [*arrived[:-2], told] if first else [masks]
+            tiles = (held(part), held(far), blocks, vert)
+            near = (*arrived[half:-2], *beside)
             if step < ITERS - 1:
                 lam, *rest = call(
-                    partial(update_kernel, number, two, first),
-                    [pair] + [tile] * (number + len(beside)) + ([masks_type] if first else []),
-                    (group, total, far, *told),
-                    [SMEM] + [VMEM] * (2 + len(told)),
+                    partial(update_kernel, number, two, half),
+                    [pair] + [tile] * (number + len(beside)),
+                    (meta, group, *tiles, *near, *told),
+                    [SMEM] * 2 + [VMEM] * (4 + len(near) + number),
                     flops=one,
                 )
                 lam = held(lam)
-                if first:
-                    masks = held(rest.pop())
                 sends, outer = rest[:number], rest[number:]
             else:
                 adjoint, pieces = call(
-                    partial(last_kernel, columns, two),
+                    partial(last_kernel, number, two, half, columns),
                     [
                         jax.ShapeDtypeStruct((2, rows, width), BF16),
                         pltpu.VMEM(
                             (2 * columns, modes // columns // 2, rows) if two else (rows, modes), F32
                         ),
                     ],
-                    (well_cells[0], well_gain[0], total, far, held(sens[0].transpose(1, 0, 2)), held(basis[0])),
-                    [SMEM] * 2 + [VMEM] * 4,
+                    (
+                        meta,
+                        group,
+                        well_cells[0],
+                        well_gain[0],
+                        *tiles,
+                        held(sens[0].transpose(1, 0, 2)),
+                        held(basis[0]),
+                        *near,
+                    ),
+                    [SMEM] * 4 + [VMEM] * (6 + len(near)),
                     flops=one,
                 )
 

time: 77.7 us -> 84 us (1.081)
  Pallas kernels: 15.8 us -> 18.1 us
  waiting for transfers between devices: 8.2 us -> 10.5 us
  starting transfers between devices: 39.1 us -> 41.4 us
    ppermute x19 -> x24, waiting for transfers between devices: 8.19 us -> 10.5 us  [moved_by(): return held(lax.ppermute(x, 'areal', pairs))]
    ppermute x19 -> x24, starting transfers between devices: 39.1 us -> 41.4 us  [moved_by(): return held(lax.ppermute(x, 'areal', pairs))]
    pallas_call x19 -> x16, Pallas kernels: 15.8 us -> 18.1 us  [call(): pl.pallas_call(kernel, out_shape=outs, in_specs=specs, out_specs=out_spec...]
  transfers between devices with their start and end apart: 22 -> 27, of which waited for: 6 -> 10; matrix products, arithmetic and copies ran while one was open for 0% -> 0% of each run, Pallas kernels for 15% -> 13%
where the time goes in v2:
time: 84 us; the launch traced here: 83.8 us
  starting transfers between devices  41.4 us (49%)
  Pallas kernels  18.1 us (22%)
  blocking collectives  12.2 us (15%)
  waiting for transfers between devices  10.5 us (12%)
  between operations  1.55 us (2%)
    ppermute x24, starting transfers between devices, moved_by(): return held(lax.ppermute(x, 'areal', pairs))  41.4 us
    pallas_call x16, Pallas kernels, call(): pl.pallas_call(kernel, out_shape=outs, in_specs=specs, out_specs=out_spec...  18.1 us
    all_to_all x1, blocking collectives, on_device(): landed = lax.all_to_all(pieces, ('areal', 'layer'), 0, 0, tiled=True)  12.2 us
    ppermute x24, waiting for transfers between devices, moved_by(): return held(lax.ppermute(x, 'areal', pairs))  10.5 us
  transfers between devices with their start and end apart: 27, of which 10 were waited for; matrix products, arithmetic and copies ran while one was open for 0% of the time, Pallas kernels for 13%

profile of v2, /device:TPU:0, one launch (start us, length us, event | category | flops | bytes accessed | tf_op | source)
XLA Modules:
  0.0 83.8 jit_solution(8003679436078928675)
XLA Ops:
  1.3 1.3 %plan.2 = (s32[12]{0:T(128)S(1)}, f32[8,128]{1,0:T(8,128)S(1)}) custom-call(s32[6]{0:T(128)} %bitcast.23, s32[1]{0:T(128)} %bitcast.15.count, s32[32]{0:T(128)} %tile_map.1, s32[1]{0:T(128)} %bitcast.2.me), custom_call_target="tpu_custom_call" | custom-call | tf_op jit(solution)/shard_map/plan/pallas_call | solution.py:201
  2.6 4.1 %collective-permute-start.5 = (f32[8,128]{1,0:T(8,128)S(1)}, f32[8,128]{1,0:T(8,128)S(1)}, u32[]{:S(2)}, u32[]{:S(2)}) collective-permute-start(f32[8,128]{1,0:T(8,128)S(1)} %get-tuple-element.33), channel_id=1, source_target_pairs={{16,0},{18,2},{20,4},{22,6},{24,8},{26,10},{28,12},{30,14},{0,16},... | collective-permute-start | bytes 12296 | tf_op jit(solution)/shard_map/plan/ppermute | solution.py:215
  6.7 1.3 %collective-permute-start.4 = (f32[8,128]{1,0:T(8,128)S(1)}, f32[8,128]{1,0:T(8,128)S(1)}, u32[]{:S(2)}, u32[]{:S(2)}) collective-permute-start(f32[8,128]{1,0:T(8,128)S(1)} %get-tuple-element.33), channel_id=1, source_target_pairs={{14,0},{16,2},{18,4},{20,6},{22,8},{24,10},{26,12},{28,14},{30,16}... | collective-permute-start | bytes 12296 | tf_op jit(solution)/shard_map/plan/ppermute | solution.py:215
  8.0 1.5 %collective-permute-start.3 = (f32[8,128]{1,0:T(8,128)S(1)}, f32[8,128]{1,0:T(8,128)S(1)}, u32[]{:S(2)}, u32[]{:S(2)}) collective-permute-start(f32[8,128]{1,0:T(8,128)S(1)} %get-tuple-element.33), channel_id=1, source_target_pairs={{2,0},{0,2},{6,4},{4,6},{10,8},{8,10},{14,12},{12,14},{18,16},{16,... | collective-permute-start | bytes 12296 | tf_op jit(solution)/shard_map/plan/ppermute | solution.py:215
  9.5 1.5 %collective-permute-start.2 = (f32[8,128]{1,0:T(8,128)S(1)}, f32[8,128]{1,0:T(8,128)S(1)}, u32[]{:S(2)}, u32[]{:S(2)}) collective-permute-start(f32[8,128]{1,0:T(8,128)S(1)} %get-tuple-element.33), channel_id=1, source_target_pairs={{4,0},{6,2},{0,4},{2,6},{12,8},{14,10},{8,12},{10,14},{20,16},{22,... | collective-permute-start | bytes 12296 | tf_op jit(solution)/shard_map/plan/ppermute | solution.py:215
  11.0 3.5 %collective-permute-start.1 = (f32[8,128]{1,0:T(8,128)S(1)}, f32[8,128]{1,0:T(8,128)S(1)}, u32[]{:S(2)}, u32[]{:S(2)}) collective-permute-start(f32[8,128]{1,0:T(8,128)S(1)} %get-tuple-element.33), channel_id=1, source_target_pairs={{30,0},{4,2},{2,4},{8,6},{6,8},{12,10},{10,12},{16,14},{14,16},{20... | collective-permute-start | bytes 12296 | tf_op jit(solution)/shard_map/plan/ppermute | solution.py:215
  14.5 1.5 %collective-permute-start = (f32[8,128]{1,0:T(8,128)S(1)}, f32[8,128]{1,0:T(8,128)S(1)}, u32[]{:S(2)}, u32[]{:S(2)}) collective-permute-start(f32[8,128]{1,0:T(8,128)S(1)} %get-tuple-element.33), channel_id=1, source_target_pairs={{28,0},{30,2},{8,4},{10,6},{4,8},{6,10},{16,12},{18,14},{12,16},{1... | collective-permute-start | bytes 12296 | tf_op jit(solution)/shard_map/plan/ppermute | solution.py:215
  16.1 2.2 %collective-permute-done.1.refs_1_.refs_4_ = f32[8,128]{1,0:T(8,128)S(1)} collective-permute-done((f32[8,128]{1,0:T(8,128)S(1)}, f32[8,128]{1,0:T(8,128)S(1)}, u32[]{:S(2)}, u32[]{:S(2)}) %collective-permute-start.1) | collective-permute-done | bytes 4128 | tf_op jit(solution)/shard_map/plan/ppermute | solution.py:215
  18.2 2.6 %collective-permute-done.refs_0_.refs_3_ = f32[8,128]{1,0:T(8,128)S(1)} collective-permute-done((f32[8,128]{1,0:T(8,128)S(1)}, f32[8,128]{1,0:T(8,128)S(1)}, u32[]{:S(2)}, u32[]{:S(2)}) %collective-permute-start) | collective-permute-done | bytes 4128 | tf_op jit(solution)/shard_map/plan/ppermute | solution.py:215
  21.8 1.6 %collective-permute-start.6 = (bf16[112,384]{1,0:T(8,128)(2,1)S(1)}, bf16[112,384]{1,0:T(8,128)(2,1)S(1)}, u32[]{:S(2)}, u32[]{:S(2)}) collective-permute-start(bf16[112,384]{1,0:T(8,128)(2,1)S(1)} %get-tuple-element.34), channel_id=1, source_target_pairs={{0,28},{2,30},{4,8},{6,10},{8,4},{10,6},{12,16},{14,18},{16,12},{1... | collective-permute-start | bytes 258056 | tf_op jit(solution)/shard_map/apply/ppermute | solution.py:215
  24.5 5.1 %collective-permute-start.9 = (bf16[112,384]{1,0:T(8,128)(2,1)S(1)}, bf16[112,384]{1,0:T(8,128)(2,1)S(1)}, u32[]{:S(2)}, u32[]{:S(2)}) collective-permute-start(bf16[112,384]{1,0:T(8,128)(2,1)S(1)} %get-tuple-element.37), channel_id=1, source_target_pairs={{0,16},{2,18},{4,20},{6,22},{8,24},{10,26},{12,28},{14,30},{16,0},... | collective-permute-start | bytes 258056 | tf_op jit(solution)/shard_map/apply/ppermute | solution.py:215
  29.9 2.6 %collective-permute-done.7.refs_1_ = bf16[112,384]{1,0:T(8,128)(2,1)S(1)} collective-permute-done((bf16[112,384]{1,0:T(8,128)(2,1)S(1)}, bf16[112,384]{1,0:T(8,128)(2,1)S(1)}, u32[]{:S(2)}, u32[]{:S(2)}) %collective-permute-start.7) | collective-permute-done | bytes 86048 | tf_op jit(solution)/shard_map/apply/ppermute | solution.py:215
  32.5 2.4 %load.1 = (bf16[2,6,384,384]{3,2,1,0:T(8,128)(2,1)S(1)}, bf16[2,2,384,384]{3,2,1,0:T(8,128)(2,1)S(1)}) custom-call(bf16[2,6,384,384]{3,2,1,0:T(8,128)(2,1)} %bitcast.20, bf16[2,2,384,384]{3,2,1,0:T(8,128)(2,1)} %bitcast.21), custom_call_target="tpu_custom_call" | custom-call | bytes 4718592 | tf_op jit(solution)/shard_map/load/pallas_call | solution.py:201
  34.9 1.3 %apply.12.part = f32[2,112,384]{2,1,0:T(8,128)S(1)} custom-call(bf16[224,384]{1,0:T(8,128)(2,1)} %bitcast.6.lam.rhs.pair, bf16[224,384]{1,0:T(8,128)(2,1)} %bitcast.6.lam.rhs.pair, bf16[2,2,384,384]{3,2,1,0:T(8,128)(2,1)S(1)} %get-tuple-element.31.vert), custom_call_target="tpu_custom_call" | custom-call | flops 33030144 | bytes 165150 | tf_op jit(solution)/shard_map/apply/pallas_call | solution.py:201
  39.1 1.6 %collective-permute-start.13 = (bf16[112,384]{1,0:T(8,128)(2,1)S(1)}, bf16[112,384]{1,0:T(8,128)(2,1)S(1)}, u32[]{:S(2)}, u32[]{:S(2)}) collective-permute-start(bf16[112,384]{1,0:T(8,128)(2,1)S(1)} %get-tuple-element.41), channel_id=1, source_target_pairs={{0,28},{2,30},{4,8},{6,10},{8,4},{10,6},{12,16},{14,18},{16,12},{1... | collective-permute-start | bytes 258056 | tf_op jit(solution)/shard_map/apply/ppermute | solution.py:215
  40.6 4.7 %collective-permute-start.14 = (bf16[112,384]{1,0:T(8,128)(2,1)S(1)}, bf16[112,384]{1,0:T(8,128)(2,1)S(1)}, u32[]{:S(2)}, u32[]{:S(2)}) collective-permute-start(bf16[112,384]{1,0:T(8,128)(2,1)S(1)} %get-tuple-element.42), channel_id=1, source_target_pairs={{0,30},{2,4},{4,2},{6,8},{8,6},{10,12},{12,10},{14,16},{16,14},{18... | collective-permute-start | bytes 258056 | tf_op jit(solution)/shard_map/apply/ppermute | solution.py:215
  45.3 1.5 %collective-permute-start.16 = (bf16[112,384]{1,0:T(8,128)(2,1)S(1)}, bf16[112,384]{1,0:T(8,128)(2,1)S(1)}, u32[]{:S(2)}, u32[]{:S(2)}) collective-permute-start(bf16[112,384]{1,0:T(8,128)(2,1)S(1)} %get-tuple-element.44), channel_id=1, source_target_pairs={{0,16},{2,18},{4,20},{6,22},{8,24},{10,26},{12,28},{14,30},{16,0},... | collective-permute-start | bytes 258056 | tf_op jit(solution)/shard_map/apply/ppermute | solution.py:215
  46.8 2.9 %collective-permute-start.18 = (bf16[112,384]{1,0:T(8,128)(2,1)S(1)}, bf16[112,384]{1,0:T(8,128)(2,1)S(1)}, u32[]{:S(2)}, u32[]{:S(2)}) collective-permute-start(bf16[112,384]{1,0:T(8,128)(2,1)S(1)} %get-tuple-element.46), channel_id=1, source_target_pairs={{0,2},{2,0},{4,6},{6,4},{8,10},{10,8},{12,14},{14,12},{16,18},{18,... | collective-permute-start | bytes 258056 | tf_op jit(solution)/shard_map/apply/ppermute | solution.py:215
  54.5 1.3 %collective-permute-start.20 = (bf16[112,384]{1,0:T(8,128)(2,1)S(1)}, bf16[112,384]{1,0:T(8,128)(2,1)S(1)}, u32[]{:S(2)}, u32[]{:S(2)}) collective-permute-start(bf16[112,384]{1,0:T(8,128)(2,1)S(1)} %get-tuple-element.49), channel_id=1, source_target_pairs={{0,28},{2,30},{4,8},{6,10},{8,4},{10,6},{12,16},{14,18},{16,12},{1... | collective-permute-start | bytes 258056 | tf_op jit(solution)/shard_map/apply/ppermute | solution.py:215
  55.8 4.6 %collective-permute-start.21 = (bf16[112,384]{1,0:T(8,128)(2,1)S(1)}, bf16[112,384]{1,0:T(8,128)(2,1)S(1)}, u32[]{:S(2)}, u32[]{:S(2)}) collective-permute-start(bf16[112,384]{1,0:T(8,128)(2,1)S(1)} %get-tuple-element.50), channel_id=1, source_target_pairs={{0,30},{2,4},{4,2},{6,8},{8,6},{10,12},{12,10},{14,16},{16,14},{18... | collective-permute-start | bytes 258056 | tf_op jit(solution)/shard_map/apply/ppermute | solution.py:215
  60.4 1.6 %collective-permute-start.23 = (bf16[112,384]{1,0:T(8,128)(2,1)S(1)}, bf16[112,384]{1,0:T(8,128)(2,1)S(1)}, u32[]{:S(2)}, u32[]{:S(2)}) collective-permute-start(bf16[112,384]{1,0:T(8,128)(2,1)S(1)} %get-tuple-element.52), channel_id=1, source_target_pairs={{0,16},{2,18},{4,20},{6,22},{8,24},{10,26},{12,28},{14,30},{16,0},... | collective-permute-start | bytes 258056 | tf_op jit(solution)/shard_map/apply/ppermute | solution.py:215
  63.1 1.8 %collective-permute-start.25 = (bf16[112,384]{1,0:T(8,128)(2,1)S(1)}, bf16[112,384]{1,0:T(8,128)(2,1)S(1)}, u32[]{:S(2)}, u32[]{:S(2)}) collective-permute-start(bf16[112,384]{1,0:T(8,128)(2,1)S(1)} %get-tuple-element.54), channel_id=1, source_target_pairs={{0,2},{2,0},{4,6},{6,4},{8,10},{10,8},{12,14},{14,12},{16,18},{18,... | collective-permute-start | bytes 258056 | tf_op jit(solution)/shard_map/apply/ppermute | solution.py:215
  69.2 1.7 %apply.23 = (bf16[2,112,384]{2,1,0:T(8,128)(2,1)}, f32[32,8,112]{2,1,0:T(8,128)S(1)}) custom-call(s32[12]{0:T(128)S(1)} %get-tuple-element.30.meta, s32[1]{0:T(128)} %bitcast.3.group, s32[2,4]{1,0:T(2,128)S(1)} %bitcast.18, f32[2,4]{1,0:T(2,128)S(1)} %bitcast.19, f32[2,112,384]{2,1,0:T(8,128)S(1)} %apply.20.part, f32[2,112,384]{2,1,0:T(8,128)S(1)} %apply.22.far, ...), custom_call_target="tpu_custom_call" | custom-call | flops 33030144 | bytes 165150 | tf_op jit(solution)/shard_map/apply/pallas_call | solution.py:201
  70.9 12.2 %all_to_all.5.pieces = f32[32,8,112]{2,1,0:T(8,128)S(1)} all-to-all(f32[32,8,112]{2,1,0:T(8,128)S(1)} %get-tuple-element.57), channel_id=1, replica_groups=mesh['areal'=16,'layer'=2] {'areal','layer'}, dimensions={0} | all-to-all | bytes 229376 | tf_op jit(solution)/shard_map/project/all_to_all | solution.py:349
  (55 shorter events, 16.0 us)
Async XLA Ops:
  2.6 11.9 %collective-permute-start.5 = (f32[8,128]{1,0:T(8,128)S(1)}, f32[8,128]{1,0:T(8,128)S(1)}, u32[]{:S(2)}, u32[]{:S(2)}) collective-permute-start(f32[8,128]{1,0:T(8,128)S(1)} %get-tuple-element.33), channel_id=1, source_target_pairs={{16,0},{18,2},{20,4},{22,6},{24,8},{26,10},{28,12},{30,14},{0,16},... | collective-permute-start | bytes 12296 | tf_op jit(solution)/shard_map/plan/ppermute | solution.py:215
  6.7 9.3 %collective-permute-start.4 = (f32[8,128]{1,0:T(8,128)S(1)}, f32[8,128]{1,0:T(8,128)S(1)}, u32[]{:S(2)}, u32[]{:S(2)}) collective-permute-start(f32[8,128]{1,0:T(8,128)S(1)} %get-tuple-element.33), channel_id=1, source_target_pairs={{14,0},{16,2},{18,4},{20,6},{22,8},{24,10},{26,12},{28,14},{30,16}... | collective-permute-start | bytes 12296 | tf_op jit(solution)/shard_map/plan/ppermute | solution.py:215
  8.0 8.1 %collective-permute-start.3 = (f32[8,128]{1,0:T(8,128)S(1)}, f32[8,128]{1,0:T(8,128)S(1)}, u32[]{:S(2)}, u32[]{:S(2)}) collective-permute-start(f32[8,128]{1,0:T(8,128)S(1)} %get-tuple-element.33), channel_id=1, source_target_pairs={{2,0},{0,2},{6,4},{4,6},{10,8},{8,10},{14,12},{12,14},{18,16},{16,... | collective-permute-start | bytes 12296 | tf_op jit(solution)/shard_map/plan/ppermute | solution.py:215
  9.5 6.6 %collective-permute-start.2 = (f32[8,128]{1,0:T(8,128)S(1)}, f32[8,128]{1,0:T(8,128)S(1)}, u32[]{:S(2)}, u32[]{:S(2)}) collective-permute-start(f32[8,128]{1,0:T(8,128)S(1)} %get-tuple-element.33), channel_id=1, source_target_pairs={{4,0},{6,2},{0,4},{2,6},{12,8},{14,10},{8,12},{10,14},{20,16},{22,... | collective-permute-start | bytes 12296 | tf_op jit(solution)/shard_map/plan/ppermute | solution.py:215
  11.0 7.2 %collective-permute-start.1 = (f32[8,128]{1,0:T(8,128)S(1)}, f32[8,128]{1,0:T(8,128)S(1)}, u32[]{:S(2)}, u32[]{:S(2)}) collective-permute-start(f32[8,128]{1,0:T(8,128)S(1)} %get-tuple-element.33), channel_id=1, source_target_pairs={{30,0},{4,2},{2,4},{8,6},{6,8},{12,10},{10,12},{16,14},{14,16},{20... | collective-permute-start | bytes 12296 | tf_op jit(solution)/shard_map/plan/ppermute | solution.py:215
  14.5 6.3 %collective-permute-start = (f32[8,128]{1,0:T(8,128)S(1)}, f32[8,128]{1,0:T(8,128)S(1)}, u32[]{:S(2)}, u32[]{:S(2)}) collective-permute-start(f32[8,128]{1,0:T(8,128)S(1)} %get-tuple-element.33), channel_id=1, source_target_pairs={{28,0},{30,2},{8,4},{10,6},{4,8},{6,10},{16,12},{18,14},{12,16},{1... | collective-permute-start | bytes 12296 | tf_op jit(solution)/shard_map/plan/ppermute | solution.py:215
  21.8 8.1 %collective-permute-start.6 = (bf16[112,384]{1,0:T(8,128)(2,1)S(1)}, bf16[112,384]{1,0:T(8,128)(2,1)S(1)}, u32[]{:S(2)}, u32[]{:S(2)}) collective-permute-start(bf16[112,384]{1,0:T(8,128)(2,1)S(1)} %get-tuple-element.34), channel_id=1, source_target_pairs={{0,28},{2,30},{4,8},{6,10},{8,4},{10,6},{12,16},{14,18},{16,12},{1... | collective-permute-start | bytes 258056 | tf_op jit(solution)/shard_map/apply/ppermute | solution.py:215
  23.4 9.1 %collective-permute-start.7 = (bf16[112,384]{1,0:T(8,128)(2,1)S(1)}, bf16[112,384]{1,0:T(8,128)(2,1)S(1)}, u32[]{:S(2)}, u32[]{:S(2)}) collective-permute-start(bf16[112,384]{1,0:T(8,128)(2,1)S(1)} %get-tuple-element.35), channel_id=1, source_target_pairs={{0,30},{2,4},{4,2},{6,8},{8,6},{10,12},{12,10},{14,16},{16,14},{18... | collective-permute-start | bytes 258056 | tf_op jit(solution)/shard_map/apply/ppermute | solution.py:215
  24.5 13.5 %collective-permute-start.12 = (bf16[224,384]{1,0:T(8,128)(2,1)}, bf16[224,384]{1,0:T(8,128)(2,1)S(1)}, u32[]{:S(2)}, u32[]{:S(2)}) collective-permute-start(bf16[224,384]{1,0:T(8,128)(2,1)} %bitcast.6.lam.rhs.pair), channel_id=1, source_target_pairs={{0,1},{1,0},{2,3},{3,2},{4,5},{5,4},{6,7},{7,6},{8,9},{9,8},{10,11... | collective-permute-start | bytes 516104 | tf_op jit(solution)/shard_map/apply/ppermute | solution.py:225
  24.5 12.6 %collective-permute-start.8 = (bf16[112,384]{1,0:T(8,128)(2,1)S(1)}, bf16[112,384]{1,0:T(8,128)(2,1)S(1)}, u32[]{:S(2)}, u32[]{:S(2)}) collective-permute-start(bf16[112,384]{1,0:T(8,128)(2,1)S(1)} %get-tuple-element.36), channel_id=1, source_target_pairs={{0,14},{2,16},{4,18},{6,20},{8,22},{10,24},{12,26},{14,28},{16,30}... | collective-permute-start | bytes 258056 | tf_op jit(solution)/shard_map/apply/ppermute | solution.py:215
  24.5 12.6 %collective-permute-start.9 = (bf16[112,384]{1,0:T(8,128)(2,1)S(1)}, bf16[112,384]{1,0:T(8,128)(2,1)S(1)}, u32[]{:S(2)}, u32[]{:S(2)}) collective-permute-start(bf16[112,384]{1,0:T(8,128)(2,1)S(1)} %get-tuple-element.37), channel_id=1, source_target_pairs={{0,16},{2,18},{4,20},{6,22},{8,24},{10,26},{12,28},{14,30},{16,0},... | collective-permute-start | bytes 258056 | tf_op jit(solution)/shard_map/apply/ppermute | solution.py:215
  29.9 8.1 %collective-permute-start.10 = (bf16[112,384]{1,0:T(8,128)(2,1)S(1)}, bf16[112,384]{1,0:T(8,128)(2,1)S(1)}, u32[]{:S(2)}, u32[]{:S(2)}) collective-permute-start(bf16[112,384]{1,0:T(8,128)(2,1)S(1)} %get-tuple-element.38), channel_id=1, source_target_pairs={{0,4},{2,6},{4,0},{6,2},{8,12},{10,14},{12,8},{14,10},{16,20},{18,... | collective-permute-start | bytes 258056 | tf_op jit(solution)/shard_map/apply/ppermute | solution.py:215
  39.1 7.8 %collective-permute-start.13 = (bf16[112,384]{1,0:T(8,128)(2,1)S(1)}, bf16[112,384]{1,0:T(8,128)(2,1)S(1)}, u32[]{:S(2)}, u32[]{:S(2)}) collective-permute-start(bf16[112,384]{1,0:T(8,128)(2,1)S(1)} %get-tuple-element.41), channel_id=1, source_target_pairs={{0,28},{2,30},{4,8},{6,10},{8,4},{10,6},{12,16},{14,18},{16,12},{1... | collective-permute-start | bytes 258056 | tf_op jit(solution)/shard_map/apply/ppermute | solution.py:215
  40.6 9.8 %collective-permute-start.14 = (bf16[112,384]{1,0:T(8,128)(2,1)S(1)}, bf16[112,384]{1,0:T(8,128)(2,1)S(1)}, u32[]{:S(2)}, u32[]{:S(2)}) collective-permute-start(bf16[112,384]{1,0:T(8,128)(2,1)S(1)} %get-tuple-element.42), channel_id=1, source_target_pairs={{0,30},{2,4},{4,2},{6,8},{8,6},{10,12},{12,10},{14,16},{16,14},{18... | collective-permute-start | bytes 258056 | tf_op jit(solution)/shard_map/apply/ppermute | solution.py:215
  45.3 7.3 %collective-permute-start.15 = (bf16[112,384]{1,0:T(8,128)(2,1)S(1)}, bf16[112,384]{1,0:T(8,128)(2,1)S(1)}, u32[]{:S(2)}, u32[]{:S(2)}) collective-permute-start(bf16[112,384]{1,0:T(8,128)(2,1)S(1)} %get-tuple-element.43), channel_id=1, source_target_pairs={{0,14},{2,16},{4,18},{6,20},{8,22},{10,24},{12,26},{14,28},{16,30}... | collective-permute-start | bytes 258056 | tf_op jit(solution)/shard_map/apply/ppermute | solution.py:215
  45.3 7.3 %collective-permute-start.16 = (bf16[112,384]{1,0:T(8,128)(2,1)S(1)}, bf16[112,384]{1,0:T(8,128)(2,1)S(1)}, u32[]{:S(2)}, u32[]{:S(2)}) collective-permute-start(bf16[112,384]{1,0:T(8,128)(2,1)S(1)} %get-tuple-element.44), channel_id=1, source_target_pairs={{0,16},{2,18},{4,20},{6,22},{8,24},{10,26},{12,28},{14,30},{16,0},... | collective-permute-start | bytes 258056 | tf_op jit(solution)/shard_map/apply/ppermute | solution.py:215
  46.8 6.7 %collective-permute-start.17 = (bf16[112,384]{1,0:T(8,128)(2,1)S(1)}, bf16[112,384]{1,0:T(8,128)(2,1)S(1)}, u32[]{:S(2)}, u32[]{:S(2)}) collective-permute-start(bf16[112,384]{1,0:T(8,128)(2,1)S(1)} %get-tuple-element.45), channel_id=1, source_target_pairs={{0,4},{2,6},{4,0},{6,2},{8,12},{10,14},{12,8},{14,10},{16,20},{18,... | collective-permute-start | bytes 258056 | tf_op jit(solution)/shard_map/apply/ppermute | solution.py:215
  46.8 6.7 %collective-permute-start.18 = (bf16[112,384]{1,0:T(8,128)(2,1)S(1)}, bf16[112,384]{1,0:T(8,128)(2,1)S(1)}, u32[]{:S(2)}, u32[]{:S(2)}) collective-permute-start(bf16[112,384]{1,0:T(8,128)(2,1)S(1)} %get-tuple-element.46), channel_id=1, source_target_pairs={{0,2},{2,0},{4,6},{6,4},{8,10},{10,8},{12,14},{14,12},{16,18},{18,... | collective-permute-start | bytes 258056 | tf_op jit(solution)/shard_map/apply/ppermute | solution.py:215
  54.5 8.5 %collective-permute-start.20 = (bf16[112,384]{1,0:T(8,128)(2,1)S(1)}, bf16[112,384]{1,0:T(8,128)(2,1)S(1)}, u32[]{:S(2)}, u32[]{:S(2)}) collective-permute-start(bf16[112,384]{1,0:T(8,128)(2,1)S(1)} %get-tuple-element.49), channel_id=1, source_target_pairs={{0,28},{2,30},{4,8},{6,10},{8,4},{10,6},{12,16},{14,18},{16,12},{1... | collective-permute-start | bytes 258056 | tf_op jit(solution)/shard_map/apply/ppermute | solution.py:215
  55.8 9.9 %collective-permute-start.21 = (bf16[112,384]{1,0:T(8,128)(2,1)S(1)}, bf16[112,384]{1,0:T(8,128)(2,1)S(1)}, u32[]{:S(2)}, u32[]{:S(2)}) collective-permute-start(bf16[112,384]{1,0:T(8,128)(2,1)S(1)} %get-tuple-element.50), channel_id=1, source_target_pairs={{0,30},{2,4},{4,2},{6,8},{8,6},{10,12},{12,10},{14,16},{16,14},{18... | collective-permute-start | bytes 258056 | tf_op jit(solution)/shard_map/apply/ppermute | solution.py:215
  60.4 7.5 %collective-permute-start.22 = (bf16[112,384]{1,0:T(8,128)(2,1)S(1)}, bf16[112,384]{1,0:T(8,128)(2,1)S(1)}, u32[]{:S(2)}, u32[]{:S(2)}) collective-permute-start(bf16[112,384]{1,0:T(8,128)(2,1)S(1)} %get-tuple-element.51), channel_id=1, source_target_pairs={{0,14},{2,16},{4,18},{6,20},{8,22},{10,24},{12,26},{14,28},{16,30}... | collective-permute-start | bytes 258056 | tf_op jit(solution)/shard_map/apply/ppermute | solution.py:215
  60.4 7.9 %collective-permute-start.23 = (bf16[112,384]{1,0:T(8,128)(2,1)S(1)}, bf16[112,384]{1,0:T(8,128)(2,1)S(1)}, u32[]{:S(2)}, u32[]{:S(2)}) collective-permute-start(bf16[112,384]{1,0:T(8,128)(2,1)S(1)} %get-tuple-element.52), channel_id=1, source_target_pairs={{0,16},{2,18},{4,20},{6,22},{8,24},{10,26},{12,28},{14,30},{16,0},... | collective-permute-start | bytes 258056 | tf_op jit(solution)/shard_map/apply/ppermute | solution.py:215
  62.0 7.2 %collective-permute-start.24 = (bf16[112,384]{1,0:T(8,128)(2,1)S(1)}, bf16[112,384]{1,0:T(8,128)(2,1)S(1)}, u32[]{:S(2)}, u32[]{:S(2)}) collective-permute-start(bf16[112,384]{1,0:T(8,128)(2,1)S(1)} %get-tuple-element.53), channel_id=1, source_target_pairs={{0,4},{2,6},{4,0},{6,2},{8,12},{10,14},{12,8},{14,10},{16,20},{18,... | collective-permute-start | bytes 258056 | tf_op jit(solution)/shard_map/apply/ppermute | solution.py:215
  63.1 6.1 %collective-permute-start.25 = (bf16[112,384]{1,0:T(8,128)(2,1)S(1)}, bf16[112,384]{1,0:T(8,128)(2,1)S(1)}, u32[]{:S(2)}, u32[]{:S(2)}) collective-permute-start(bf16[112,384]{1,0:T(8,128)(2,1)S(1)} %get-tuple-element.54), channel_id=1, source_target_pairs={{0,2},{2,0},{4,6},{6,4},{8,10},{10,8},{12,14},{14,12},{16,18},{18,... | collective-permute-start | bytes 258056 | tf_op jit(solution)/shard_map/apply/ppermute | solution.py:215
  (7 other events, 21.3 us)

commit v3 on v2

--- a/solution.py
+++ b/solution.py
@@ -33,7 +33,7 @@
     return jnp.dot(a, b, preferred_element_type=F32)
 
 
-def plan_kernel(columns, swaps, src, count, tile_map, me, meta, asks):
+def plan_kernel(columns, swaps, src, count, tile_map, me, rhs, table, asks, payload):
     steps = [
         jnp.where(lax.rem(lax.div(me[0], k), 2) == color, k, columns - k) for k, color in swaps
     ] + [columns // 2 + 1, columns // 2]
@@ -50,36 +50,78 @@
             hit = away == k
             conn[i] = jnp.where(hit, s, conn[i])
             slots[i] = jnp.where(hit, slot, slots[i])
-    line = lax.broadcasted_iota(jnp.int32, asks.shape, 0)
-    asked = jnp.zeros(asks.shape, F32)
+    rows, width = rhs.shape
+    line = lax.broadcasted_iota(jnp.int32, (16, width), 0)
+    asked = jnp.zeros(line.shape, F32)
     for i in range(number):
-        meta[i] = conn[i]
-        meta[number + i] = jnp.where(conn[i] < count[0], 1, 0)
+        table[i] = conn[i]
+        table[number + i] = jnp.where(conn[i] < count[0], 1, 0)
         asked = jnp.where(line == i, slots[i].astype(F32), asked)
-    asks[...] = asked
-
-
-def load_kernel(blocks, vert, blocks_held, vert_held, sems):
-    first = pltpu.make_async_copy(vert, vert_held, sems.at[0])
-    second = pltpu.make_async_copy(blocks, blocks_held, sems.at[1])
-    first.start()
-    second.start()
-    first.wait()
-    second.wait()
-
-
-def pick(told, sends, low, high):
-    for i, (ask, send) in enumerate(zip(told, sends)):
-        mask = ask[i : i + 1, :]
-        mask = jnp.concatenate([mask] * (send.shape[1] // mask.shape[1]), axis=1)
-        send[...] = jnp.where(mask > 0.5, high, low).astype(BF16)
-
-
-def pick_kernel(pair, *refs):
-    number = len(refs) // 2
-    rows = pair.shape[0] // 2
-    low, high = pair[0:rows].astype(F32), pair[rows:].astype(F32)
-    pick(refs[:number], refs[number:], low, high)
+    asks[...] = asked[0:8, 0:128]
+    payload[0:rows] = rhs[...]
+    payload[rows:] = asked.astype(BF16)
+
+
+def load_kernel(number, table, blocks, vert, bands, vert_held, sems):
+    width = vert.shape[-1]
+    side = pltpu.make_async_copy(vert, vert_held, sems.at[2 * number])
+    side.start()
+
+    def copies(i):
+        return [
+            pltpu.make_async_copy(
+                blocks.at[d, table[i]],
+                bands.at[i, :, pl.ds(d * width, width)],
+                sems.at[2 * i + d],
+            )
+            for d in range(2)
+        ]
+
+    for i in range(number):
+
+        @pl.when(table[number + i] > 0)
+        def _():
+            for copy in copies(i):
+                copy.start()
+
+        @pl.when(table[number + i] == 0)
+        def _():
+            bands[i] = jnp.zeros(bands.shape[1:], bands.dtype)
+
+    for i in range(number):
+
+        @pl.when(table[number + i] > 0)
+        def _():
+            for copy in copies(i):
+                copy.wait()
+
+    side.wait()
+
+
+def wide(mask, width):
+    return jnp.concatenate([mask] * (width // mask.shape[1]), axis=1)
+
+
+def chosen(mask, low, high):
+    return jnp.where(wide(mask, low.shape[1]) > 0.5, high, low).astype(BF16)
+
+
+def asks_of(payload):
+    return payload[payload.shape[0] - 16 :, 0:128].astype(F32)
+
+
+def tile_of(ref, mask, rows):
+    if ref.shape[0] == rows:
+        return ref[...]
+    return chosen(mask, ref[0:rows].astype(F32), ref[rows : 2 * rows].astype(F32))
+
+
+def far_pick_kernel(number, me, pair, even, odd, told9, told8, tile, told):
+    rows = tile.shape[0]
+    theirs = jnp.where(lax.rem(me[0], 2) == 0, asks_of(even), asks_of(odd))
+    tile[...] = tile_of(pair, theirs[number - 2 : number - 1, :], rows)
+    line = lax.broadcasted_iota(jnp.int32, told.shape, 0)
+    told[...] = jnp.where(line == number - 2, told9[...], told8[...])
 
 
 def own_kernel(lam, rhs, vert, part):
@@ -88,65 +130,68 @@
     part[1] = rhs[rows:].astype(F32) - dot(lam[0:rows], vert[1, 0])
 
 
-def source_sums(number, meta, blocks, numbered):
-    tiles, bands = [], []
-    for i, ref in numbered:
-        tile = ref[...]
-        tiles.append(jnp.where(meta[number + i] > 0, tile, jnp.zeros_like(tile)))
-        bands.append(jnp.concatenate([blocks[0, meta[i]], blocks[1, meta[i]]], axis=1))
-    both = dot(jnp.concatenate(tiles, axis=1), jnp.concatenate(bands, axis=0))
-    width = blocks.shape[-1]
-    return both[:, :width], both[:, width:]
-
-
-def tile_of(ref, slot, rows):
-    if ref.shape[0] == rows:
-        return ref[...]
-    return ref[pl.ds(pl.multiple_of(slot * rows, 16), rows), :]
+def source_sums(asks, bands, begin, refs, rows):
+    tiles = [tile_of(ref, asks[i : i + 1, :], rows) for i, ref in enumerate(refs, begin)]
+    count, width, both = len(refs), bands.shape[1], bands.shape[2]
+    band = bands[begin : begin + count].reshape(count * width, both)
+    sums = dot(jnp.concatenate(tiles, axis=1), band)
+    return sums[:, :width], sums[:, width:]
 
 
 def beside_sums(two, group, vert, beside, rows):
+    def tile(ref, slot):
+        if ref.shape[0] == rows:
+            return ref[...]
+        return ref[pl.ds(pl.multiple_of(slot * rows, 16), rows), :]
+
     if two:
         mine = group[0]
-        term = dot(tile_of(beside[0], mine, rows), vert[1 - mine, 1 - mine])
+        term = dot(tile(beside[0], mine), vert[1 - mine, 1 - mine])
         none = jnp.zeros_like(term)
         return jnp.where(mine == 1, term, none), jnp.where(mine == 0, term, none)
-    return [dot(tile_of(beside[d], 1 - d, rows), vert[d, d]) for d in range(2)]
-
-
-def cross_kernel(number, meta, blocks, *refs):
+    return [dot(tile(beside[d], 1 - d), vert[d, d]) for d in range(2)]
+
+
+def cross_kernel(asks, bands, *refs):
     arrived, out = refs[:-1], refs[-1]
-    out[0], out[1] = source_sums(number, meta, blocks, list(enumerate(arrived)))
-
-
-def far_kernel(number, meta, blocks, cross, *refs):
+    out[0], out[1] = source_sums(asks, bands, 0, arrived, out.shape[1])
+
+
+def far_kernel(asks, bands, cross, *refs):
     far, out = refs[:-1], refs[-1]
-    low, high = source_sums(number, meta, blocks, list(enumerate(far, number - len(far))))
+    low, high = source_sums(asks, bands, bands.shape[0] - len(far), far, out.shape[1])
     out[0] = cross[0] + low
     out[1] = cross[1] + high
 
 
-def updated(number, two, first_index, meta, group, part, far, blocks, vert, near, beside):
-    numbered = list(enumerate(near, first_index))
-    sums = source_sums(number, meta, blocks, numbered)
-    terms = beside_sums(two, group, vert, beside, part.shape[1])
+def updated(two, begin, group, part, far, asks, bands, vert, near, beside):
+    rows = part.shape[1]
+    sums = source_sums(asks, bands, begin, near, rows)
+    terms = beside_sums(two, group, vert, beside, rows)
     return [part[d] - far[d] - sums[d] - terms[d] for d in range(2)]
 
 
-def update_kernel(number, two, first_index, meta, group, part, far, blocks, vert, *refs):
+def update_kernel(number, two, begin, first, group, part, far, asks, bands, vert, *refs):
     sides = 1 if two else 2
-    here = number - 2 - first_index
+    here = number - 2 - begin
     near, refs = refs[:here], refs[here:]
     beside, refs = refs[:sides], refs[sides:]
-    told, refs = refs[:number], refs[number:]
-    low, high = updated(
-        number, two, first_index, meta, group, part, far, blocks, vert, near, beside
-    )
-    lam, sends, outer = refs[0], refs[1 : 1 + number], refs[1 + number :]
+    count = number - 1 if first else 1
+    told, refs = refs[:count], refs[count:]
+    low, high = updated(two, begin, group, part, far, asks, bands, vert, near, beside)
+    lam, sends, refs = refs[0], refs[1 : 1 + number], refs[1 + number :]
+    outer, refs = refs[:sides], refs[sides:]
+    masks = told[0]
+    if first:
+        masks = refs[0]
+        masks[...] = told[-1][...]
+        for i in range(number - 2):
+            masks[i : i + 1, :] = asks_of(told[i])[i : i + 1, :]
     rows = low.shape[0]
     lam[0:rows] = low.astype(BF16)
     lam[rows:] = high.astype(BF16)
-    pick(told, sends, low, high)
+    for i, send in enumerate(sends):
+        send[...] = chosen(masks[i : i + 1, :], low, high)
     if two:
         outer[0][...] = jnp.where(group[0] == 0, high, low).astype(BF16)
     else:
@@ -154,12 +199,10 @@
         outer[1][...] = low.astype(BF16)
 
 
-def last_kernel(
-    number, two, first_index, columns, meta, group, wells, gains, part, far, blocks, vert, sens, basis, *refs
-):
-    here = number - 2 - first_index
+def last_kernel(number, two, begin, columns, group, wells, gains, part, far, asks, bands, vert, sens, basis, *refs):
+    here = number - 2 - begin
     near, beside, (lam, pieces) = refs[:here], refs[here:-2], refs[-2:]
-    sums = updated(number, two, first_index, meta, group, part, far, blocks, vert, near, beside)
+    sums = updated(two, begin, group, part, far, asks, bands, vert, near, beside)
     phases, _, cells = sens.shape
     spot = lax.broadcasted_iota(jnp.int32, (1, cells), 1)
     projected = None
@@ -263,63 +306,83 @@
     one = 2 * rows * width * width
     partial = functools.partial
 
+    masks_type = pltpu.VMEM((8, 128), F32)
     with jax.named_scope("plan"):
-        meta, asks = call(
+        far_pair = moved_by(rhs, routes[-1])
+        table, asks, payload = call(
             partial(plan_kernel, columns, swaps),
-            [jax.ShapeDtypeStruct((2 * number,), jnp.int32), pltpu.VMEM((8, 128), F32)],
-            (outside(conn_src[0, 0]), conn_count[0], outside(tile_map), me),
-            [SMEM] * 4,
-            out_specs=[SMEM, VMEM],
+            [
+                jax.ShapeDtypeStruct((2 * number,), jnp.int32),
+                masks_type,
+                pltpu.VMEM((2 * rows + 16, width), BF16),
+            ],
+            (outside(conn_src[0, 0]), conn_count[0], outside(tile_map), me, outside(rhs)),
+            [SMEM] * 4 + [VMEM],
+            out_specs=[SMEM] + [VMEM] * 2,
         )
-        asks = held(asks)
-        told = [moved_by(asks, [(to, at) for at, to in pairs]) for pairs in routes]
-        rhs_held = held(rhs)
-        sends = call(pick_kernel, [tile] * number, (rhs_held, *told), [VMEM] * (1 + number))
+        asks, payload = held(asks), held(payload)
+        told9 = moved_by(asks, [(to, at) for at, to in routes[-2]])
+        told8 = moved_by(asks, routes[-1])
 
     with jax.named_scope("load"):
-        blocks, vert = call(
-            load_kernel,
-            [pltpu.VMEM(areal_blocks.shape[1:], BF16), pltpu.VMEM(vertical_blocks.shape[1:], BF16)],
-            (outside(areal_blocks[0]), outside(vertical_blocks[0])),
-            [pl.BlockSpec(memory_space=pltpu.HBM)] * 2,
-            [pltpu.SemaphoreType.DMA((2,))],
+        bands, vert = call(
+            partial(load_kernel, number),
+            [pltpu.VMEM((number, width, 2 * width), BF16), pltpu.VMEM(vertical_blocks.shape[1:], BF16)],
+            (table, outside(areal_blocks[0]), outside(vertical_blocks[0])),
+            [SMEM] + [pl.BlockSpec(memory_space=pltpu.HBM)] * 2,
+            [pltpu.SemaphoreType.DMA((2 * number + 1,))],
             moved=areal_blocks.size * 2 + vertical_blocks.size * 2,
         )
-        blocks, vert = held(blocks), held(vert)
-
+        bands, vert = held(bands), held(vert)
+
+    rhs_held = held(rhs)
     lam = rhs_held
-    outer = [rhs]
+    sends = [payload] * (number - 2)
+    outer = [payload]
     half = len(swaps) // 2
     for step in range(ITERS):
+        first = step == 0
         with jax.named_scope("apply"):
             arrived = [moved_by(x, pairs) for x, pairs in zip(sends, routes)]
+            if first:
+                even, odd = (arrived[swaps.index((1, color))] for color in (1, 0))
+                picked, told = call(
+                    partial(far_pick_kernel, number),
+                    [tile, masks_type],
+                    (me, far_pair, even, odd, told9, told8),
+                    [SMEM] + [VMEM] * 5,
+                )
+                arrived = [*arrived, moved_by(picked, shift_pairs(columns, 1)), far_pair]
+                told = [*arrived[:-2], held(told)]
             beside = beside_layers(outer)
             (part,) = call(own_kernel, [sums], (lam, rhs_held, vert), [VMEM] * 3, flops=one)
             (cross,) = call(
-                partial(cross_kernel, number),
+                cross_kernel,
                 [sums],
-                (meta, blocks, *arrived[:half]),
-                [SMEM] + [VMEM] * (1 + half),
+                (asks, bands, *arrived[:half]),
+                [VMEM] * (2 + half),
                 flops=4 * one,
             )
             (far,) = call(
-                partial(far_kernel, number),
+                far_kernel,
                 [sums],
-                (meta, blocks, held(cross), *arrived[-2:]),
-                [SMEM] + [VMEM] * 4,
+                (asks, bands, held(cross), *arrived[-2:]),
+                [VMEM] * 5,
                 flops=4 * one,
             )
-            tiles = (held(part), held(far), blocks, vert)
+            tiles = (held(part), held(far), asks, bands, vert)
             near = (*arrived[half:-2], *beside)
             if step < ITERS - 1:
                 lam, *rest = call(
-                    partial(update_kernel, number, two, half),
-                    [pair] + [tile] * (number + len(beside)),
-                    (meta, group, *tiles, *near, *told),
-                    [SMEM] * 2 + [VMEM] * (4 + len(near) + number),
+                    partial(update_kernel, number, two, half, first),
+                    [pair] + [tile] * (number + len(beside)) + ([masks_type] if first else []),
+                    (group, *tiles, *near, *told),
+                    [SMEM] + [VMEM] * (5 + len(near) + len(told)),
                     flops=one,
                 )
                 lam = held(lam)
+                if first:
+                    told = [held(rest.pop())]
                 sends, outer = rest[:number], rest[number:]
             else:
                 adjoint, pieces = call(
@@ -331,7 +394,6 @@
                         ),
                     ],
                     (
-                        meta,
                         group,
                         well_cells[0],
                         well_gain[0],
@@ -340,7 +402,7 @@
                         held(basis[0]),
                         *near,
                     ),
-                    [SMEM] * 4 + [VMEM] * (6 + len(near)),
+                    [SMEM] * 3 + [VMEM] * (7 + len(near)),
                     flops=one,
                 )
 

time: 84 us -> 82.4 us (0.981)
  waiting for transfers between devices: 10.5 us -> 20.1 us
  Pallas kernels: 18.1 us -> 10 us
  starting transfers between devices: 41.4 us -> 38.7 us
    ppermute x24 -> x20, waiting for transfers between devices: 10.5 us -> 20.1 us  [moved_by(): return held(lax.ppermute(x, 'areal', pairs))]
    pallas_call x16, Pallas kernels: 18.1 us -> 10 us  [call(): pl.pallas_call(kernel, out_shape=outs, in_specs=specs, out_specs=out_spec...]
    ppermute x24 -> x20, starting transfers between devices: 41.4 us -> 38.7 us  [moved_by(): return held(lax.ppermute(x, 'areal', pairs))]
  transfers between devices with their start and end apart: 27 -> 23, of which waited for: 10 -> 6; matrix products, arithmetic and copies ran while one was open for 0% -> 0% of each run, Pallas kernels for 13% -> 8%
where the time goes in v3:
time: 82.4 us; the launch traced here: 82.3 us
  starting transfers between devices  38.7 us (47%)
  waiting for transfers between devices  20.1 us (24%)
  blocking collectives  11.9 us (14%)
  Pallas kernels  10 us (12%)
  between operations  1.56 us (2%)
    ppermute x20, starting transfers between devices, moved_by(): return held(lax.ppermute(x, 'areal', pairs))  38.7 us
    ppermute x20, waiting for transfers between devices, moved_by(): return held(lax.ppermute(x, 'areal', pairs))  20.1 us
    all_to_all x1, blocking collectives, on_device(): landed = lax.all_to_all(pieces, ('areal', 'layer'), 0, 0, tiled=True)  11.9 us
    pallas_call x16, Pallas kernels, call(): pl.pallas_call(kernel, out_shape=outs, in_specs=specs, out_specs=out_spec...  10 us
  transfers between devices with their start and end apart: 23, of which 6 were waited for; matrix products, arithmetic and copies ran while one was open for 0% of the time, Pallas kernels for 8%

profile of v3, /device:TPU:0, one launch (start us, length us, event | category | flops | bytes accessed | tf_op | source)
XLA Modules:
  0.0 82.3 jit_solution(4303972737203029601)
XLA Ops:
  0.6 4.1 %collective-permute-start.2 = (bf16[224,384]{1,0:T(8,128)(2,1)}, bf16[224,384]{1,0:T(8,128)(2,1)S(1)}, u32[]{:S(2)}, u32[]{:S(2)}) collective-permute-start(bf16[224,384]{1,0:T(8,128)(2,1)} %bitcast.16), channel_id=1, source_target_pairs={{0,16},{2,18},{4,20},{6,22},{8,24},{10,26},{12,28},{14,30},{16,0},... | collective-permute-start | bytes 516104 | tf_op jit(solution)/shard_map/plan/ppermute | solution.py:258
  5.4 1.6 %plan.1 = (s32[12]{0:T(128)S(1)}, f32[8,128]{1,0:T(8,128)S(1)}, bf16[240,384]{1,0:T(8,128)(2,1)S(1)}) custom-call(s32[6]{0:T(128)} %bitcast.29, s32[1]{0:T(128)} %bitcast.15.count, s32[32]{0:T(128)} %tile_map.1, s32[1]{0:T(128)} %bitcast.6.me, bf16[224,384]{1,0:T(8,128)(2,1)} %bitcast.17), custom_call_target="tpu_custom_call" | custom-call | tf_op jit(solution)/shard_map/plan/pallas_call | solution.py:244
  7.0 1.6 %collective-permute-start.3 = (bf16[240,384]{1,0:T(8,128)(2,1)S(1)}, bf16[240,384]{1,0:T(8,128)(2,1)S(1)}, u32[]{:S(2)}, u32[]{:S(2)}) collective-permute-start(bf16[240,384]{1,0:T(8,128)(2,1)S(1)} %get-tuple-element.32), channel_id=1, source_target_pairs={{0,2},{2,0},{4,6},{6,4},{8,10},{10,8},{12,14},{14,12},{16,18},{18,... | collective-permute-start | bytes 552968 | tf_op jit(solution)/shard_map/apply/ppermute | solution.py:258
  8.6 2.3 %collective-permute-start.1 = (bf16[240,384]{1,0:T(8,128)(2,1)S(1)}, bf16[240,384]{1,0:T(8,128)(2,1)S(1)}, u32[]{:S(2)}, u32[]{:S(2)}) collective-permute-start(bf16[240,384]{1,0:T(8,128)(2,1)S(1)} %get-tuple-element.32), channel_id=1, source_target_pairs={{0,30},{2,4},{4,2},{6,8},{8,6},{10,12},{12,10},{14,16},{16,14},{18... | collective-permute-start | bytes 552968 | tf_op jit(solution)/shard_map/apply/ppermute | solution.py:258
  11.3 1.7 %collective-permute-start.5 = (f32[8,128]{1,0:T(8,128)S(1)}, f32[8,128]{1,0:T(8,128)S(1)}, u32[]{:S(2)}, u32[]{:S(2)}) collective-permute-start(f32[8,128]{1,0:T(8,128)S(1)} %get-tuple-element.30.asks), channel_id=1, source_target_pairs={{0,16},{2,18},{4,20},{6,22},{8,24},{10,26},{12,28},{14,30},{16,0},... | collective-permute-start | bytes 12296 | tf_op jit(solution)/shard_map/plan/ppermute | solution.py:258
  13.0 9.1 %collective-permute-done.5.told8 = f32[8,128]{1,0:T(8,128)S(1)} collective-permute-done((f32[8,128]{1,0:T(8,128)S(1)}, f32[8,128]{1,0:T(8,128)S(1)}, u32[]{:S(2)}, u32[]{:S(2)}) %collective-permute-start.5) | collective-permute-done | bytes 4128 | tf_op jit(solution)/shard_map/plan/ppermute | solution.py:258
  22.2 5.4 %collective-permute-done.4.told9 = f32[8,128]{1,0:T(8,128)S(1)} collective-permute-done((f32[8,128]{1,0:T(8,128)S(1)}, f32[8,128]{1,0:T(8,128)S(1)}, u32[]{:S(2)}, u32[]{:S(2)}) %collective-permute-start.4) | collective-permute-done | bytes 4128 | tf_op jit(solution)/shard_map/plan/ppermute | solution.py:258
  27.6 6.0 %collective-permute-start.6 = (bf16[112,384]{1,0:T(8,128)(2,1)S(1)}, bf16[112,384]{1,0:T(8,128)(2,1)S(1)}, u32[]{:S(2)}, u32[]{:S(2)}) collective-permute-start(bf16[112,384]{1,0:T(8,128)(2,1)S(1)} %get-tuple-element.33), channel_id=1, source_target_pairs={{0,30},{2,0},{4,2},{6,4},{8,6},{10,8},{12,10},{14,12},{16,14},{18,... | collective-permute-start | bytes 258056 | tf_op jit(solution)/shard_map/apply/ppermute | solution.py:258
  33.6 2.2 %load.1 = (bf16[6,384,768]{2,1,0:T(8,128)(2,1)S(1)}, bf16[2,2,384,384]{3,2,1,0:T(8,128)(2,1)S(1)}) custom-call(s32[12]{0:T(128)S(1)} %get-tuple-element.28.table, bf16[2,6,384,384]{3,2,1,0:T(8,128)(2,1)} %bitcast.26, bf16[2,2,384,384]{3,2,1,0:T(8,128)(2,1)} %bitcast.27), custom_call_target="tpu_custom_call" | custom-call | bytes 4718592 | tf_op jit(solution)/shard_map/load/pallas_call | solution.py:244
  37.4 2.1 %collective-permute-start.9 = (bf16[112,384]{1,0:T(8,128)(2,1)S(1)}, bf16[112,384]{1,0:T(8,128)(2,1)S(1)}, u32[]{:S(2)}, u32[]{:S(2)}) collective-permute-start(bf16[112,384]{1,0:T(8,128)(2,1)S(1)} %get-tuple-element.36), channel_id=1, source_target_pairs={{0,28},{2,30},{4,8},{6,10},{8,4},{10,6},{12,16},{14,18},{16,12},{1... | collective-permute-start | bytes 258056 | tf_op jit(solution)/shard_map/apply/ppermute | solution.py:258
  39.5 3.8 %collective-permute-start.10 = (bf16[112,384]{1,0:T(8,128)(2,1)S(1)}, bf16[112,384]{1,0:T(8,128)(2,1)S(1)}, u32[]{:S(2)}, u32[]{:S(2)}) collective-permute-start(bf16[112,384]{1,0:T(8,128)(2,1)S(1)} %get-tuple-element.37), channel_id=1, source_target_pairs={{0,30},{2,4},{4,2},{6,8},{8,6},{10,12},{12,10},{14,16},{16,14},{18... | collective-permute-start | bytes 258056 | tf_op jit(solution)/shard_map/apply/ppermute | solution.py:258
  43.3 2.4 %collective-permute-start.12 = (bf16[112,384]{1,0:T(8,128)(2,1)S(1)}, bf16[112,384]{1,0:T(8,128)(2,1)S(1)}, u32[]{:S(2)}, u32[]{:S(2)}) collective-permute-start(bf16[112,384]{1,0:T(8,128)(2,1)S(1)} %get-tuple-element.39), channel_id=1, source_target_pairs={{0,16},{2,18},{4,20},{6,22},{8,24},{10,26},{12,28},{14,30},{16,0},... | collective-permute-start | bytes 258056 | tf_op jit(solution)/shard_map/apply/ppermute | solution.py:258
  45.7 1.9 %collective-permute-start.13 = (bf16[112,384]{1,0:T(8,128)(2,1)S(1)}, bf16[112,384]{1,0:T(8,128)(2,1)S(1)}, u32[]{:S(2)}, u32[]{:S(2)}) collective-permute-start(bf16[112,384]{1,0:T(8,128)(2,1)S(1)} %get-tuple-element.40), channel_id=1, source_target_pairs={{0,4},{2,6},{4,0},{6,2},{8,12},{10,14},{12,8},{14,10},{16,20},{18,... | collective-permute-start | bytes 258056 | tf_op jit(solution)/shard_map/apply/ppermute | solution.py:258
  47.6 2.0 %collective-permute-start.14 = (bf16[112,384]{1,0:T(8,128)(2,1)S(1)}, bf16[112,384]{1,0:T(8,128)(2,1)S(1)}, u32[]{:S(2)}, u32[]{:S(2)}) collective-permute-start(bf16[112,384]{1,0:T(8,128)(2,1)S(1)} %get-tuple-element.41), channel_id=1, source_target_pairs={{0,2},{2,0},{4,6},{6,4},{8,10},{10,8},{12,14},{14,12},{16,18},{18,... | collective-permute-start | bytes 258056 | tf_op jit(solution)/shard_map/apply/ppermute | solution.py:258
  50.3 1.8 %collective-permute-done.11.refs_0_ = bf16[112,384]{1,0:T(8,128)(2,1)S(1)} collective-permute-done((bf16[112,384]{1,0:T(8,128)(2,1)S(1)}, bf16[112,384]{1,0:T(8,128)(2,1)S(1)}, u32[]{:S(2)}, u32[]{:S(2)}) %collective-permute-start.11) | collective-permute-done | bytes 86048 | tf_op jit(solution)/shard_map/apply/ppermute | solution.py:258
  53.0 2.8 %collective-permute-start.16 = (bf16[112,384]{1,0:T(8,128)(2,1)S(1)}, bf16[112,384]{1,0:T(8,128)(2,1)S(1)}, u32[]{:S(2)}, u32[]{:S(2)}) collective-permute-start(bf16[112,384]{1,0:T(8,128)(2,1)S(1)} %get-tuple-element.45), channel_id=1, source_target_pairs={{0,28},{2,30},{4,8},{6,10},{8,4},{10,6},{12,16},{14,18},{16,12},{1... | collective-permute-start | bytes 258056 | tf_op jit(solution)/shard_map/apply/ppermute | solution.py:258
  55.9 3.0 %collective-permute-start.17 = (bf16[112,384]{1,0:T(8,128)(2,1)S(1)}, bf16[112,384]{1,0:T(8,128)(2,1)S(1)}, u32[]{:S(2)}, u32[]{:S(2)}) collective-permute-start(bf16[112,384]{1,0:T(8,128)(2,1)S(1)} %get-tuple-element.46), channel_id=1, source_target_pairs={{0,30},{2,4},{4,2},{6,8},{8,6},{10,12},{12,10},{14,16},{16,14},{18... | collective-permute-start | bytes 258056 | tf_op jit(solution)/shard_map/apply/ppermute | solution.py:258
  58.8 3.2 %collective-permute-start.19 = (bf16[112,384]{1,0:T(8,128)(2,1)S(1)}, bf16[112,384]{1,0:T(8,128)(2,1)S(1)}, u32[]{:S(2)}, u32[]{:S(2)}) collective-permute-start(bf16[112,384]{1,0:T(8,128)(2,1)S(1)} %get-tuple-element.48), channel_id=1, source_target_pairs={{0,16},{2,18},{4,20},{6,22},{8,24},{10,26},{12,28},{14,30},{16,0},... | collective-permute-start | bytes 258056 | tf_op jit(solution)/shard_map/apply/ppermute | solution.py:258
  62.1 1.3 %collective-permute-start.21 = (bf16[112,384]{1,0:T(8,128)(2,1)S(1)}, bf16[112,384]{1,0:T(8,128)(2,1)S(1)}, u32[]{:S(2)}, u32[]{:S(2)}) collective-permute-start(bf16[112,384]{1,0:T(8,128)(2,1)S(1)} %get-tuple-element.50), channel_id=1, source_target_pairs={{0,2},{2,0},{4,6},{6,4},{8,10},{10,8},{12,14},{14,12},{16,18},{18,... | collective-permute-start | bytes 258056 | tf_op jit(solution)/shard_map/apply/ppermute | solution.py:258
  63.4 1.4 %collective-permute-done.17.refs_1_ = bf16[112,384]{1,0:T(8,128)(2,1)S(1)} collective-permute-done((bf16[112,384]{1,0:T(8,128)(2,1)S(1)}, bf16[112,384]{1,0:T(8,128)(2,1)S(1)}, u32[]{:S(2)}, u32[]{:S(2)}) %collective-permute-start.17) | collective-permute-done | bytes 86048 | tf_op jit(solution)/shard_map/apply/ppermute | solution.py:258
  65.5 2.1 %collective-permute-done.18.refs_0_ = bf16[112,384]{1,0:T(8,128)(2,1)S(1)} collective-permute-done((bf16[112,384]{1,0:T(8,128)(2,1)S(1)}, bf16[112,384]{1,0:T(8,128)(2,1)S(1)}, u32[]{:S(2)}, u32[]{:S(2)}) %collective-permute-start.18) | collective-permute-done | bytes 86048 | tf_op jit(solution)/shard_map/apply/ppermute | solution.py:258
  68.0 1.7 %apply.25 = (bf16[2,112,384]{2,1,0:T(8,128)(2,1)}, f32[32,8,112]{2,1,0:T(8,128)S(1)}) custom-call(s32[1]{0:T(128)} %bitcast.group, s32[2,4]{1,0:T(2,128)S(1)} %bitcast.24, f32[2,4]{1,0:T(2,128)S(1)} %bitcast.25, f32[2,112,384]{2,1,0:T(8,128)S(1)} %apply.22.part, f32[2,112,384]{2,1,0:T(8,128)S(1)} %apply.24.far, f32[8,128]{1,0:T(8,128)S(1)} %get-tuple-element.30.asks, ...), custom_call_target="tpu_custom_call" | custom-call | flops 33030144 | bytes 165150 | tf_op jit(solution)/shard_map/apply/pallas_call | solution.py:244
  69.7 11.9 %all_to_all.5.pieces = f32[32,8,112]{2,1,0:T(8,128)S(1)} all-to-all(f32[32,8,112]{2,1,0:T(8,128)S(1)} %get-tuple-element.53), channel_id=1, replica_groups=mesh['areal'=16,'layer'=2] {'areal','layer'}, dimensions={0} | all-to-all | bytes 229376 | tf_op jit(solution)/shard_map/project/all_to_all | solution.py:411
  81.6 0.7 project.1
  (49 shorter events, 4.6 us)
Async XLA Ops:
  0.6 35.3 %copy-start = (bf16[1,2,112,384]{3,2,1,0:T(8,128)(2,1)S(1)}, bf16[1,2,112,384]{3,2,1,0:T(8,128)(2,1)}, u32[]{:S(2)}) copy-start(bf16[1,2,112,384]{3,2,1,0:T(8,128)(2,1)} %param.10) | copy-start | bytes 516100
  0.6 26.9 %collective-permute-start.2 = (bf16[224,384]{1,0:T(8,128)(2,1)}, bf16[224,384]{1,0:T(8,128)(2,1)S(1)}, u32[]{:S(2)}, u32[]{:S(2)}) collective-permute-start(bf16[224,384]{1,0:T(8,128)(2,1)} %bitcast.16), channel_id=1, source_target_pairs={{0,16},{2,18},{4,20},{6,22},{8,24},{10,26},{12,28},{14,30},{16,0},... | collective-permute-start | bytes 516104 | tf_op jit(solution)/shard_map/plan/ppermute | solution.py:258
  7.0 20.6 %collective-permute-start.3 = (bf16[240,384]{1,0:T(8,128)(2,1)S(1)}, bf16[240,384]{1,0:T(8,128)(2,1)S(1)}, u32[]{:S(2)}, u32[]{:S(2)}) collective-permute-start(bf16[240,384]{1,0:T(8,128)(2,1)S(1)} %get-tuple-element.32), channel_id=1, source_target_pairs={{0,2},{2,0},{4,6},{6,4},{8,10},{10,8},{12,14},{14,12},{16,18},{18,... | collective-permute-start | bytes 552968 | tf_op jit(solution)/shard_map/apply/ppermute | solution.py:258
  8.6 19.0 %collective-permute-start.1 = (bf16[240,384]{1,0:T(8,128)(2,1)S(1)}, bf16[240,384]{1,0:T(8,128)(2,1)S(1)}, u32[]{:S(2)}, u32[]{:S(2)}) collective-permute-start(bf16[240,384]{1,0:T(8,128)(2,1)S(1)} %get-tuple-element.32), channel_id=1, source_target_pairs={{0,30},{2,4},{4,2},{6,8},{8,6},{10,12},{12,10},{14,16},{16,14},{18... | collective-permute-start | bytes 552968 | tf_op jit(solution)/shard_map/apply/ppermute | solution.py:258
  10.8 25.4 %collective-permute-start = (bf16[240,384]{1,0:T(8,128)(2,1)S(1)}, bf16[240,384]{1,0:T(8,128)(2,1)S(1)}, u32[]{:S(2)}, u32[]{:S(2)}) collective-permute-start(bf16[240,384]{1,0:T(8,128)(2,1)S(1)} %get-tuple-element.32), channel_id=1, source_target_pairs={{0,28},{2,30},{4,8},{6,10},{8,4},{10,6},{12,16},{14,18},{16,12},{1... | collective-permute-start | bytes 552968 | tf_op jit(solution)/shard_map/apply/ppermute | solution.py:258
  11.3 10.8 %collective-permute-start.5 = (f32[8,128]{1,0:T(8,128)S(1)}, f32[8,128]{1,0:T(8,128)S(1)}, u32[]{:S(2)}, u32[]{:S(2)}) collective-permute-start(f32[8,128]{1,0:T(8,128)S(1)} %get-tuple-element.30.asks), channel_id=1, source_target_pairs={{0,16},{2,18},{4,20},{6,22},{8,24},{10,26},{12,28},{14,30},{16,0},... | collective-permute-start | bytes 12296 | tf_op jit(solution)/shard_map/plan/ppermute | solution.py:258
  22.1 5.4 %collective-permute-start.4 = (f32[8,128]{1,0:T(8,128)S(1)}, f32[8,128]{1,0:T(8,128)S(1)}, u32[]{:S(2)}, u32[]{:S(2)}) collective-permute-start(f32[8,128]{1,0:T(8,128)S(1)} %get-tuple-element.30.asks), channel_id=1, source_target_pairs={{14,0},{16,2},{18,4},{20,6},{22,8},{24,10},{26,12},{28,14},{30,16}... | collective-permute-start | bytes 12296 | tf_op jit(solution)/shard_map/plan/ppermute | solution.py:258
  27.6 9.3 %collective-permute-start.8 = (bf16[240,384]{1,0:T(8,128)(2,1)S(1)}, bf16[240,384]{1,0:T(8,128)(2,1)S(1)}, u32[]{:S(2)}, u32[]{:S(2)}) collective-permute-start(bf16[240,384]{1,0:T(8,128)(2,1)S(1)} %get-tuple-element.32), channel_id=1, source_target_pairs={{0,1},{1,0},{2,3},{3,2},{4,5},{5,4},{6,7},{7,6},{8,9},{9,8},{10,11... | collective-permute-start | bytes 552968 | tf_op jit(solution)/shard_map/apply/ppermute | solution.py:268
  27.6 9.3 %collective-permute-start.7 = (bf16[240,384]{1,0:T(8,128)(2,1)S(1)}, bf16[240,384]{1,0:T(8,128)(2,1)S(1)}, u32[]{:S(2)}, u32[]{:S(2)}) collective-permute-start(bf16[240,384]{1,0:T(8,128)(2,1)S(1)} %get-tuple-element.32), channel_id=1, source_target_pairs={{0,4},{2,6},{4,0},{6,2},{8,12},{10,14},{12,8},{14,10},{16,20},{18,... | collective-permute-start | bytes 552968 | tf_op jit(solution)/shard_map/apply/ppermute | solution.py:258
  27.6 8.9 %collective-permute-start.6 = (bf16[112,384]{1,0:T(8,128)(2,1)S(1)}, bf16[112,384]{1,0:T(8,128)(2,1)S(1)}, u32[]{:S(2)}, u32[]{:S(2)}) collective-permute-start(bf16[112,384]{1,0:T(8,128)(2,1)S(1)} %get-tuple-element.33), channel_id=1, source_target_pairs={{0,30},{2,0},{4,2},{6,4},{8,6},{10,8},{12,10},{14,12},{16,14},{18,... | collective-permute-start | bytes 258056 | tf_op jit(solution)/shard_map/apply/ppermute | solution.py:258
  37.4 10.2 %collective-permute-start.9 = (bf16[112,384]{1,0:T(8,128)(2,1)S(1)}, bf16[112,384]{1,0:T(8,128)(2,1)S(1)}, u32[]{:S(2)}, u32[]{:S(2)}) collective-permute-start(bf16[112,384]{1,0:T(8,128)(2,1)S(1)} %get-tuple-element.36), channel_id=1, source_target_pairs={{0,28},{2,30},{4,8},{6,10},{8,4},{10,6},{12,16},{14,18},{16,12},{1... | collective-permute-start | bytes 258056 | tf_op jit(solution)/shard_map/apply/ppermute | solution.py:258
  39.5 10.1 %collective-permute-start.10 = (bf16[112,384]{1,0:T(8,128)(2,1)S(1)}, bf16[112,384]{1,0:T(8,128)(2,1)S(1)}, u32[]{:S(2)}, u32[]{:S(2)}) collective-permute-start(bf16[112,384]{1,0:T(8,128)(2,1)S(1)} %get-tuple-element.37), channel_id=1, source_target_pairs={{0,30},{2,4},{4,2},{6,8},{8,6},{10,12},{12,10},{14,16},{16,14},{18... | collective-permute-start | bytes 258056 | tf_op jit(solution)/shard_map/apply/ppermute | solution.py:258
  43.3 8.8 %collective-permute-start.11 = (bf16[112,384]{1,0:T(8,128)(2,1)S(1)}, bf16[112,384]{1,0:T(8,128)(2,1)S(1)}, u32[]{:S(2)}, u32[]{:S(2)}) collective-permute-start(bf16[112,384]{1,0:T(8,128)(2,1)S(1)} %get-tuple-element.38), channel_id=1, source_target_pairs={{0,14},{2,16},{4,18},{6,20},{8,22},{10,24},{12,26},{14,28},{16,30}... | collective-permute-start | bytes 258056 | tf_op jit(solution)/shard_map/apply/ppermute | solution.py:258
  43.3 8.8 %collective-permute-start.12 = (bf16[112,384]{1,0:T(8,128)(2,1)S(1)}, bf16[112,384]{1,0:T(8,128)(2,1)S(1)}, u32[]{:S(2)}, u32[]{:S(2)}) collective-permute-start(bf16[112,384]{1,0:T(8,128)(2,1)S(1)} %get-tuple-element.39), channel_id=1, source_target_pairs={{0,16},{2,18},{4,20},{6,22},{8,24},{10,26},{12,28},{14,30},{16,0},... | collective-permute-start | bytes 258056 | tf_op jit(solution)/shard_map/apply/ppermute | solution.py:258
  45.7 6.7 %collective-permute-start.13 = (bf16[112,384]{1,0:T(8,128)(2,1)S(1)}, bf16[112,384]{1,0:T(8,128)(2,1)S(1)}, u32[]{:S(2)}, u32[]{:S(2)}) collective-permute-start(bf16[112,384]{1,0:T(8,128)(2,1)S(1)} %get-tuple-element.40), channel_id=1, source_target_pairs={{0,4},{2,6},{4,0},{6,2},{8,12},{10,14},{12,8},{14,10},{16,20},{18,... | collective-permute-start | bytes 258056 | tf_op jit(solution)/shard_map/apply/ppermute | solution.py:258
  47.6 4.9 %collective-permute-start.14 = (bf16[112,384]{1,0:T(8,128)(2,1)S(1)}, bf16[112,384]{1,0:T(8,128)(2,1)S(1)}, u32[]{:S(2)}, u32[]{:S(2)}) collective-permute-start(bf16[112,384]{1,0:T(8,128)(2,1)S(1)} %get-tuple-element.41), channel_id=1, source_target_pairs={{0,2},{2,0},{4,6},{6,4},{8,10},{10,8},{12,14},{14,12},{16,18},{18,... | collective-permute-start | bytes 258056 | tf_op jit(solution)/shard_map/apply/ppermute | solution.py:258
  49.6 2.9 %collective-permute-start.15 = (bf16[112,384]{1,0:T(8,128)(2,1)S(1)}, bf16[112,384]{1,0:T(8,128)(2,1)S(1)}, u32[]{:S(2)}, u32[]{:S(2)}) collective-permute-start(bf16[112,384]{1,0:T(8,128)(2,1)S(1)} %get-tuple-element.42), channel_id=1, source_target_pairs={{0,1},{1,0},{2,3},{3,2},{4,5},{5,4},{6,7},{7,6},{8,9},{9,8},{10,11... | collective-permute-start | bytes 258056 | tf_op jit(solution)/shard_map/apply/ppermute | solution.py:268
  53.0 9.0 %collective-permute-start.16 = (bf16[112,384]{1,0:T(8,128)(2,1)S(1)}, bf16[112,384]{1,0:T(8,128)(2,1)S(1)}, u32[]{:S(2)}, u32[]{:S(2)}) collective-permute-start(bf16[112,384]{1,0:T(8,128)(2,1)S(1)} %get-tuple-element.45), channel_id=1, source_target_pairs={{0,28},{2,30},{4,8},{6,10},{8,4},{10,6},{12,16},{14,18},{16,12},{1... | collective-permute-start | bytes 258056 | tf_op jit(solution)/shard_map/apply/ppermute | solution.py:258
  55.9 8.9 %collective-permute-start.17 = (bf16[112,384]{1,0:T(8,128)(2,1)S(1)}, bf16[112,384]{1,0:T(8,128)(2,1)S(1)}, u32[]{:S(2)}, u32[]{:S(2)}) collective-permute-start(bf16[112,384]{1,0:T(8,128)(2,1)S(1)} %get-tuple-element.46), channel_id=1, source_target_pairs={{0,30},{2,4},{4,2},{6,8},{8,6},{10,12},{12,10},{14,16},{16,14},{18... | collective-permute-start | bytes 258056 | tf_op jit(solution)/shard_map/apply/ppermute | solution.py:258
  58.8 8.8 %collective-permute-start.18 = (bf16[112,384]{1,0:T(8,128)(2,1)S(1)}, bf16[112,384]{1,0:T(8,128)(2,1)S(1)}, u32[]{:S(2)}, u32[]{:S(2)}) collective-permute-start(bf16[112,384]{1,0:T(8,128)(2,1)S(1)} %get-tuple-element.47), channel_id=1, source_target_pairs={{0,14},{2,16},{4,18},{6,20},{8,22},{10,24},{12,26},{14,28},{16,30}... | collective-permute-start | bytes 258056 | tf_op jit(solution)/shard_map/apply/ppermute | solution.py:258
  58.8 8.8 %collective-permute-start.19 = (bf16[112,384]{1,0:T(8,128)(2,1)S(1)}, bf16[112,384]{1,0:T(8,128)(2,1)S(1)}, u32[]{:S(2)}, u32[]{:S(2)}) collective-permute-start(bf16[112,384]{1,0:T(8,128)(2,1)S(1)} %get-tuple-element.48), channel_id=1, source_target_pairs={{0,16},{2,18},{4,20},{6,22},{8,24},{10,26},{12,28},{14,30},{16,0},... | collective-permute-start | bytes 258056 | tf_op jit(solution)/shard_map/apply/ppermute | solution.py:258
  62.1 5.9 %collective-permute-start.20 = (bf16[112,384]{1,0:T(8,128)(2,1)S(1)}, bf16[112,384]{1,0:T(8,128)(2,1)S(1)}, u32[]{:S(2)}, u32[]{:S(2)}) collective-permute-start(bf16[112,384]{1,0:T(8,128)(2,1)S(1)} %get-tuple-element.49), channel_id=1, source_target_pairs={{0,4},{2,6},{4,0},{6,2},{8,12},{10,14},{12,8},{14,10},{16,20},{18,... | collective-permute-start | bytes 258056 | tf_op jit(solution)/shard_map/apply/ppermute | solution.py:258
  62.1 5.9 %collective-permute-start.21 = (bf16[112,384]{1,0:T(8,128)(2,1)S(1)}, bf16[112,384]{1,0:T(8,128)(2,1)S(1)}, u32[]{:S(2)}, u32[]{:S(2)}) collective-permute-start(bf16[112,384]{1,0:T(8,128)(2,1)S(1)} %get-tuple-element.50), channel_id=1, source_target_pairs={{0,2},{2,0},{4,6},{6,4},{8,10},{10,8},{12,14},{14,12},{16,18},{18,... | collective-permute-start | bytes 258056 | tf_op jit(solution)/shard_map/apply/ppermute | solution.py:258
  64.8 3.2 %collective-permute-start.22 = (bf16[112,384]{1,0:T(8,128)(2,1)S(1)}, bf16[112,384]{1,0:T(8,128)(2,1)S(1)}, u32[]{:S(2)}, u32[]{:S(2)}) collective-permute-start(bf16[112,384]{1,0:T(8,128)(2,1)S(1)} %get-tuple-element.51), channel_id=1, source_target_pairs={{0,1},{1,0},{2,3},{3,2},{4,5},{5,4},{6,7},{7,6},{8,9},{9,8},{10,11... | collective-permute-start | bytes 258056 | tf_op jit(solution)/shard_map/apply/ppermute | solution.py:268
  (4 other events, 11.6 us)

commit v4 on v3

--- a/solution.py
+++ b/solution.py
@@ -116,12 +116,12 @@
     return chosen(mask, ref[0:rows].astype(F32), ref[rows : 2 * rows].astype(F32))
 
 
-def far_pick_kernel(number, me, pair, even, odd, told9, told8, tile, told):
+def far_pick_kernel(number, me, pair, asks, even, odd, part, tile, relayed):
     rows = tile.shape[0]
     theirs = jnp.where(lax.rem(me[0], 2) == 0, asks_of(even), asks_of(odd))
     tile[...] = tile_of(pair, theirs[number - 2 : number - 1, :], rows)
-    line = lax.broadcasted_iota(jnp.int32, told.shape, 0)
-    told[...] = jnp.where(line == number - 2, told9[...], told8[...])
+    relayed[...] = asks[...]
+    relayed[number - 2 : number - 1, :] = theirs[number - 2 : number - 1, :]
 
 
 def own_kernel(lam, rhs, vert, part):
@@ -321,8 +321,6 @@
             out_specs=[SMEM] + [VMEM] * 2,
         )
         asks, payload = held(asks), held(payload)
-        told9 = moved_by(asks, [(to, at) for at, to in routes[-2]])
-        told8 = moved_by(asks, routes[-1])
 
     with jax.named_scope("load"):
         bands, vert = call(
@@ -344,18 +342,19 @@
         first = step == 0
         with jax.named_scope("apply"):
             arrived = [moved_by(x, pairs) for x, pairs in zip(sends, routes)]
+            (part,) = call(own_kernel, [sums], (lam, rhs_held, vert), [VMEM] * 3, flops=one)
+            part = held(part)
             if first:
                 even, odd = (arrived[swaps.index((1, color))] for color in (1, 0))
-                picked, told = call(
+                picked, relayed = call(
                     partial(far_pick_kernel, number),
                     [tile, masks_type],
-                    (me, far_pair, even, odd, told9, told8),
+                    (me, far_pair, asks, even, odd, part),
                     [SMEM] + [VMEM] * 5,
                 )
                 arrived = [*arrived, moved_by(picked, shift_pairs(columns, 1)), far_pair]
-                told = [*arrived[:-2], held(told)]
+                told = [*arrived[:-2], moved_by(relayed, routes[-1])]
             beside = beside_layers(outer)
-            (part,) = call(own_kernel, [sums], (lam, rhs_held, vert), [VMEM] * 3, flops=one)
             (cross,) = call(
                 cross_kernel,
                 [sums],
@@ -370,7 +369,7 @@
                 [VMEM] * 5,
                 flops=4 * one,
             )
-            tiles = (held(part), held(far), asks, bands, vert)
+            tiles = (part, held(far), asks, bands, vert)
             near = (*arrived[half:-2], *beside)
             if step < ITERS - 1:
                 lam, *rest = call(

time: 82.4 us -> 80.2 us (0.973)
  waiting for transfers between devices: 20.1 us -> 14.7 us
  starting transfers between devices: 38.7 us -> 34.3 us
  Pallas kernels: 10 us -> 14 us
  local copies, waits for them, and re-layouts: 0.03 us -> 3.43 us
    ppermute x20 -> x19, waiting for transfers between devices: 20.1 us -> 14.7 us  [moved_by(): return held(lax.ppermute(x, 'areal', pairs))]
    ppermute x20 -> x19, starting transfers between devices: 38.7 us -> 34.2 us  [moved_by(): return held(lax.ppermute(x, 'areal', pairs))]
    pallas_call x16, Pallas kernels: 10 us -> 14 us  [call(): pl.pallas_call(kernel, out_shape=outs, in_specs=specs, out_specs=out_spec...]
    unnamed x10 -> x36, local copies, waits for them, and re-layouts: 0.03 us -> 3.43 us
  transfers between devices with their start and end apart: 23 -> 22, of which waited for: 6 -> 8; matrix products, arithmetic and copies ran while one was open for 0% -> 0% of each run, Pallas kernels for 8% -> 12%
where the time goes in v4:
time: 80.2 us; the launch traced here: 80 us
  starting transfers between devices  34.3 us (43%)
  waiting for transfers between devices  14.7 us (18%)
  Pallas kernels  14 us (17%)
  blocking collectives  12.1 us (15%)
  local copies, waits for them, and re-layouts  3.43 us (4%)
  between operations  1.61 us (2%)
    ppermute x19, starting transfers between devices, moved_by(): return held(lax.ppermute(x, 'areal', pairs))  34.2 us
    ppermute x19, waiting for transfers between devices, moved_by(): return held(lax.ppermute(x, 'areal', pairs))  14.7 us
    pallas_call x16, Pallas kernels, call(): pl.pallas_call(kernel, out_shape=outs, in_specs=specs, out_specs=out_spec...  14 us
    all_to_all x1, blocking collectives, on_device(): landed = lax.all_to_all(pieces, ('areal', 'layer'), 0, 0, tiled=True)  12.1 us
    unnamed x36, local copies, waits for them, and re-layouts  3.43 us
  transfers between devices with their start and end apart: 22, of which 8 were waited for; matrix products, arithmetic and copies ran while one was open for 0% of the time, Pallas kernels for 12%

profile of v4, /device:TPU:0, one launch (start us, length us, event | category | flops | bytes accessed | tf_op | source)
XLA Modules:
  0.0 80.0 jit_solution(15322967129014658802)
XLA Ops:
  0.6 4.1 %collective-permute-start.2 = (bf16[224,384]{1,0:T(8,128)(2,1)}, bf16[224,384]{1,0:T(8,128)(2,1)S(1)}, u32[]{:S(2)}, u32[]{:S(2)}) collective-permute-start(bf16[224,384]{1,0:T(8,128)(2,1)} %bitcast.16), channel_id=1, source_target_pairs={{0,16},{2,18},{4,20},{6,22},{8,24},{10,26},{12,28},{14,30},{16,0},... | collective-permute-start | bytes 516104 | tf_op jit(solution)/shard_map/plan/ppermute | solution.py:258
  5.4 1.7 %plan.1 = (s32[12]{0:T(128)S(1)}, f32[8,128]{1,0:T(8,128)S(1)}, bf16[240,384]{1,0:T(8,128)(2,1)}) custom-call(s32[6]{0:T(128)} %bitcast.29, s32[1]{0:T(128)} %bitcast.15.count, s32[32]{0:T(128)} %tile_map.1, s32[1]{0:T(128)} %bitcast.6.me, bf16[224,384]{1,0:T(8,128)(2,1)} %bitcast.17), custom_call_target="tpu_custom_call" | custom-call | tf_op jit(solution)/shard_map/plan/pallas_call | solution.py:244
  7.1 1.6 %collective-permute-start.3 = (bf16[240,384]{1,0:T(8,128)(2,1)}, bf16[240,384]{1,0:T(8,128)(2,1)S(1)}, u32[]{:S(2)}, u32[]{:S(2)}) collective-permute-start(bf16[240,384]{1,0:T(8,128)(2,1)} %get-tuple-element.32), channel_id=1, source_target_pairs={{0,2},{2,0},{4,6},{6,4},{8,10},{10,8},{12,14},{14,12},{16,18},{18,... | collective-permute-start | bytes 552968 | tf_op jit(solution)/shard_map/apply/ppermute | solution.py:258
  8.7 2.3 %collective-permute-start.1 = (bf16[240,384]{1,0:T(8,128)(2,1)}, bf16[240,384]{1,0:T(8,128)(2,1)S(1)}, u32[]{:S(2)}, u32[]{:S(2)}) collective-permute-start(bf16[240,384]{1,0:T(8,128)(2,1)} %get-tuple-element.32), channel_id=1, source_target_pairs={{0,30},{2,4},{4,2},{6,8},{8,6},{10,12},{12,10},{14,16},{16,14},{18... | collective-permute-start | bytes 552968 | tf_op jit(solution)/shard_map/apply/ppermute | solution.py:258
  11.5 1.8 %collective-permute-done.2.pair.refs_1_ = bf16[224,384]{1,0:T(8,128)(2,1)S(1)} collective-permute-done((bf16[224,384]{1,0:T(8,128)(2,1)}, bf16[224,384]{1,0:T(8,128)(2,1)S(1)}, u32[]{:S(2)}, u32[]{:S(2)}) %collective-permute-start.2) | collective-permute-done | bytes 172064 | tf_op jit(solution)/shard_map/plan/ppermute | solution.py:258
  13.9 1.3 %collective-permute-start.5 = (bf16[240,384]{1,0:T(8,128)(2,1)}, bf16[240,384]{1,0:T(8,128)(2,1)}, u32[]{:S(2)}, u32[]{:S(2)}) collective-permute-start(bf16[240,384]{1,0:T(8,128)(2,1)} %get-tuple-element.32), channel_id=1, source_target_pairs={{0,4},{2,6},{4,0},{6,2},{8,12},{10,14},{12,8},{14,10},{16,20},{18,... | collective-permute-start | bytes 552968 | tf_op jit(solution)/shard_map/apply/ppermute | solution.py:258
  15.2 2.3 %load.1 = (bf16[6,384,768]{2,1,0:T(8,128)(2,1)S(1)}, bf16[2,2,384,384]{3,2,1,0:T(8,128)(2,1)S(1)}) custom-call(s32[12]{0:T(128)S(1)} %get-tuple-element.28.table, bf16[2,6,384,384]{3,2,1,0:T(8,128)(2,1)} %bitcast.26, bf16[2,2,384,384]{3,2,1,0:T(8,128)(2,1)} %bitcast.27), custom_call_target="tpu_custom_call" | custom-call | bytes 4718592 | tf_op jit(solution)/shard_map/load/pallas_call | solution.py:244
  18.8 3.2 %collective-permute-done.1.refs_1_.even.refs_4_ = bf16[240,384]{1,0:T(8,128)(2,1)S(1)} collective-permute-done((bf16[240,384]{1,0:T(8,128)(2,1)}, bf16[240,384]{1,0:T(8,128)(2,1)S(1)}, u32[]{:S(2)}, u32[]{:S(2)}) %collective-permute-start.1) | collective-permute-done | bytes 184352 | tf_op jit(solution)/shard_map/apply/ppermute | solution.py:258
  23.5 1.9 %collective-permute-start.4 = (bf16[112,384]{1,0:T(8,128)(2,1)}, bf16[112,384]{1,0:T(8,128)(2,1)}, u32[]{:S(2)}, u32[]{:S(2)}) collective-permute-start(bf16[112,384]{1,0:T(8,128)(2,1)} %get-tuple-element.33), channel_id=1, source_target_pairs={{0,30},{2,0},{4,2},{6,4},{8,6},{10,8},{12,10},{14,12},{16,14},{18,... | collective-permute-start | bytes 258056 | tf_op jit(solution)/shard_map/apply/ppermute | solution.py:258
  27.1 1.4 %apply.14.cross = f32[2,112,384]{2,1,0:T(8,128)S(1)} custom-call(f32[8,128]{1,0:T(8,128)S(1)} %get-tuple-element.30.asks, bf16[6,384,768]{2,1,0:T(8,128)(2,1)S(1)} %get-tuple-element.31.bands, bf16[240,384]{1,0:T(8,128)(2,1)} %collective-permute-done.refs_0_.refs_3_, bf16[240,384]{1,0:T(8,128)(2,1)S(1)} %copy-done.7), custom_call_target="tpu_custom_call" | custom-call | flops 132120576 | bytes 660602 | tf_op jit(solution)/shard_map/apply/pallas_call | solution.py:244
  28.5 5.3 %collective-permute-done.4.refs_0_ = bf16[112,384]{1,0:T(8,128)(2,1)} collective-permute-done((bf16[112,384]{1,0:T(8,128)(2,1)}, bf16[112,384]{1,0:T(8,128)(2,1)}, u32[]{:S(2)}, u32[]{:S(2)}) %collective-permute-start.4) | collective-permute-done | bytes 86048 | tf_op jit(solution)/shard_map/apply/ppermute | solution.py:258
  35.1 1.7 %apply.17 = (bf16[224,384]{1,0:T(8,128)(2,1)S(1)}, bf16[112,384]{1,0:T(8,128)(2,1)S(1)}, bf16[112,384]{1,0:T(8,128)(2,1)S(1)}, bf16[112,384]{1,0:T(8,128)(2,1)S(...) custom-call(s32[1]{0:T(128)} %bitcast.group, ...), custom_call_target="tpu_custom_call" | custom-call | flops 33030144 | bytes 165150 | tf_op jit(solution)/shard_map/apply/pallas_call | solution.py:244
  36.8 2.6 %collective-permute-start.8 = (bf16[112,384]{1,0:T(8,128)(2,1)S(1)}, bf16[112,384]{1,0:T(8,128)(2,1)S(1)}, u32[]{:S(2)}, u32[]{:S(2)}) collective-permute-start(bf16[112,384]{1,0:T(8,128)(2,1)S(1)} %get-tuple-element.36), channel_id=1, source_target_pairs={{0,28},{2,30},{4,8},{6,10},{8,4},{10,6},{12,16},{14,18},{16,12},{1... | collective-permute-start | bytes 258056 | tf_op jit(solution)/shard_map/apply/ppermute | solution.py:258
  39.4 4.6 %collective-permute-start.9 = (bf16[112,384]{1,0:T(8,128)(2,1)S(1)}, bf16[112,384]{1,0:T(8,128)(2,1)S(1)}, u32[]{:S(2)}, u32[]{:S(2)}) collective-permute-start(bf16[112,384]{1,0:T(8,128)(2,1)S(1)} %get-tuple-element.37), channel_id=1, source_target_pairs={{0,30},{2,4},{4,2},{6,8},{8,6},{10,12},{12,10},{14,16},{16,14},{18... | collective-permute-start | bytes 258056 | tf_op jit(solution)/shard_map/apply/ppermute | solution.py:258
  43.9 1.6 %collective-permute-start.11 = (bf16[112,384]{1,0:T(8,128)(2,1)S(1)}, bf16[112,384]{1,0:T(8,128)(2,1)S(1)}, u32[]{:S(2)}, u32[]{:S(2)}) collective-permute-start(bf16[112,384]{1,0:T(8,128)(2,1)S(1)} %get-tuple-element.39), channel_id=1, source_target_pairs={{0,16},{2,18},{4,20},{6,22},{8,24},{10,26},{12,28},{14,30},{16,0},... | collective-permute-start | bytes 258056 | tf_op jit(solution)/shard_map/apply/ppermute | solution.py:258
  45.6 2.8 %collective-permute-start.13 = (bf16[112,384]{1,0:T(8,128)(2,1)S(1)}, bf16[112,384]{1,0:T(8,128)(2,1)S(1)}, u32[]{:S(2)}, u32[]{:S(2)}) collective-permute-start(bf16[112,384]{1,0:T(8,128)(2,1)S(1)} %get-tuple-element.41), channel_id=1, source_target_pairs={{0,2},{2,0},{4,6},{6,4},{8,10},{10,8},{12,14},{14,12},{16,18},{18,... | collective-permute-start | bytes 258056 | tf_op jit(solution)/shard_map/apply/ppermute | solution.py:258
  51.6 2.5 %collective-permute-start.15 = (bf16[112,384]{1,0:T(8,128)(2,1)S(1)}, bf16[112,384]{1,0:T(8,128)(2,1)S(1)}, u32[]{:S(2)}, u32[]{:S(2)}) collective-permute-start(bf16[112,384]{1,0:T(8,128)(2,1)S(1)} %get-tuple-element.45), channel_id=1, source_target_pairs={{0,28},{2,30},{4,8},{6,10},{8,4},{10,6},{12,16},{14,18},{16,12},{1... | collective-permute-start | bytes 258056 | tf_op jit(solution)/shard_map/apply/ppermute | solution.py:258
  54.1 3.4 %collective-permute-start.16 = (bf16[112,384]{1,0:T(8,128)(2,1)S(1)}, bf16[112,384]{1,0:T(8,128)(2,1)S(1)}, u32[]{:S(2)}, u32[]{:S(2)}) collective-permute-start(bf16[112,384]{1,0:T(8,128)(2,1)S(1)} %get-tuple-element.46), channel_id=1, source_target_pairs={{0,30},{2,4},{4,2},{6,8},{8,6},{10,12},{12,10},{14,16},{16,14},{18... | collective-permute-start | bytes 258056 | tf_op jit(solution)/shard_map/apply/ppermute | solution.py:258
  57.5 2.8 %collective-permute-start.18 = (bf16[112,384]{1,0:T(8,128)(2,1)S(1)}, bf16[112,384]{1,0:T(8,128)(2,1)S(1)}, u32[]{:S(2)}, u32[]{:S(2)}) collective-permute-start(bf16[112,384]{1,0:T(8,128)(2,1)S(1)} %get-tuple-element.48), channel_id=1, source_target_pairs={{0,16},{2,18},{4,20},{6,22},{8,24},{10,26},{12,28},{14,30},{16,0},... | collective-permute-start | bytes 258056 | tf_op jit(solution)/shard_map/apply/ppermute | solution.py:258
  60.3 1.6 %collective-permute-start.20 = (bf16[112,384]{1,0:T(8,128)(2,1)S(1)}, bf16[112,384]{1,0:T(8,128)(2,1)S(1)}, u32[]{:S(2)}, u32[]{:S(2)}) collective-permute-start(bf16[112,384]{1,0:T(8,128)(2,1)S(1)} %get-tuple-element.50), channel_id=1, source_target_pairs={{0,2},{2,0},{4,6},{6,4},{8,10},{10,8},{12,14},{14,12},{16,18},{18,... | collective-permute-start | bytes 258056 | tf_op jit(solution)/shard_map/apply/ppermute | solution.py:258
  61.9 1.2 %collective-permute-done.16.refs_1_ = bf16[112,384]{1,0:T(8,128)(2,1)S(1)} collective-permute-done((bf16[112,384]{1,0:T(8,128)(2,1)S(1)}, bf16[112,384]{1,0:T(8,128)(2,1)S(1)}, u32[]{:S(2)}, u32[]{:S(2)}) %collective-permute-start.16) | collective-permute-done | bytes 86048 | tf_op jit(solution)/shard_map/apply/ppermute | solution.py:258
  63.9 1.3 %collective-permute-done.17.refs_0_ = bf16[112,384]{1,0:T(8,128)(2,1)S(1)} collective-permute-done((bf16[112,384]{1,0:T(8,128)(2,1)S(1)}, bf16[112,384]{1,0:T(8,128)(2,1)S(1)}, u32[]{:S(2)}, u32[]{:S(2)}) %collective-permute-start.17) | collective-permute-done | bytes 86048 | tf_op jit(solution)/shard_map/apply/ppermute | solution.py:258
  65.6 1.7 %apply.25 = (bf16[2,112,384]{2,1,0:T(8,128)(2,1)}, f32[32,8,112]{2,1,0:T(8,128)S(1)}) custom-call(s32[1]{0:T(128)} %bitcast.group, s32[2,4]{1,0:T(2,128)S(1)} %bitcast.24, f32[2,4]{1,0:T(2,128)S(1)} %bitcast.25, f32[2,112,384]{2,1,0:T(8,128)S(1)} %apply.22.part, f32[2,112,384]{2,1,0:T(8,128)S(1)} %apply.24.far, f32[8,128]{1,0:T(8,128)S(1)} %get-tuple-element.30.asks, ...), custom_call_target="tpu_custom_call" | custom-call | flops 33030144 | bytes 165150 | tf_op jit(solution)/shard_map/apply/pallas_call | solution.py:244
  67.2 12.1 %all_to_all.5.pieces = f32[32,8,112]{2,1,0:T(8,128)S(1)} all-to-all(f32[32,8,112]{2,1,0:T(8,128)S(1)} %get-tuple-element.53), channel_id=1, replica_groups=mesh['areal'=16,'layer'=2] {'areal','layer'}, dimensions={0} | all-to-all | bytes 229376 | tf_op jit(solution)/shard_map/project/all_to_all | solution.py:410
  (73 shorter events, 11.8 us)
Async XLA Ops:
  0.6 12.6 %collective-permute-start.2 = (bf16[224,384]{1,0:T(8,128)(2,1)}, bf16[224,384]{1,0:T(8,128)(2,1)S(1)}, u32[]{:S(2)}, u32[]{:S(2)}) collective-permute-start(bf16[224,384]{1,0:T(8,128)(2,1)} %bitcast.16), channel_id=1, source_target_pairs={{0,16},{2,18},{4,20},{6,22},{8,24},{10,26},{12,28},{14,30},{16,0},... | collective-permute-start | bytes 516104 | tf_op jit(solution)/shard_map/plan/ppermute | solution.py:258
  4.7 12.8 %copy-start.2 = (bf16[1,2,112,384]{3,2,1,0:T(8,128)(2,1)S(1)}, bf16[1,2,112,384]{3,2,1,0:T(8,128)(2,1)}, u32[]{:S(2)}) copy-start(bf16[1,2,112,384]{3,2,1,0:T(8,128)(2,1)} %param.10) | copy-start | bytes 516100
  7.1 11.7 %collective-permute-start.3 = (bf16[240,384]{1,0:T(8,128)(2,1)}, bf16[240,384]{1,0:T(8,128)(2,1)S(1)}, u32[]{:S(2)}, u32[]{:S(2)}) collective-permute-start(bf16[240,384]{1,0:T(8,128)(2,1)} %get-tuple-element.32), channel_id=1, source_target_pairs={{0,2},{2,0},{4,6},{6,4},{8,10},{10,8},{12,14},{14,12},{16,18},{18,... | collective-permute-start | bytes 552968 | tf_op jit(solution)/shard_map/apply/ppermute | solution.py:258
  8.7 13.3 %collective-permute-start.1 = (bf16[240,384]{1,0:T(8,128)(2,1)}, bf16[240,384]{1,0:T(8,128)(2,1)S(1)}, u32[]{:S(2)}, u32[]{:S(2)}) collective-permute-start(bf16[240,384]{1,0:T(8,128)(2,1)} %get-tuple-element.32), channel_id=1, source_target_pairs={{0,30},{2,4},{4,2},{6,8},{8,6},{10,12},{12,10},{14,16},{16,14},{18... | collective-permute-start | bytes 552968 | tf_op jit(solution)/shard_map/apply/ppermute | solution.py:258
  11.0 15.2 %collective-permute-start = (bf16[240,384]{1,0:T(8,128)(2,1)}, bf16[240,384]{1,0:T(8,128)(2,1)}, u32[]{:S(2)}, u32[]{:S(2)}) collective-permute-start(bf16[240,384]{1,0:T(8,128)(2,1)} %get-tuple-element.32), channel_id=1, source_target_pairs={{0,28},{2,30},{4,8},{6,10},{8,4},{10,6},{12,16},{14,18},{16,12},{1... | collective-permute-start | bytes 552968 | tf_op jit(solution)/shard_map/apply/ppermute | solution.py:258
  11.5 23.6 %collective-permute-start.6 = (bf16[240,384]{1,0:T(8,128)(2,1)}, bf16[240,384]{1,0:T(8,128)(2,1)}, u32[]{:S(2)}, u32[]{:S(2)}) collective-permute-start(bf16[240,384]{1,0:T(8,128)(2,1)} %get-tuple-element.32), channel_id=1, source_target_pairs={{0,1},{1,0},{2,3},{3,2},{4,5},{5,4},{6,7},{7,6},{8,9},{9,8},{10,11... | collective-permute-start | bytes 552968 | tf_op jit(solution)/shard_map/apply/ppermute | solution.py:268
  13.9 21.1 %collective-permute-start.5 = (bf16[240,384]{1,0:T(8,128)(2,1)}, bf16[240,384]{1,0:T(8,128)(2,1)}, u32[]{:S(2)}, u32[]{:S(2)}) collective-permute-start(bf16[240,384]{1,0:T(8,128)(2,1)} %get-tuple-element.32), channel_id=1, source_target_pairs={{0,4},{2,6},{4,0},{6,2},{8,12},{10,14},{12,8},{14,10},{16,20},{18,... | collective-permute-start | bytes 552968 | tf_op jit(solution)/shard_map/apply/ppermute | solution.py:258
  23.5 10.3 %collective-permute-start.4 = (bf16[112,384]{1,0:T(8,128)(2,1)}, bf16[112,384]{1,0:T(8,128)(2,1)}, u32[]{:S(2)}, u32[]{:S(2)}) collective-permute-start(bf16[112,384]{1,0:T(8,128)(2,1)} %get-tuple-element.33), channel_id=1, source_target_pairs={{0,30},{2,0},{4,2},{6,4},{8,6},{10,8},{12,10},{14,12},{16,14},{18,... | collective-permute-start | bytes 258056 | tf_op jit(solution)/shard_map/apply/ppermute | solution.py:258
  25.4 9.6 %collective-permute-start.7 = (f32[8,128]{1,0:T(8,128)S(1)}, f32[8,128]{1,0:T(8,128)S(1)}, u32[]{:S(2)}, u32[]{:S(2)}) collective-permute-start(f32[8,128]{1,0:T(8,128)S(1)} %get-tuple-element.34), channel_id=1, source_target_pairs={{0,16},{2,18},{4,20},{6,22},{8,24},{10,26},{12,28},{14,30},{16,0},... | collective-permute-start | bytes 12296 | tf_op jit(solution)/shard_map/apply/ppermute | solution.py:258
  35.0 13.6 %copy-start.3 = (bf16[1,2,112,384]{3,2,1,0:T(8,128)(2,1)S(1)}, bf16[1,2,112,384]{3,2,1,0:T(8,128)(2,1)}, u32[]{:S(2)}) copy-start(bf16[1,2,112,384]{3,2,1,0:T(8,128)(2,1)} %param.10) | copy-start | bytes 516100
  36.8 8.8 %collective-permute-start.8 = (bf16[112,384]{1,0:T(8,128)(2,1)S(1)}, bf16[112,384]{1,0:T(8,128)(2,1)S(1)}, u32[]{:S(2)}, u32[]{:S(2)}) collective-permute-start(bf16[112,384]{1,0:T(8,128)(2,1)S(1)} %get-tuple-element.36), channel_id=1, source_target_pairs={{0,28},{2,30},{4,8},{6,10},{8,4},{10,6},{12,16},{14,18},{16,12},{1... | collective-permute-start | bytes 258056 | tf_op jit(solution)/shard_map/apply/ppermute | solution.py:258
  39.4 9.3 %collective-permute-start.9 = (bf16[112,384]{1,0:T(8,128)(2,1)S(1)}, bf16[112,384]{1,0:T(8,128)(2,1)S(1)}, u32[]{:S(2)}, u32[]{:S(2)}) collective-permute-start(bf16[112,384]{1,0:T(8,128)(2,1)S(1)} %get-tuple-element.37), channel_id=1, source_target_pairs={{0,30},{2,4},{4,2},{6,8},{8,6},{10,12},{12,10},{14,16},{16,14},{18... | collective-permute-start | bytes 258056 | tf_op jit(solution)/shard_map/apply/ppermute | solution.py:258
  43.9 6.3 %collective-permute-start.10 = (bf16[112,384]{1,0:T(8,128)(2,1)S(1)}, bf16[112,384]{1,0:T(8,128)(2,1)S(1)}, u32[]{:S(2)}, u32[]{:S(2)}) collective-permute-start(bf16[112,384]{1,0:T(8,128)(2,1)S(1)} %get-tuple-element.38), channel_id=1, source_target_pairs={{0,14},{2,16},{4,18},{6,20},{8,22},{10,24},{12,26},{14,28},{16,30}... | collective-permute-start | bytes 258056 | tf_op jit(solution)/shard_map/apply/ppermute | solution.py:258
  43.9 6.3 %collective-permute-start.11 = (bf16[112,384]{1,0:T(8,128)(2,1)S(1)}, bf16[112,384]{1,0:T(8,128)(2,1)S(1)}, u32[]{:S(2)}, u32[]{:S(2)}) collective-permute-start(bf16[112,384]{1,0:T(8,128)(2,1)S(1)} %get-tuple-element.39), channel_id=1, source_target_pairs={{0,16},{2,18},{4,20},{6,22},{8,24},{10,26},{12,28},{14,30},{16,0},... | collective-permute-start | bytes 258056 | tf_op jit(solution)/shard_map/apply/ppermute | solution.py:258
  45.6 5.0 %collective-permute-start.12 = (bf16[112,384]{1,0:T(8,128)(2,1)S(1)}, bf16[112,384]{1,0:T(8,128)(2,1)S(1)}, u32[]{:S(2)}, u32[]{:S(2)}) collective-permute-start(bf16[112,384]{1,0:T(8,128)(2,1)S(1)} %get-tuple-element.40), channel_id=1, source_target_pairs={{0,4},{2,6},{4,0},{6,2},{8,12},{10,14},{12,8},{14,10},{16,20},{18,... | collective-permute-start | bytes 258056 | tf_op jit(solution)/shard_map/apply/ppermute | solution.py:258
  45.6 5.6 %collective-permute-start.13 = (bf16[112,384]{1,0:T(8,128)(2,1)S(1)}, bf16[112,384]{1,0:T(8,128)(2,1)S(1)}, u32[]{:S(2)}, u32[]{:S(2)}) collective-permute-start(bf16[112,384]{1,0:T(8,128)(2,1)S(1)} %get-tuple-element.41), channel_id=1, source_target_pairs={{0,2},{2,0},{4,6},{6,4},{8,10},{10,8},{12,14},{14,12},{16,18},{18,... | collective-permute-start | bytes 258056 | tf_op jit(solution)/shard_map/apply/ppermute | solution.py:258
  48.7 2.5 %collective-permute-start.14 = (bf16[112,384]{1,0:T(8,128)(2,1)S(1)}, bf16[112,384]{1,0:T(8,128)(2,1)S(1)}, u32[]{:S(2)}, u32[]{:S(2)}) collective-permute-start(bf16[112,384]{1,0:T(8,128)(2,1)S(1)} %get-tuple-element.42), channel_id=1, source_target_pairs={{0,1},{1,0},{2,3},{3,2},{4,5},{5,4},{6,7},{7,6},{8,9},{9,8},{10,11... | collective-permute-start | bytes 258056 | tf_op jit(solution)/shard_map/apply/ppermute | solution.py:268
  51.6 8.7 %collective-permute-start.15 = (bf16[112,384]{1,0:T(8,128)(2,1)S(1)}, bf16[112,384]{1,0:T(8,128)(2,1)S(1)}, u32[]{:S(2)}, u32[]{:S(2)}) collective-permute-start(bf16[112,384]{1,0:T(8,128)(2,1)S(1)} %get-tuple-element.45), channel_id=1, source_target_pairs={{0,28},{2,30},{4,8},{6,10},{8,4},{10,6},{12,16},{14,18},{16,12},{1... | collective-permute-start | bytes 258056 | tf_op jit(solution)/shard_map/apply/ppermute | solution.py:258
  54.1 9.0 %collective-permute-start.16 = (bf16[112,384]{1,0:T(8,128)(2,1)S(1)}, bf16[112,384]{1,0:T(8,128)(2,1)S(1)}, u32[]{:S(2)}, u32[]{:S(2)}) collective-permute-start(bf16[112,384]{1,0:T(8,128)(2,1)S(1)} %get-tuple-element.46), channel_id=1, source_target_pairs={{0,30},{2,4},{4,2},{6,8},{8,6},{10,12},{12,10},{14,16},{16,14},{18... | collective-permute-start | bytes 258056 | tf_op jit(solution)/shard_map/apply/ppermute | solution.py:258
  57.5 7.6 %collective-permute-start.17 = (bf16[112,384]{1,0:T(8,128)(2,1)S(1)}, bf16[112,384]{1,0:T(8,128)(2,1)S(1)}, u32[]{:S(2)}, u32[]{:S(2)}) collective-permute-start(bf16[112,384]{1,0:T(8,128)(2,1)S(1)} %get-tuple-element.47), channel_id=1, source_target_pairs={{0,14},{2,16},{4,18},{6,20},{8,22},{10,24},{12,26},{14,28},{16,30}... | collective-permute-start | bytes 258056 | tf_op jit(solution)/shard_map/apply/ppermute | solution.py:258
  57.5 7.6 %collective-permute-start.18 = (bf16[112,384]{1,0:T(8,128)(2,1)S(1)}, bf16[112,384]{1,0:T(8,128)(2,1)S(1)}, u32[]{:S(2)}, u32[]{:S(2)}) collective-permute-start(bf16[112,384]{1,0:T(8,128)(2,1)S(1)} %get-tuple-element.48), channel_id=1, source_target_pairs={{0,16},{2,18},{4,20},{6,22},{8,24},{10,26},{12,28},{14,30},{16,0},... | collective-permute-start | bytes 258056 | tf_op jit(solution)/shard_map/apply/ppermute | solution.py:258
  60.3 5.2 %collective-permute-start.19 = (bf16[112,384]{1,0:T(8,128)(2,1)S(1)}, bf16[112,384]{1,0:T(8,128)(2,1)S(1)}, u32[]{:S(2)}, u32[]{:S(2)}) collective-permute-start(bf16[112,384]{1,0:T(8,128)(2,1)S(1)} %get-tuple-element.49), channel_id=1, source_target_pairs={{0,4},{2,6},{4,0},{6,2},{8,12},{10,14},{12,8},{14,10},{16,20},{18,... | collective-permute-start | bytes 258056 | tf_op jit(solution)/shard_map/apply/ppermute | solution.py:258
  60.3 5.2 %collective-permute-start.20 = (bf16[112,384]{1,0:T(8,128)(2,1)S(1)}, bf16[112,384]{1,0:T(8,128)(2,1)S(1)}, u32[]{:S(2)}, u32[]{:S(2)}) collective-permute-start(bf16[112,384]{1,0:T(8,128)(2,1)S(1)} %get-tuple-element.50), channel_id=1, source_target_pairs={{0,2},{2,0},{4,6},{6,4},{8,10},{10,8},{12,14},{14,12},{16,18},{18,... | collective-permute-start | bytes 258056 | tf_op jit(solution)/shard_map/apply/ppermute | solution.py:258
  63.2 2.4 %collective-permute-start.21 = (bf16[112,384]{1,0:T(8,128)(2,1)S(1)}, bf16[112,384]{1,0:T(8,128)(2,1)S(1)}, u32[]{:S(2)}, u32[]{:S(2)}) collective-permute-start(bf16[112,384]{1,0:T(8,128)(2,1)S(1)} %get-tuple-element.51), channel_id=1, source_target_pairs={{0,1},{1,0},{2,3},{3,2},{4,5},{5,4},{6,7},{7,6},{8,9},{9,8},{10,11... | collective-permute-start | bytes 258056 | tf_op jit(solution)/shard_map/apply/ppermute | solution.py:268
  (16 other events, 62.6 us)
